TPU v7x, 128 devices: a whole 4x4x4 slice. The times are simulated.
128 devices in a mesh: gx: 16 (over x, y), gy: 8 (over z, core).
Axes of the slice: x: 4, y: 4, z: 4, core: 2. Of those that a mesh axis runs over, the one named last changes fastest.
Arguments:
- fields: float32 [6, 256, 256, 128], P(None, 'gx', 'gy'), may hold values from -0.0029296875 to 0.0029296875
- region: int32 [256, 256, 128], P('gx', 'gy'), may hold values from 0 to 15
- eps_table: float32 [16], replicated, may hold values from 1 to 2
Outputs:
- advanced: float32 [6, 256, 256, 128], P(None, 'gx', 'gy')
All inputs are finite; a program needn't handle non-finite values.
Results may differ from a plain program's by a relative error of at most 0.0003.
Values sent between devices are 32-bit elements; how exact they have to be, the bound alone decides.
No kernel may reach another device: no remote copies, remote signals or barrier semaphores. Data moves between devices by JAX's collectives and lax.ppermute only.
A program may use at most 128 MiB of HBM per device.

v0:
```python
import functools

import jax
import jax.numpy as jnp
from jax import lax
from jax.experimental import pallas as pl
from jax.experimental.pallas import tpu as pltpu
from jax.sharding import PartitionSpec as P

PX, PY, PZ = 16, 32, 128
XR = 40
YR = 24
F32 = jnp.float32
EX, EY, EZ, HX, HY, HZ = range(6)


def lane():
    return lax.broadcasted_iota(jnp.int32, (PY, PZ), 1)


def sub():
    return lax.broadcasted_iota(jnp.int32, (PY, PZ), 0)


def lanes_of(v):
    return lax.broadcasted_iota(jnp.int32, v.shape, 1)


def z_next(v):
    return jnp.where(lanes_of(v) == PZ - 1, 0.0, pltpu.roll(v, PZ - 1, 1))


def z_prev(v):
    return jnp.where(lanes_of(v) == 0, 0.0, pltpu.roll(v, 1, 1))


def fz(v):
    return z_next(v) - v


def bz(v):
    return v - z_prev(v)


def y_prev(v, row):
    return jnp.where(sub() == 0, row, pltpu.roll(v, 1, 0))


def y_next(v, row):
    return jnp.where(sub() == PY - 1, row, pltpu.roll(v, PY - 1, 0))


def plane(ref, k, size=PY):
    return ref[pl.ds(k * size, size), :]


def put(ref, k, v, size=PY):
    ref[pl.ds(k * size, size), :] = v


def fplane(ref, f, x):
    return plane(ref, f * PX + x)


def lookup(region, table):
    level = [table[i] for i in range(16)]
    for bit in range(4):
        on = (region & (1 << bit)) != 0
        level = [jnp.where(on, level[2 * i + 1], level[2 * i]) for i in range(len(level) // 2)]
    return level[0]


def k_edges(f, reg, table, eps, xup, xdn, yup, ydn):
    tab = [table[i] for i in range(16)]
    for x in range(PX):
        put(eps, x, lookup(plane(reg, x), tab))
    for i, c in enumerate((EX, EY, HY, HZ)):
        put(xup, i, fplane(f, c, PX - 1))
    put(xup, 4, plane(eps, PX - 1))
    for i, c in enumerate((EY, EZ, HX, HZ)):
        put(xdn, i, fplane(f, c, 0))
    put(xdn, 4, plane(eps, 0))

    def row(ref, base, y):
        return ref[pl.ds(base * PX * PY + y, PX, stride=PY), :]

    for i, (c, y) in enumerate(((EX, 31), (HY, 31), (EZ, 31), (HX, 31), (HX, 30))):
        put(yup, i, row(f, c, y), PX)
    put(yup, 5, row(eps, 0, PY - 1), PX)
    for i, c in enumerate((EX, HY, EZ, HX)):
        put(ydn, i, row(f, c, 0), PX)
    put(ydn, 4, row(eps, 0, 0), PX)


def factor(m_at, count, first, h, b, rows):
    hv = jnp.ones((rows, PZ), F32)
    hs = jnp.where(first, jnp.zeros_like(hv), jnp.ones_like(hv))
    bv = jnp.ones((rows, PZ), F32)
    bs = jnp.ones((rows, PZ), F32)
    for i in range(count):
        k = count - 1 - i
        put(h, i, hv, rows)
        put(b, k, bv, rows)
        hs = hs + m_at(i) * hv
        bs = bs + m_at(k) * bv
        hlast, blast = hv, bv
        hv = hv + hs
        bv = bv + bs
    hn = 1.0 / hv
    bn = 1.0 / bv
    return hn, bn, blast * bn, hn, hlast * hn


def sweep(m_at, r_at, count, v, rows):
    vv = jnp.zeros((rows, PZ), F32)
    vs = jnp.zeros((rows, PZ), F32)
    for i in range(count):
        put(v, i, vv, rows)
        vs = vs + m_at(i) * (vv - r_at(i))
        last = vv
        vv = vv + vs
    return last, vv


def ends(last, vn, hn, c):
    return -vn * hn, last - c * vn


def spread(msg, count, values):
    block = sum(v.shape[0] for v in values)
    for k in range(count):
        at = k * block
        for v in values:
            msg[pl.ds(at, v.shape[0]), :] = v
            at += v.shape[0]


def k_x1(f, eps, xl, xr, yl, yr, msg, q1, m, h, b, v, hb, r):
    gx = lax.axis_index("gx")
    gy = lax.axis_index("gy")
    n = lax.axis_size("gx")
    xlo = gx > 0
    ylo = gy > 0
    yhi = gy < lax.axis_size("gy") - 1
    yin = jnp.where(ylo, 1.0, 0.0)
    yon = jnp.where(yhi, 1.0, 0.0)
    q1lo = yin * (plane(yl, 1, PX) - 0.5 * fz(plane(yl, 0, PX)))
    q1hi = yon * (plane(yr, 1, PX) - 0.5 * fz(plane(yr, 0, PX)))
    hxlo = yin * plane(yl, 3, PX)
    epslo = plane(yl, 5, PX)
    epshi = plane(yr, 4, PX)
    hx31 = f[pl.ds(HX * PX * PY + PY - 1, PX, stride=PY), :]
    bxlo = jnp.concatenate([q1lo[:1], q1lo[1:] - q1lo[:-1]], 0)
    bxhi = jnp.concatenate([q1hi[:1], q1hi[1:] - q1hi[:-1]], 0)
    rlo = yin * plane(yl, 2, PX) + (32.0 / epslo) * (bxlo - (hxlo - yin * plane(yl, 4, PX)))
    rhi = yon * plane(yr, 2, PX) + (32.0 / epshi) * (bxhi - (yon * plane(yr, 3, PX) - hx31))
    pad = jnp.zeros((XR - PY - 2, PZ), F32)
    one = jnp.ones((XR - PY - 2, PZ), F32)
    before = jnp.where(xlo, plane(xl, 2) - 0.5 * fz(plane(xl, 0)), 0.0)
    for x in range(PX):
        q = fplane(f, HY, x) - 0.5 * fz(fplane(f, EX, x))
        put(q1, x, q)
        e = plane(eps, x)
        hx = fplane(f, HX, x)
        ce = 32.0 / e
        rr = fplane(f, EZ, x) + ce * ((q - before) - (hx - y_prev(hx, hxlo[x : x + 1])))
        before = q
        r[pl.ds(x * XR, PY), :] = rr
        r[pl.ds(x * XR + PY, 8), :] = jnp.concatenate([rlo[x : x + 1], rhi[x : x + 1], pad], 0)
        m[pl.ds(x * XR, PY), :] = e * (1.0 / 1024.0)
        m[pl.ds(x * XR + PY, 8), :] = (
            jnp.concatenate([epslo[x : x + 1], epshi[x : x + 1], one], 0) * (1.0 / 1024.0)
        )
    m_at = lambda i: plane(m, i, XR)
    hn, bn, a, bb, c = factor(m_at, PX, gx == 0, h, b, XR)
    last, vn = sweep(m_at, lambda i: plane(r, i, XR), PX, v, XR)
    pf, plast = ends(last, vn, hn, c)
    put(hb, 0, hn, XR)
    put(hb, 1, bn, XR)
    put(hb, 2, c, XR)
    put(hb, 3, vn, XR)
    zq = jnp.zeros((6, PZ), F32)
    qq = jnp.concatenate([q1lo[PX - 1 :], q1hi[PX - 1 :], zq], 0) * (-1.0 / 32.0)
    spread(msg, n, (pf, plast, a, bb, c, qq))


def k_y1(f, eps, xl, xr, order, msg, p1, ey1, m, h, b, v, hb, r, ep):
    gx = lax.axis_index("gx")
    gy = lax.axis_index("gy")
    n = lax.axis_size("gy")
    xlo = gx > 0
    xin = jnp.where(xlo, 1.0, 0.0)
    xon = jnp.where(gx < lax.axis_size("gx") - 1, 1.0, 0.0)
    zero = jnp.zeros((1, PZ), F32)
    zeros = jnp.zeros((PY, PZ), F32)
    exl, eyl, hyl, hzl = [xin * plane(xl, i) for i in range(4)]
    eyr, ezr, hxr, hzr = [xon * plane(xr, i) for i in range(4)]
    for x in range(PX):
        put(ep, x, plane(eps, x))
    put(ep, PX, plane(xl, 4))
    put(ep, PX + 1, plane(xr, 4))
    for x in range(PX + 2, YR):
        put(ep, x, zeros + 1.0)
        put(r, x, zeros)
    put(r, PX + 1, zeros)

    def rex(ex, hy, pp, e):
        ie = 1.0 / e
        return ex + (32.0 * ie) * (pp - y_prev(pp, zero)) - (0.5 * ie) * bz(hy)

    p = hzl - 32.0 * (fplane(f, EY, 0) - eyl)
    p = jnp.where(xlo, p, 0.0)
    put(p1, PX, p)
    put(r, PX, rex(exl, hyl, p, plane(ep, PX)))
    for x in range(PX):
        ey = fplane(f, EY, x)
        nxt = fplane(f, EY, x + 1) if x < PX - 1 else eyr
        hz = fplane(f, HZ, x)
        hzp = fplane(f, HZ, x - 1) if x > 0 else hzl
        e = plane(ep, x)
        p = hz - 32.0 * (nxt - ey)
        put(p1, x, p)
        put(r, x, rex(fplane(f, EX, x), fplane(f, HY, x), p, e))
        ie = 1.0 / e
        put(ey1, x, ey + (0.5 * ie) * bz(fplane(f, HX, x)) - (32.0 * ie) * (hz - hzp))
    ie = 1.0 / plane(ep, PX + 1)
    put(ey1, PX, eyr + (0.5 * ie) * bz(hxr) - (32.0 * ie) * (hzr - fplane(f, HZ, PX - 1)))

    def rows(ref, j):
        return ref[pl.ds(j, YR, stride=PY), :]

    for j in range(PY):
        put(m, j, rows(ep, j) * (1.0 / 1024.0), YR)
    m_at = lambda j: plane(m, j, YR)
    hn, bn, a, bb, c = factor(m_at, PY, gy == 0, h, b, YR)
    last, vn = sweep(m_at, lambda j: rows(r, j), PY, v, YR)
    pf, plast = ends(last, vn, hn, c)
    put(hb, 0, hn, YR)
    put(hb, 1, bn, YR)
    put(hb, 2, c, YR)
    put(hb, 3, vn, YR)
    lastrow = lambda ref, at, k: ref[pl.ds(at * PY + PY - 1, k, stride=PY), :]
    tail = jnp.zeros((7, PZ), F32)
    qq = jnp.concatenate([lastrow(p1, 0, PX), lastrow(p1, PX, 1), tail], 0) * (-1.0 / 32.0)
    tail = jnp.zeros((6, PZ), F32)
    ee = fz(jnp.concatenate([lastrow(ey1, 0, PX), zero, lastrow(ey1, PX, 1), tail], 0))
    spread(msg, n, (pf, plast, a, bb, c, qq, ee))


def coefficients(part, n, rows, tp, bp, ts, bs, bet, dele):
    zero = jnp.zeros((rows, PZ), F32)
    beta = zero
    put(bet, 0, zero, rows)
    for j in range(n):
        a, b, c = part(j, 2), part(j, 3), part(j, 4)
        bd = b / (1.0 - a * beta)
        t = bd * beta
        put(tp, j, t, rows)
        put(bp, j, bd, rows)
        beta = c + t * b
        put(bet, j + 1, beta, rows)
    delta = zero
    put(dele, n, zero, rows)
    for j in range(n - 1, -1, -1):
        a, b, c = part(j, 2), part(j, 3), part(j, 4)
        bd = b / (1.0 - c * delta)
        t = bd * delta
        put(ts, j, t, rows)
        put(bs, j, bd, rows)
        delta = a + t * b
        put(dele, j, delta, rows)


def interface(part, n, me, rows, tp, bp, ts, bs, bet, dele, al, ga, crows=None):
    crows = crows or rows
    zero = jnp.zeros((rows, PZ), F32)
    take = lambda ref, j: ref[pl.ds(j * crows, rows), :]
    alpha = zero
    put(al, 0, zero, rows)
    gamma = zero
    put(ga, n, zero, rows)
    for j in range(n):
        k = n - 1 - j
        alpha = part(j, 1) + take(tp, j) * part(j, 0) + take(bp, j) * alpha
        gamma = part(k, 0) + take(ts, k) * part(k, 1) + take(bs, k) * gamma
        put(al, j + 1, alpha, rows)
        put(ga, k, gamma, rows)
    at = lambda ref, d, size: ref[pl.ds(pl.multiple_of(d * size, 8), rows), :]
    a0, a1 = at(al, me, rows), at(al, me + 1, rows)
    g0, g1 = at(ga, me, rows), at(ga, me + 1, rows)
    b0, b1 = at(bet, me, crows), at(bet, me + 1, crows)
    d0, d1 = at(dele, me, crows), at(dele, me + 1, crows)
    left = a0 + b0 * ((g0 + d0 * a0) / (1.0 - d0 * b0))
    right = g1 + d1 * ((a1 + b1 * g1) / (1.0 - b1 * d1))
    return left, right


def k_y2(msg, p1, h, b, v, hb, ex1, p2, elo, tp, bp, ts, bs, bet, dele, al, ga, dex):
    n = lax.axis_size("gy")
    me = lax.axis_index("gy")
    block = 7 * YR
    raw = lambda j, k: msg[pl.ds(j * block + k * YR, YR), :]
    coefficients(raw, n, YR, tp, bp, ts, bs, bet, dele)

    def part(j, k):
        own = raw(j, k)
        if j == 0:
            return own
        return own + raw(j, 2 + k) * raw(j - 1, 5)

    left, right = interface(part, n, me, YR, tp, bp, ts, bs, bet, dele, al, ga)
    prev = pl.multiple_of(jnp.maximum(me - 1, 0) * block, 8)
    live = jnp.where(me > 0, 1.0, 0.0)
    q = live * msg[pl.ds(prev + 5 * YR, YR), :]
    elo[...] = live * msg[pl.ds(prev + 6 * YR, YR), :]
    lw = (left + q) * plane(hb, 1, YR)
    rw = (right - plane(hb, 3, YR)) * plane(hb, 0, YR)
    later = right
    for j in range(PY - 1, -1, -1):
        w = plane(v, j, YR) + plane(b, j, YR) * lw + plane(h, j, YR) * rw
        ex1[pl.ds(j, YR, stride=PY), :] = w
        dex[pl.ds(j, YR, stride=PY), :] = later - w
        later = w
    live = jnp.where(lax.axis_index("gx") > 0, 1.0, 0.0)
    for x in range(PX):
        put(p2, x, plane(p1, x) + 64.0 * plane(dex, x))
    put(p2, PX, live * (plane(p1, PX) + 64.0 * plane(dex, PX)))


def k_x2(msg, f, eps, q1, ey1, p2, h, b, v, m, hb, ez1, hx1, msg2, v2, vn2, tp, bp, ts, bs, bet, dele, al, ga, r):
    n = lax.axis_size("gx")
    me = lax.axis_index("gx")
    gy = lax.axis_index("gy")
    yon = jnp.where(gy < lax.axis_size("gy") - 1, 1.0, 0.0)
    block = 5 * XR + 8
    raw = lambda j, k: msg[pl.ds(j * block + k * XR, XR), :]
    coefficients(raw, n, XR, tp, bp, ts, bs, bet, dele)

    def part(j, k):
        if j == 0:
            return raw(j, k)
        own = msg[pl.ds(j * block + k * XR, PY), :]
        more = (
            msg[pl.ds(j * block + k * XR + PY, 8), :]
            + msg[pl.ds(j * block + (2 + k) * XR + PY, 8), :] * msg[pl.ds((j - 1) * block + 5 * XR, 8), :]
        )
        return jnp.concatenate([own, more], 0)

    left, right = interface(part, n, me, XR, tp, bp, ts, bs, bet, dele, al, ga)
    prev = pl.multiple_of(jnp.maximum(me - 1, 0) * block, 8)
    q = jnp.where(me > 0, 1.0, 0.0) * msg[pl.ds(prev + 5 * XR, 8), :]
    left = jnp.concatenate([left[:PY], left[PY:] + q], 0)
    lw = left * plane(hb, 1, XR)
    rw = (right - plane(hb, 3, XR)) * plane(hb, 0, XR)
    for x in range(PX):
        put(ez1, x, plane(v, x, XR) + plane(b, x, XR) * lw + plane(h, x, XR) * rw, XR)
    put(ez1, PX, right, XR)
    before = plane(p2, PX)
    for x in range(PX):
        z = ez1[pl.ds(x * XR, PY), :]
        z32 = yon * ez1[pl.ds(x * XR + PY + 1, 1), :]
        ey = plane(ey1, x)
        t = fplane(f, HX, x) - 32.0 * (y_next(z, z32) - z) + 0.5 * fz(ey)
        put(hx1, x, t)
        p = plane(p2, x)
        ie = 1.0 / plane(eps, x)
        put(r, x, ey + (0.5 * ie) * bz(t) - (32.0 * ie) * (p - before))
        before = p
    last, vn = sweep(lambda i: m[pl.ds(i * XR, PY), :], lambda i: plane(r, i), PX, v2, PY)
    vn2[...] = vn
    pf, plast = ends(last, vn, hb[pl.ds(0, PY), :], hb[pl.ds(2 * XR, PY), :])
    spread(msg2, n, (pf, plast))


def k_y3(f, xr, q1, eps, ey1, ez1, hx1, ex1, elo, m, hb, msg2, v2, vn2, ex2, hy1, q2, r):
    n = lax.axis_size("gy")
    gy = lax.axis_index("gy")
    yon = jnp.where(gy < n - 1, 1.0, 0.0)
    yin = jnp.where(gy > 0, 1.0, 0.0)
    zeros = jnp.zeros((PY, PZ), F32)
    for x in range(PX + 2, YR):
        put(r, x, zeros)
    put(r, PX, zeros)
    for x in range(PX + 1):
        at = x * XR
        z = ez1[pl.ds(at, PY), :]
        zlo = ez1[pl.ds(at + PY, 1), :]
        zhi = yon * ez1[pl.ds(at + PY + 1, 1), :]
        fe = fz(plane(ey1, x))
        d = 32.0 * (y_next(z, zhi) - z) - fe
        k = x if x < PX else PX + 1
        dlo = yin * (32.0 * (z[:1] - zlo) - elo[pl.ds(k, 1), :])
        ez = fplane(f, EZ, x) if x < PX else plane(xr, 1)
        e = plane(eps, x) if x < PX else plane(xr, 4)
        ie = 1.0 / e
        put(r, k, 2.0 * z - ez + (32.0 * ie) * (d - y_prev(d, dlo)))
        if x < PX:
            t = plane(q1, x) + 32.0 * (ez1[pl.ds(at + XR, PY), :] - z)
            put(hy1, x, t)
            put(ex2, x, 2.0 * plane(ex1, x) - fplane(f, EX, x) + (0.5 * ie) * bz(fplane(f, HY, x) - t))
            put(q2, x, plane(hx1, x) + 0.5 * fe)
    m_at = lambda j: plane(m, j, YR)
    last, vn = sweep(m_at, lambda j: r[pl.ds(j, YR, stride=PY), :], PY, v2, YR)
    vn2[...] = vn
    pf, plast = ends(last, vn, plane(hb, 0, YR), plane(hb, 2, YR))
    spread(msg2, n, (pf, plast))


def k_y4(msg, h, b, v2, vn2, hb, tp, bp, ts, bs, bet, dele, ex2, hy1, q2, ez2, hx2, hy2, al, ga, w2, dw):
    n = lax.axis_size("gy")
    me = lax.axis_index("gy")
    part = lambda j, k: msg[pl.ds((2 * j + k) * YR, YR), :]
    left, right = interface(part, n, me, YR, tp, bp, ts, bs, bet, dele, al, ga)
    lw = left * plane(hb, 1, YR)
    rw = (right - vn2[...]) * plane(hb, 0, YR)
    later = right
    for j in range(PY - 1, -1, -1):
        w = plane(v2, j, YR) + plane(b, j, YR) * lw + plane(h, j, YR) * rw
        w2[pl.ds(j, YR, stride=PY), :] = w
        dw[pl.ds(j, YR, stride=PY), :] = later - w
        later = w
    xon = jnp.where(lax.axis_index("gx") < lax.axis_size("gx") - 1, 1.0, 0.0)
    for x in range(PX):
        w = plane(w2, x)
        nxt = plane(w2, x + 1) if x < PX - 1 else xon * plane(w2, PX + 1)
        put(ez2, x, w)
        put(hx2, x, plane(q2, x) - 32.0 * plane(dw, x))
        put(hy2, x, plane(hy1, x) - 0.5 * fz(plane(ex2, x)) + 32.0 * (nxt - w))


def k_x4(msg, h, b, v2, vn2, hb, tp, bp, ts, bs, bet, dele, p2, ex2, ez2, hx2, hy2, out, al, ga):
    n = lax.axis_size("gx")
    me = lax.axis_index("gx")
    part = lambda j, k: msg[pl.ds((2 * j + k) * PY, PY), :]
    left, right = interface(part, n, me, PY, tp, bp, ts, bs, bet, dele, al, ga, XR)
    lw = left * hb[pl.ds(XR, PY), :]
    rw = (right - vn2[...]) * hb[pl.ds(0, PY), :]
    later = right
    for x in range(PX - 1, -1, -1):
        w = plane(v2, x) + b[pl.ds(x * XR, PY), :] * lw + h[pl.ds(x * XR, PY), :] * rw
        put(out, EY * PX + x, w)
        put(out, HZ * PX + x, plane(p2, x) - 32.0 * (later - w))
        later = w
        put(out, EX * PX + x, plane(ex2, x))
        put(out, EZ * PX + x, plane(ez2, x))
        put(out, HX * PX + x, plane(hx2, x))
        put(out, HY * PX + x, plane(hy2, x))


def rows_of(*counts):
    return [jax.ShapeDtypeStruct((c, PZ), F32) for c in counts]


def call(kernel, outs, args, scratch=(), smem=(), name=None):
    vm = pl.BlockSpec(memory_space=pltpu.VMEM)
    sm = pl.BlockSpec(memory_space=pltpu.SMEM)
    return pl.pallas_call(
        kernel,
        out_shape=rows_of(*outs),
        in_specs=[sm if i in smem else vm for i in range(len(args))],
        out_specs=[vm] * len(outs),
        scratch_shapes=[pltpu.VMEM((c, PZ), F32) for c in scratch],
        compiler_params=pltpu.CompilerParams(vmem_limit_bytes=24 * 1024 * 1024),
        cost_estimate=pl.CostEstimate(flops=4_000_000, bytes_accessed=4_000_000, transcendentals=0),
        name=name,
    )(*args)


def ring(block, axis, step):
    n = lax.axis_size(axis)
    return lax.ppermute(block, axis, [(i, (i + step) % n) for i in range(n)])


def swap(msg, axis):
    n = lax.axis_size(axis)
    got = lax.all_to_all(msg.reshape(n, -1, PZ), axis, 0, 0, tiled=True)
    return got.reshape(-1, PZ)


def local(fields, region, eps_table):
    nx = lax.axis_size("gx")
    ny = lax.axis_size("gy")
    cells = PX * PY
    f = fields.reshape(6 * cells, PZ)
    reg = region.reshape(cells, PZ)
    eps, xup, xdn, yup, ydn = call(
        k_edges, (cells, 5 * PY, 5 * PY, 6 * PX, 6 * PX), (f, reg, eps_table), smem=(2,), name="edges"
    )
    xl = ring(xup, "gx", 1)
    xr = ring(xdn, "gx", -1)
    yl = ring(yup, "gy", 1)
    yr = ring(ydn, "gy", -1)
    nxl, nyl = PX * XR, PY * YR
    msgx, q1, mx, hx, bx, vx, hbx = call(
        k_x1,
        (nx * (5 * XR + 8), cells, nxl, nxl, nxl, nxl, 4 * XR),
        (f, eps, xl, xr, yl, yr),
        (nxl,),
        name="x1",
    )
    gotx = swap(msgx, "gx")
    msgy, p1, ey1, my, hy, by, vy, hby = call(
        k_y1,
        (ny * 7 * YR, cells + PY, cells + PY, nyl, nyl, nyl, nyl, 4 * YR),
        (f, eps, xl, xr, hbx),
        (YR * PY, YR * PY),
        name="y1",
    )
    goty = swap(msgy, "gy")
    chain = lambda n, rows: (n * rows,) * 4 + ((n + 1) * rows,) * 2
    ex1, p2, elo, *cy = call(
        k_y2,
        (YR * PY, cells + PY, YR) + chain(ny, YR),
        (goty, p1, hy, by, vy, hby),
        ((ny + 1) * YR, (ny + 1) * YR, YR * PY),
        name="y2",
    )
    ez1, hx1, msgx2, vx2, vnx2, *cx = call(
        k_x2,
        (nxl + XR, cells, nx * 2 * PY, cells, PY) + chain(nx, XR),
        (gotx, f, eps, q1, ey1, p2, hx, bx, vx, mx, hbx),
        ((nx + 1) * XR, (nx + 1) * XR, cells),
        name="x2",
    )
    gotx2 = swap(msgx2, "gx")
    msgy2, vy2, vny2, ex2, hy1, q2 = call(
        k_y3,
        (ny * 2 * YR, nyl, YR, cells, cells, cells),
        (f, xr, q1, eps, ey1, ez1, hx1, ex1, elo, my, hby),
        (YR * PY,),
        name="y3",
    )
    goty2 = swap(msgy2, "gy")
    ez2, hx2, hy2 = call(
        k_y4,
        (cells, cells, cells),
        (goty2, hy, by, vy2, vny2, hby, *cy, ex2, hy1, q2),
        ((ny + 1) * YR, (ny + 1) * YR, YR * PY, YR * PY),
        name="y4",
    )
    (out,) = call(
        k_x4,
        (6 * cells,),
        (gotx2, hx, bx, vx2, vnx2, hbx, *cx, p2, ex2, ez2, hx2, hy2),
        ((nx + 1) * PY, (nx + 1) * PY),
        name="x4",
    )
    return out.reshape(6, PX, PY, PZ)


def solution(mesh):
    return jax.shard_map(
        local,
        mesh=mesh,
        in_specs=(P(None, "gx", "gy", None), P("gx", "gy", None), P()),
        out_specs=P(None, "gx", "gy", None),
        check_vma=False,
    )
```

profile of v0, /device:TPU:0, one launch (start us, length us, event | category | flops | bytes accessed | tf_op | source)
XLA Modules:
  0.0 119.1 jit_solution(13697558452636832564)
XLA Ops:
  0.0 1.4 %copy-done = f32[6,16,32,128]{3,2,1,0:T(8,128)S(1)} copy-done((f32[6,16,32,128]{3,2,1,0:T(8,128)S(1)}, f32[6,16,32,128]{3,2,1,0:T(8,128)}, u32[]{:S(2)}) %copy-start) | copy-done | bytes 1572888
  1.4 0.9 copy-done.64
  3.0 0.8 edges.1
  3.8 1.7 %collective-permute-start = (f32[160,128]{1,0:T(8,128)S(1)}, f32[160,128]{1,0:T(8,128)S(1)}, u32[]{:S(2)}, u32[]{:S(2)}) collective-permute-start(f32[160,128]{1,0:T(8,128)S(1)} %get-tuple-element.55), channel_id=1, source_target_pairs={{0,8},{8,16},{16,24},{24,32},{32,40},{40,48},{48,56},{56,64},{64,7... | collective-permute-start | bytes 245768 | tf_op jit(solution)/shard_map/ppermute | solution.py:471
  5.6 3.7 %collective-permute-start.1 = (f32[160,128]{1,0:T(8,128)S(1)}, f32[160,128]{1,0:T(8,128)S(1)}, u32[]{:S(2)}, u32[]{:S(2)}) collective-permute-start(f32[160,128]{1,0:T(8,128)S(1)} %get-tuple-element.56), channel_id=1, source_target_pairs={{0,120},{8,0},{16,8},{24,16},{32,24},{40,32},{48,40},{56,48},{64,5... | collective-permute-start | bytes 245768 | tf_op jit(solution)/shard_map/ppermute | solution.py:471
  9.3 3.2 %collective-permute-start.3 = (f32[96,128]{1,0:T(8,128)S(1)}, f32[96,128]{1,0:T(8,128)S(1)}, u32[]{:S(2)}, u32[]{:S(2)}) collective-permute-start(f32[96,128]{1,0:T(8,128)S(1)} %get-tuple-element.58), channel_id=1, source_target_pairs={{0,7},{1,0},{2,1},{3,2},{4,3},{5,4},{6,5},{7,6},{8,15},{9,8},{10,9... | collective-permute-start | bytes 147464 | tf_op jit(solution)/shard_map/ppermute | solution.py:471
  12.5 1.8 %collective-permute-done.2.yl = f32[96,128]{1,0:T(8,128)S(1)} collective-permute-done((f32[96,128]{1,0:T(8,128)S(1)}, f32[96,128]{1,0:T(8,128)S(1)}, u32[]{:S(2)}, u32[]{:S(2)}) %collective-permute-start.2) | collective-permute-done | bytes 49184 | tf_op jit(solution)/shard_map/ppermute | solution.py:471
  14.7 1.2 copy-done.3
  15.8 0.7 copy-done.10
  16.6 0.7 copy-done.13
  17.3 0.7 copy-done.21
  18.0 0.7 copy-done.50
  18.8 0.7 copy-done.52
  19.5 0.9 y1.1
  20.4 0.7 copy-done.4
  21.2 0.8 copy-done.7
  21.9 0.7 copy-done.19
  22.6 17.1 %all_to_all.20 = f32[8,168,128]{2,1,0:T(8,128)} all-to-all(f32[8,168,128]{2,1,0:T(8,128)S(1)} %bitcast.21), channel_id=1, replica_groups=mesh['gx'=16,'gy'=8] {'gy'}, dimensions={0} | all-to-all | bytes 1376256 | tf_op jit(solution)/shard_map/all_to_all | solution.py:476
  39.8 4.4 %all-to-all-start = ((f32[16,208,128]{2,1,0:T(8,128)}), f32[16,208,128]{2,1,0:T(8,128)S(1)}, u32[]{:S(2)}, u32[]{:S(2)}) async-start(f32[16,208,128]{2,1,0:T(8,128)} %bitcast.19), calls=%async_computation | async-start | bytes 3407872 | tf_op jit(solution)/shard_map/all_to_all | solution.py:476
  44.3 1.2 %copy-done.2 = f32[8,168,128]{2,1,0:T(8,128)S(1)} copy-done((f32[8,168,128]{2,1,0:T(8,128)S(1)}, f32[8,168,128]{2,1,0:T(8,128)}, u32[]{:S(2)}) %copy-start.2) | copy-done | bytes 688152
  45.5 1.0 copy-done.5
  46.5 1.0 copy-done.8
  47.5 0.8 copy-done.29
  48.3 1.0 copy-done.33
  49.3 1.0 copy-done.55
  50.2 0.8 y2.1
  51.7 0.7 copy-done.36
  56.3 13.0 %all-to-all-done = f32[16,208,128]{2,1,0:T(8,128)S(1)} async-done(((f32[16,208,128]{2,1,0:T(8,128)}), f32[16,208,128]{2,1,0:T(8,128)S(1)}, u32[]{:S(2)}, u32[]{:S(2)}) %all-to-all-start) | async-done | bytes 1703968 | tf_op jit(solution)/shard_map/all_to_all | solution.py:476
  69.3 1.0 copy-done.11
  70.3 1.0 copy-done.14
  71.3 1.0 copy-done.17
  72.2 1.0 copy-done.20
  73.2 0.9 copy-done.22
  74.1 0.9 copy-done.26
  75.0 1.0 copy-done.51
  76.0 1.0 copy-done.53
  77.0 1.6 %x2.1 = (f32[680,128]{1,0:T(8,128)S(1)}, f32[512,128]{1,0:T(8,128)S(1)}, f32[1024,128]{1,0:T(8,128)}, f32[512,128]{1,0:T(8,128)S(1)}, f32[32,128]{1,0:T(8,128)S(...) custom-call(f32[3328,128]{1,0:T(8,128)S(1)} %bitcast.16, ...), custom_call_target="tpu_custom_call" | custom-call | flops 4000000 | bytes 4000000 | tf_op jit(solution)/shard_map/x2/pallas_call | solution.py:457
  78.5 0.7 copy-done.38
  79.2 0.8 copy-done.40
  80.0 0.7 copy-done.42
  80.7 0.7 copy-done.44
  82.4 0.7 copy-done.65
  83.1 0.7 copy-done.67
  83.9 9.4 %all_to_all.21 = f32[8,48,128]{2,1,0:T(8,128)S(1)} all-to-all(f32[8,48,128]{2,1,0:T(8,128)S(1)} %bitcast.23), channel_id=1, replica_groups=mesh['gx'=16,'gy'=8] {'gy'}, dimensions={0} | all-to-all | bytes 393216 | tf_op jit(solution)/shard_map/all_to_all | solution.py:476
  93.2 3.8 %all-to-all-start.2 = ((f32[16,64,128]{2,1,0:T(8,128)}), f32[16,64,128]{2,1,0:T(8,128)S(1)}, u32[]{:S(2)}, u32[]{:S(2)}) async-start(f32[16,64,128]{2,1,0:T(8,128)} %bitcast.6), calls=%async_computation.2 | async-start | bytes 1048576 | tf_op jit(solution)/shard_map/all_to_all | solution.py:476
  97.1 1.0 copy-done.66
  98.1 0.9 copy-done.68
  99.1 0.9 copy-done.70
  100.0 0.9 copy-done.72
  100.9 0.9 copy-done.74
  101.8 0.9 copy-done.76
  102.7 0.9 copy-done.78
  103.6 0.9 copy-done.80
  108.3 1.0 copy-done.39
  109.3 1.0 copy-done.41
  110.2 1.0 copy-done.45
  111.2 1.0 copy-done.47
  112.2 1.0 copy-done.49
  113.2 0.9 copy-done.57
  114.1 0.9 copy-done.59
  115.1 0.9 copy-done.61
  116.0 0.9 copy-done.63
  117.0 0.7 copy-done.82
  117.7 1.4 %x4.1 = f32[3072,128]{1,0:T(8,128)} custom-call(f32[1024,128]{1,0:T(8,128)S(1)} %bitcast.18, f32[640,128]{1,0:T(8,128)S(1)} %copy-done.12, f32[640,128]{1,0:T(8,128)S(1)} %copy-done.15, f32[512,128]{1,0:T(8,128)S(1)} %copy-done.57, f32[32,128]{1,0:T(8,128)S(1)} %copy-done.82, f32[160,128]{1,0:T(8,128)S(1)} %copy-done.27, f32[640,128]{1,0:T(8,128)S(1)} %copy-done.43, ...), custom_call_target="tpu_custom_call" | custom-call | flops 4000000 | bytes 4000000 | tf_op jit(solution)/shard_map/x4/pallas_call | solution.py:457
  (130 shorter events, 10.4 us)
Async XLA Ops:
  0.0 1.4 %copy-start = (f32[6,16,32,128]{3,2,1,0:T(8,128)S(1)}, f32[6,16,32,128]{3,2,1,0:T(8,128)}, u32[]{:S(2)}) copy-start(f32[6,16,32,128]{3,2,1,0:T(8,128)} %param.3) | copy-start | bytes 4718596
  1.4 0.9 copy-start.64
  3.8 10.4 %collective-permute-start = (f32[160,128]{1,0:T(8,128)S(1)}, f32[160,128]{1,0:T(8,128)S(1)}, u32[]{:S(2)}, u32[]{:S(2)}) collective-permute-start(f32[160,128]{1,0:T(8,128)S(1)} %get-tuple-element.55), channel_id=1, source_target_pairs={{0,8},{8,16},{16,24},{24,32},{32,40},{40,48},{48,56},{56,64},{64,7... | collective-permute-start | bytes 245768 | tf_op jit(solution)/shard_map/ppermute | solution.py:471
  5.6 8.7 %collective-permute-start.1 = (f32[160,128]{1,0:T(8,128)S(1)}, f32[160,128]{1,0:T(8,128)S(1)}, u32[]{:S(2)}, u32[]{:S(2)}) collective-permute-start(f32[160,128]{1,0:T(8,128)S(1)} %get-tuple-element.56), channel_id=1, source_target_pairs={{0,120},{8,0},{16,8},{24,16},{32,24},{40,32},{48,40},{56,48},{64,5... | collective-permute-start | bytes 245768 | tf_op jit(solution)/shard_map/ppermute | solution.py:471
  9.3 5.0 %collective-permute-start.2 = (f32[96,128]{1,0:T(8,128)S(1)}, f32[96,128]{1,0:T(8,128)S(1)}, u32[]{:S(2)}, u32[]{:S(2)}) collective-permute-start(f32[96,128]{1,0:T(8,128)S(1)} %get-tuple-element.57), channel_id=1, source_target_pairs={{0,1},{1,2},{2,3},{3,4},{4,5},{5,6},{6,7},{7,0},{8,9},{9,10},{10,1... | collective-permute-start | bytes 147464 | tf_op jit(solution)/shard_map/ppermute | solution.py:471
  9.3 5.0 %collective-permute-start.3 = (f32[96,128]{1,0:T(8,128)S(1)}, f32[96,128]{1,0:T(8,128)S(1)}, u32[]{:S(2)}, u32[]{:S(2)}) collective-permute-start(f32[96,128]{1,0:T(8,128)S(1)} %get-tuple-element.58), channel_id=1, source_target_pairs={{0,7},{1,0},{2,1},{3,2},{4,3},{5,4},{6,5},{7,6},{8,15},{9,8},{10,9... | collective-permute-start | bytes 147464 | tf_op jit(solution)/shard_map/ppermute | solution.py:471
  14.3 6.2 %copy-start.23 = (f32[160,128]{1,0:T(8,128)}, f32[160,128]{1,0:T(8,128)S(1)}, u32[]{:S(2)}) copy-start(f32[160,128]{1,0:T(8,128)S(1)} %collective-permute-done.1.xr) | copy-start | bytes 245764
  14.6 1.2 copy-start.3
  19.5 20.3 %copy-start.25 = (f32[160,128]{1,0:T(8,128)}, f32[160,128]{1,0:T(8,128)S(1)}, u32[]{:S(2)}) copy-start(f32[160,128]{1,0:T(8,128)S(1)} %get-tuple-element.61.order.hb) | copy-start | bytes 245764
  22.6 17.2 %copy-start.28 = (f32[96,128]{1,0:T(8,128)}, f32[96,128]{1,0:T(8,128)S(1)}, u32[]{:S(2)}) copy-start(f32[96,128]{1,0:T(8,128)S(1)} %get-tuple-element.68.hb) | copy-start | bytes 147460
  22.6 17.2 %copy-start.32 = (f32[768,128]{1,0:T(8,128)}, f32[768,128]{1,0:T(8,128)S(1)}, u32[]{:S(2)}) copy-start(f32[768,128]{1,0:T(8,128)S(1)} %get-tuple-element.67.v) | copy-start | bytes 1179652
  22.6 17.2 %copy-start.34 = (f32[768,128]{1,0:T(8,128)}, f32[768,128]{1,0:T(8,128)S(1)}, u32[]{:S(2)}) copy-start(f32[768,128]{1,0:T(8,128)S(1)} %get-tuple-element.87.m) | copy-start | bytes 1179652
  22.6 17.2 %copy-start.54 = (f32[544,128]{1,0:T(8,128)}, f32[544,128]{1,0:T(8,128)S(1)}, u32[]{:S(2)}) copy-start(f32[544,128]{1,0:T(8,128)S(1)} %get-tuple-element.64.p1) | copy-start | bytes 835588
  39.8 29.5 %all-to-all-start = ((f32[16,208,128]{2,1,0:T(8,128)}), f32[16,208,128]{2,1,0:T(8,128)S(1)}, u32[]{:S(2)}, u32[]{:S(2)}) async-start(f32[16,208,128]{2,1,0:T(8,128)} %bitcast.19), calls=%async_computation | async-start | bytes 3407872 | tf_op jit(solution)/shard_map/all_to_all | solution.py:476
  44.3 25.0 %copy-start.1 = (f32[6,16,32,128]{3,2,1,0:T(8,128)S(1)}, f32[6,16,32,128]{3,2,1,0:T(8,128)}, u32[]{:S(2)}) copy-start(f32[6,16,32,128]{3,2,1,0:T(8,128)} %param.3) | copy-start | bytes 4718596
  44.3 1.2 %copy-start.2 = (f32[8,168,128]{2,1,0:T(8,128)S(1)}, f32[8,168,128]{2,1,0:T(8,128)}, u32[]{:S(2)}) copy-start(f32[8,168,128]{2,1,0:T(8,128)} %all_to_all.20) | copy-start | bytes 2064388
  45.5 1.0 copy-start.5
  46.5 1.0 copy-start.8
  47.5 0.8 copy-start.29
  48.3 1.0 copy-start.33
  49.3 1.0 copy-start.55
  69.3 1.0 copy-start.11
  70.3 1.0 copy-start.14
  71.3 1.0 copy-start.17
  72.2 1.0 copy-start.20
  73.2 0.9 copy-start.22
  74.1 0.9 copy-start.26
  75.0 1.0 copy-start.51
  76.0 1.0 copy-start.53
  77.0 4.5 %copy-start.24 = (f32[160,128]{1,0:T(8,128)S(1)}, f32[160,128]{1,0:T(8,128)}, u32[]{:S(2)}) copy-start(f32[160,128]{1,0:T(8,128)} %copy-done.23) | copy-start | bytes 245764
  77.0 4.5 %copy-start.30 = (f32[96,128]{1,0:T(8,128)S(1)}, f32[96,128]{1,0:T(8,128)}, u32[]{:S(2)}) copy-start(f32[96,128]{1,0:T(8,128)} %copy-done.28) | copy-start | bytes 147460
  77.0 4.5 %copy-start.35 = (f32[768,128]{1,0:T(8,128)S(1)}, f32[768,128]{1,0:T(8,128)}, u32[]{:S(2)}) copy-start(f32[768,128]{1,0:T(8,128)} %copy-done.34) | copy-start | bytes 1179652
  77.0 4.5 %copy-start.37 = (f32[768,128]{1,0:T(8,128)S(1)}, f32[768,128]{1,0:T(8,128)}, u32[]{:S(2)}) copy-start(f32[768,128]{1,0:T(8,128)} %copy-done.36) | copy-start | bytes 1179652
  79.2 0.8 copy-start.40
  81.5 0.8 copy-start.48
  81.5 0.9 copy-start.56
  81.5 0.9 copy-start.81
  81.5 15.6 %copy-start.31 = (f32[96,128]{1,0:T(8,128)S(1)}, f32[96,128]{1,0:T(8,128)}, u32[]{:S(2)}) copy-start(f32[96,128]{1,0:T(8,128)} %copy-done.28) | copy-start | bytes 147460
  83.8 9.4 %copy-start.83 = (f32[24,128]{1,0:T(8,128)}, f32[24,128]{1,0:T(8,128)S(1)}, u32[]{:S(2)}) copy-start(f32[24,128]{1,0:T(8,128)S(1)} %get-tuple-element.91.vn2) | copy-start | bytes 36868
  83.9 13.2 %copy-start.6 = (f32[768,128]{1,0:T(8,128)S(1)}, f32[768,128]{1,0:T(8,128)}, u32[]{:S(2)}) copy-start(f32[768,128]{1,0:T(8,128)} %copy-done.4) | copy-start | bytes 1179652
  83.9 13.2 %copy-start.9 = (f32[768,128]{1,0:T(8,128)S(1)}, f32[768,128]{1,0:T(8,128)}, u32[]{:S(2)}) copy-start(f32[768,128]{1,0:T(8,128)} %copy-done.7) | copy-start | bytes 1179652
  93.2 15.0 %all-to-all-start.2 = ((f32[16,64,128]{2,1,0:T(8,128)}), f32[16,64,128]{2,1,0:T(8,128)S(1)}, u32[]{:S(2)}, u32[]{:S(2)}) async-start(f32[16,64,128]{2,1,0:T(8,128)} %bitcast.6), calls=%async_computation.2 | async-start | bytes 1048576 | tf_op jit(solution)/shard_map/all_to_all | solution.py:476
  97.0 11.2 %copy-start.12 = (f32[640,128]{1,0:T(8,128)S(1)}, f32[640,128]{1,0:T(8,128)}, u32[]{:S(2)}) copy-start(f32[640,128]{1,0:T(8,128)} %copy-done.10) | copy-start | bytes 983044
  97.0 11.2 %copy-start.15 = (f32[640,128]{1,0:T(8,128)S(1)}, f32[640,128]{1,0:T(8,128)}, u32[]{:S(2)}) copy-start(f32[640,128]{1,0:T(8,128)} %copy-done.13) | copy-start | bytes 983044
  97.0 11.2 %copy-start.18 = (f32[544,128]{1,0:T(8,128)S(1)}, f32[544,128]{1,0:T(8,128)}, u32[]{:S(2)}) copy-start(f32[544,128]{1,0:T(8,128)} %copy-done.16) | copy-start | bytes 835588
  97.1 11.2 %copy-start.27 = (f32[160,128]{1,0:T(8,128)S(1)}, f32[160,128]{1,0:T(8,128)}, u32[]{:S(2)}) copy-start(f32[160,128]{1,0:T(8,128)} %copy-done.25) | copy-start | bytes 245764
  97.1 11.2 %copy-start.43 = (f32[640,128]{1,0:T(8,128)S(1)}, f32[640,128]{1,0:T(8,128)}, u32[]{:S(2)}) copy-start(f32[640,128]{1,0:T(8,128)} %copy-done.42) | copy-start | bytes 983044
  97.1 1.0 copy-start.66
  98.1 0.9 copy-start.68
  99.1 0.9 copy-start.70
  100.0 0.9 copy-start.72
  100.9 0.9 copy-start.74
  101.8 0.9 copy-start.76
  102.7 0.9 copy-start.78
  103.6 0.9 copy-start.80
  108.3 1.0 copy-start.39
  109.3 1.0 copy-start.41
  110.2 1.0 copy-start.45
  111.2 1.0 copy-start.47
  112.2 1.0 copy-start.49
  113.2 0.9 copy-start.57
  114.1 0.9 copy-start.59
  115.1 0.9 copy-start.61
  116.0 0.9 copy-start.63
  (28 other events, 19.7 us)
where the time goes:
time: 121 us; the launch traced here: 119 us
  local copies, waits for them, and re-layouts  53.1 us (44%)
  blocking collectives  26.5 us (22%)
  starting transfers between devices  16.9 us (14%)
  waiting for transfers between devices  15.2 us (13%)
  Pallas kernels  7.04 us (6%)
    unnamed x172, local copies, waits for them, and re-layouts  53.1 us
    all_to_all x2, blocking collectives, swap(): got = lax.all_to_all(msg.reshape(n, -1, PZ), axis, 0, 0, tiled=True)  26.5 us
    all_to_all x2, waiting for transfers between devices, swap(): got = lax.all_to_all(msg.reshape(n, -1, PZ), axis, 0, 0, tiled=True)  13.4 us
    ppermute x4, starting transfers between devices, ring(): return lax.ppermute(block, axis, [(i, (i + step) % n) for i in range(n)])  8.64 us
    all_to_all x2, starting transfers between devices, swap(): got = lax.all_to_all(msg.reshape(n, -1, PZ), axis, 0, 0, tiled=True)  8.25 us
    pallas_call x8, Pallas kernels, call(): pl.pallas_call(kernel, out_shape=rows_of(*outs), in_specs=[sm if i in sme...  7.04 us
  transfers between devices with their start and end apart: 6, of which 3 were waited for; matrix products, arithmetic and copies ran while one was open for 0% of the time, Pallas kernels for 1%

commit v1 on v0

--- a/solution.py
+++ b/solution.py
@@ -184,7 +184,7 @@
     spread(msg, n, (pf, plast, a, bb, c, qq))
 
 
-def k_y1(f, eps, xl, xr, order, msg, p1, ey1, m, h, b, v, hb, r, ep):
+def k_y1(f, eps, xl, xr, msg, p1, ey1, m, h, b, v, hb, r, ep):
     gx = lax.axis_index("gx")
     gy = lax.axis_index("gy")
     n = lax.axis_size("gy")
@@ -244,7 +244,7 @@
     qq = jnp.concatenate([lastrow(p1, 0, PX), lastrow(p1, PX, 1), tail], 0) * (-1.0 / 32.0)
     tail = jnp.zeros((6, PZ), F32)
     ee = fz(jnp.concatenate([lastrow(ey1, 0, PX), zero, lastrow(ey1, PX, 1), tail], 0))
-    spread(msg, n, (pf, plast, a, bb, c, qq, ee))
+    spread(msg, 1, (pf, plast, a, bb, c, qq, ee))
 
 
 def coefficients(part, n, rows, tp, bp, ts, bs, bet, dele):
@@ -403,10 +403,10 @@
     last, vn = sweep(m_at, lambda j: r[pl.ds(j, YR, stride=PY), :], PY, v2, YR)
     vn2[...] = vn
     pf, plast = ends(last, vn, plane(hb, 0, YR), plane(hb, 2, YR))
-    spread(msg2, n, (pf, plast))
-
-
-def k_y4(msg, h, b, v2, vn2, hb, tp, bp, ts, bs, bet, dele, ex2, hy1, q2, ez2, hx2, hy2, al, ga, w2, dw):
+    spread(msg2, 1, (pf, plast))
+
+
+def k_y4(msg, h, b, v2, vn2, hb, tp, bp, ts, bs, bet, dele, ex2, hy1, q2, out, al, ga, w2, dw):
     n = lax.axis_size("gy")
     me = lax.axis_index("gy")
     part = lambda j, k: msg[pl.ds((2 * j + k) * YR, YR), :]
@@ -423,12 +423,14 @@
     for x in range(PX):
         w = plane(w2, x)
         nxt = plane(w2, x + 1) if x < PX - 1 else xon * plane(w2, PX + 1)
-        put(ez2, x, w)
-        put(hx2, x, plane(q2, x) - 32.0 * plane(dw, x))
-        put(hy2, x, plane(hy1, x) - 0.5 * fz(plane(ex2, x)) + 32.0 * (nxt - w))
-
-
-def k_x4(msg, h, b, v2, vn2, hb, tp, bp, ts, bs, bet, dele, p2, ex2, ez2, hx2, hy2, out, al, ga):
+        e2 = plane(ex2, x)
+        put(out, EX * PX + x, e2)
+        put(out, EZ * PX + x, w)
+        put(out, HX * PX + x, plane(q2, x) - 32.0 * plane(dw, x))
+        put(out, HY * PX + x, plane(hy1, x) - 0.5 * fz(e2) + 32.0 * (nxt - w))
+
+
+def k_x4(msg, h, b, v2, vn2, hb, tp, bp, ts, bs, bet, dele, p2, out, al, ga):
     n = lax.axis_size("gx")
     me = lax.axis_index("gx")
     part = lambda j, k: msg[pl.ds((2 * j + k) * PY, PY), :]
@@ -441,29 +443,71 @@
         put(out, EY * PX + x, w)
         put(out, HZ * PX + x, plane(p2, x) - 32.0 * (later - w))
         later = w
-        put(out, EX * PX + x, plane(ex2, x))
-        put(out, EZ * PX + x, plane(ez2, x))
-        put(out, HX * PX + x, plane(hx2, x))
-        put(out, HY * PX + x, plane(hy2, x))
-
-
-def rows_of(*counts):
-    return [jax.ShapeDtypeStruct((c, PZ), F32) for c in counts]
-
-
-def call(kernel, outs, args, scratch=(), smem=(), name=None):
-    vm = pl.BlockSpec(memory_space=pltpu.VMEM)
-    sm = pl.BlockSpec(memory_space=pltpu.SMEM)
-    return pl.pallas_call(
-        kernel,
-        out_shape=rows_of(*outs),
-        in_specs=[sm if i in smem else vm for i in range(len(args))],
-        out_specs=[vm] * len(outs),
-        scratch_shapes=[pltpu.VMEM((c, PZ), F32) for c in scratch],
-        compiler_params=pltpu.CompilerParams(vmem_limit_bytes=24 * 1024 * 1024),
-        cost_estimate=pl.CostEstimate(flops=4_000_000, bytes_accessed=4_000_000, transcendentals=0),
+
+
+def call(name, parts, args, outs, scratch=(), smem=(), into=(), flush=()):
+    into, flush, scratch = dict(into), dict(flush), dict(scratch)
+    moved = [k for k in args if k not in smem]
+    pieces = {k for group in flush.values() for k, _, _ in group}
+    last = {k: max(i for i, (_, used) in enumerate(parts) if k in used) for k in outs}
+    leave = [
+        [(k, 0, outs[k]) for k in outs if last[k] == i and k not in pieces] + list(flush.get(i, ()))
+        for i in range(len(parts))
+    ]
+    own = [k for k in moved if k not in into]
+
+    def body(*refs):
+        take = iter(refs)
+        hbm = {k: next(take) for k in args}
+        results = {k: next(take) for k in outs}
+        env = {k: next(take) for k in own}
+        env.update({k: next(take) for k in outs})
+        env.update({k: next(take) for k in scratch})
+        env.update({k: hbm[k] for k in smem})
+        sem_in, sem_out = next(take), next(take)
+        pending = {}
+        for i, k in enumerate(moved):
+            where = env.get(k)
+            if k in into:
+                buffer, row = into[k]
+                where = env[buffer].at[pl.ds(row(), args[k].shape[0]), :]
+            copy = pltpu.make_async_copy(hbm[k], where, sem_in.at[i])
+            copy.start()
+            pending.setdefault(into[k][0] if k in into else k, []).append(copy)
+        sent = []
+        for i, (function, used) in enumerate(parts):
+            for k in used:
+                for copy in pending.pop(k, ()):
+                    copy.wait()
+            function(*[env[k] for k in used])
+            for k, row, rows in leave[i]:
+                window = pl.ds(row, rows)
+                copy = pltpu.make_async_copy(
+                    env[k].at[window, :], results[k].at[window, :], sem_out.at[len(sent)]
+                )
+                copy.start()
+                sent.append(copy)
+        for copy in sent:
+            copy.wait()
+
+    anywhere = pl.BlockSpec(memory_space=pl.ANY)
+    scalars = pl.BlockSpec(memory_space=pltpu.SMEM)
+    got = pl.pallas_call(
+        body,
+        out_shape=[jax.ShapeDtypeStruct((c, PZ), F32) for c in outs.values()],
+        in_specs=[scalars if k in smem else anywhere for k in args],
+        out_specs=[anywhere] * len(outs),
+        scratch_shapes=[pltpu.VMEM(args[k].shape, args[k].dtype) for k in own]
+        + [pltpu.VMEM((c, PZ), F32) for c in list(outs.values()) + list(scratch.values())]
+        + [
+            pltpu.SemaphoreType.DMA((len(moved),)),
+            pltpu.SemaphoreType.DMA((sum(len(group) for group in leave),)),
+        ],
+        compiler_params=pltpu.CompilerParams(vmem_limit_bytes=56 * 1024 * 1024),
+        cost_estimate=pl.CostEstimate(flops=1000, bytes_accessed=1000, transcendentals=0),
         name=name,
-    )(*args)
+    )(*args.values())
+    return dict(zip(outs, got))
 
 
 def ring(block, axis, step):
@@ -477,75 +521,126 @@
     return got.reshape(-1, PZ)
 
 
+def from_all(msg, axis, buffer):
+    n = lax.axis_size(axis)
+    rows = msg.shape[0]
+    args, into = {}, {}
+    for step in range(n):
+        k = buffer + str(step)
+        args[k] = ring(msg, axis, step) if step else msg
+
+        def row(step=step):
+            return pl.multiple_of(lax.rem(lax.axis_index(axis) - step + n, n) * rows, 8)
+
+        into[k] = (buffer, row)
+    return args, into
+
+
 def local(fields, region, eps_table):
     nx = lax.axis_size("gx")
     ny = lax.axis_size("gy")
     cells = PX * PY
+    nxl, nyl = PX * XR, PY * YR
     f = fields.reshape(6 * cells, PZ)
     reg = region.reshape(cells, PZ)
-    eps, xup, xdn, yup, ydn = call(
-        k_edges, (cells, 5 * PY, 5 * PY, 6 * PX, 6 * PX), (f, reg, eps_table), smem=(2,), name="edges"
+    halo = ("xup", "xdn", "yup", "ydn")
+    got = call(
+        "edges",
+        [(k_edges, ("f", "reg", "table", "eps") + halo)],
+        dict(f=f, reg=reg, table=eps_table),
+        dict(eps=cells, xup=5 * PY, xdn=5 * PY, yup=6 * PX, ydn=6 * PX),
+        smem=("table",),
     )
-    xl = ring(xup, "gx", 1)
-    xr = ring(xdn, "gx", -1)
-    yl = ring(yup, "gy", 1)
-    yr = ring(ydn, "gy", -1)
-    nxl, nyl = PX * XR, PY * YR
-    msgx, q1, mx, hx, bx, vx, hbx = call(
-        k_x1,
-        (nx * (5 * XR + 8), cells, nxl, nxl, nxl, nxl, 4 * XR),
-        (f, eps, xl, xr, yl, yr),
-        (nxl,),
-        name="x1",
+    base = dict(f=f, eps=got["eps"])
+    xl = ring(got["xup"], "gx", 1)
+    xr = ring(got["xdn"], "gx", -1)
+    yl = ring(got["yup"], "gy", 1)
+    yr = ring(got["ydn"], "gy", -1)
+    linex = ("mx", "hx", "bx", "vx", "hbx")
+    liney = ("my", "hy", "by", "vy", "hby")
+    one = call(
+        "one",
+        [
+            (k_x1, ("f", "eps", "xl", "xr", "yl", "yr", "msgx", "q1") + linex + ("r",)),
+            (k_y1, ("f", "eps", "xl", "xr", "msgy", "p1", "ey1") + liney + ("rt", "ep")),
+        ],
+        dict(base, xl=xl, xr=xr, yl=yl, yr=yr),
+        dict(
+            zip(
+                ("msgx", "q1") + linex + ("msgy", "p1", "ey1") + liney,
+                (nx * (5 * XR + 8), cells, nxl, nxl, nxl, nxl, 4 * XR)
+                + (7 * YR, cells + PY, cells + PY, nyl, nyl, nyl, nyl, 4 * YR),
+            )
+        ),
+        dict(r=nxl, rt=YR * PY, ep=YR * PY),
     )
-    gotx = swap(msgx, "gx")
-    msgy, p1, ey1, my, hy, by, vy, hby = call(
-        k_y1,
-        (ny * 7 * YR, cells + PY, cells + PY, nyl, nyl, nyl, nyl, 4 * YR),
-        (f, eps, xl, xr, hbx),
-        (YR * PY, YR * PY),
-        name="y1",
+    gotx = swap(one["msgx"], "gx")
+    argy, into = from_all(one["msgy"], "gy", "gy")
+    chains = ("tp", "bp", "ts", "bs", "bet", "del")
+    cx, cy = [tuple(k + a for k in chains) for a in "xy"]
+    size = lambda n, rows: (n * rows,) * 4 + ((n + 1) * rows,) * 2
+    keep = {k: one[k] for k in ("q1", "p1", "ey1") + linex + liney}
+    two = call(
+        "two",
+        [
+            (k_y2, ("gy", "p1", "hy", "by", "vy", "hby", "ex1", "p2", "elo") + cy + ("aly", "gay", "dex")),
+            (
+                k_x2,
+                ("gx", "f", "eps", "q1", "ey1", "p2", "hx", "bx", "vx", "mx", "hbx")
+                + ("ez1", "hx1", "msgx2", "vx2", "vnx2")
+                + cx
+                + ("alx", "gax", "r"),
+            ),
+            (
+                k_y3,
+                ("f", "xr", "q1", "eps", "ey1", "ez1", "hx1", "ex1", "elo", "my", "hby")
+                + ("msgy2", "vy2", "vny2", "ex2", "hy1", "q2", "rt"),
+            ),
+        ],
+        dict(argy, gx=gotx, xr=xr, **base, **keep),
+        dict(
+            zip(
+                ("p2",) + cy + ("msgx2", "vx2", "vnx2") + cx + ("msgy2", "vy2", "vny2", "ex2", "hy1", "q2"),
+                (cells + PY,)
+                + size(ny, YR)
+                + (nx * 2 * PY, cells, PY)
+                + size(nx, XR)
+                + (2 * YR, nyl, YR, cells, cells, cells),
+            )
+        ),
+        dict(
+            gy=ny * 7 * YR, ex1=YR * PY, elo=YR, aly=(ny + 1) * YR, gay=(ny + 1) * YR, dex=YR * PY,
+            ez1=nxl + XR, hx1=cells, alx=(nx + 1) * XR, gax=(nx + 1) * XR, r=cells, rt=YR * PY,
+        ),
+        into=into,
     )
-    goty = swap(msgy, "gy")
-    chain = lambda n, rows: (n * rows,) * 4 + ((n + 1) * rows,) * 2
-    ex1, p2, elo, *cy = call(
-        k_y2,
-        (YR * PY, cells + PY, YR) + chain(ny, YR),
-        (goty, p1, hy, by, vy, hby),
-        ((ny + 1) * YR, (ny + 1) * YR, YR * PY),
-        name="y2",
+    gotx = swap(two["msgx2"], "gx")
+    argy, into = from_all(two["msgy2"], "gy", "gy")
+    need = {k: one[k] for k in ("hx", "bx", "hbx", "hy", "by", "hby")}
+    need.update({k: two[k] for k in ("p2",) + cy + cx + ("vx2", "vnx2", "vy2", "vny2", "ex2", "hy1", "q2")})
+    three = call(
+        "three",
+        [
+            (
+                k_y4,
+                ("gy", "hy", "by", "vy2", "vny2", "hby") + cy + ("ex2", "hy1", "q2", "out")
+                + ("aly", "gay", "w2", "dw"),
+            ),
+            (k_x4, ("gx", "hx", "bx", "vx2", "vnx2", "hbx") + cx + ("p2", "out", "alx", "gax")),
+        ],
+        dict(argy, gx=gotx, **need),
+        dict(out=6 * cells),
+        dict(
+            gy=ny * 2 * YR, aly=(ny + 1) * YR, gay=(ny + 1) * YR, w2=YR * PY, dw=YR * PY,
+            alx=(nx + 1) * PY, gax=(nx + 1) * PY,
+        ),
+        into=into,
+        flush={
+            0: [("out", EX * cells, cells), ("out", EZ * cells, 3 * cells)],
+            1: [("out", EY * cells, cells), ("out", HZ * cells, cells)],
+        },
     )
-    ez1, hx1, msgx2, vx2, vnx2, *cx = call(
-        k_x2,
-        (nxl + XR, cells, nx * 2 * PY, cells, PY) + chain(nx, XR),
-        (gotx, f, eps, q1, ey1, p2, hx, bx, vx, mx, hbx),
-        ((nx + 1) * XR, (nx + 1) * XR, cells),
-        name="x2",
-    )
-    gotx2 = swap(msgx2, "gx")
-    msgy2, vy2, vny2, ex2, hy1, q2 = call(
-        k_y3,
-        (ny * 2 * YR, nyl, YR, cells, cells, cells),
-        (f, xr, q1, eps, ey1, ez1, hx1, ex1, elo, my, hby),
-        (YR * PY,),
-        name="y3",
-    )
-    goty2 = swap(msgy2, "gy")
-    ez2, hx2, hy2 = call(
-        k_y4,
-        (cells, cells, cells),
-        (goty2, hy, by, vy2, vny2, hby, *cy, ex2, hy1, q2),
-        ((ny + 1) * YR, (ny + 1) * YR, YR * PY, YR * PY),
-        name="y4",
-    )
-    (out,) = call(
-        k_x4,
-        (6 * cells,),
-        (gotx2, hx, bx, vx2, vnx2, hbx, *cx, p2, ex2, ez2, hx2, hy2),
-        ((nx + 1) * PY, (nx + 1) * PY),
-        name="x4",
-    )
-    return out.reshape(6, PX, PY, PZ)
+    return three["out"].reshape(6, PX, PY, PZ)
 
 
 def solution(mesh):

time: 121 us -> 80.9 us (0.67)
  local copies, waits for them, and re-layouts: 53.1 us -> 2.6 us
  blocking collectives: 26.5 us -> 0 us
  starting transfers between devices: 16.9 us -> 32.5 us
  Pallas kernels: 7.04 us -> 20 us
  waiting for transfers between devices: 15.2 us -> 24.8 us
    unnamed x172 -> x42, local copies, waits for them, and re-layouts: 53.1 us -> 2.6 us
    all_to_all x2 -> x0, blocking collectives: 26.5 us -> none  [swap(): got = lax.all_to_all(msg.reshape(n, -1, PZ), axis, 0, 0, tiled=True)]
    ppermute x4 -> x18, starting transfers between devices: 8.64 us -> 24.7 us  [ring(): return lax.ppermute(block, axis, [(i, (i + step) % n) for i in range(n)])]
    pallas_call x8 -> x4, Pallas kernels: 7.04 us -> 20 us  [call(): pl.pallas_call(body, out_shape=[jax.ShapeDtypeStruct((c, PZ), F32) for c...]
    ppermute x4 -> x18, waiting for transfers between devices: 1.78 us -> 14.1 us  [ring(): return lax.ppermute(block, axis, [(i, (i + step) % n) for i in range(n)])]
    all_to_all x2, waiting for transfers between devices: 13.4 us -> 10.7 us  [swap(): got = lax.all_to_all(msg.reshape(n, -1, PZ), axis, 0, 0, tiled=True)]
  transfers between devices with their start and end apart: 6 -> 20, of which waited for: 3 -> 13; matrix products, arithmetic and copies ran while one was open for 0% -> 0% of each run, Pallas kernels for 1% -> 0%
where the time goes in v1:
time: 80.9 us; the launch traced here: 80 us
  starting transfers between devices  32.5 us (40%)
  waiting for transfers between devices  24.8 us (31%)
  Pallas kernels  20 us (25%)
  local copies, waits for them, and re-layouts  2.6 us (3%)
    ppermute x18, starting transfers between devices, ring(): return lax.ppermute(block, axis, [(i, (i + step) % n) for i in range(n)])  24.7 us
    pallas_call x4, Pallas kernels, call(): pl.pallas_call(body, out_shape=[jax.ShapeDtypeStruct((c, PZ), F32) for c...  20 us
    ppermute x18, waiting for transfers between devices, ring(): return lax.ppermute(block, axis, [(i, (i + step) % n) for i in range(n)])  14.1 us
    all_to_all x2, waiting for transfers between devices, swap(): got = lax.all_to_all(msg.reshape(n, -1, PZ), axis, 0, 0, tiled=True)  10.7 us
    all_to_all x2, starting transfers between devices, swap(): got = lax.all_to_all(msg.reshape(n, -1, PZ), axis, 0, 0, tiled=True)  7.77 us
    unnamed x42, local copies, waits for them, and re-layouts  2.6 us
  transfers between devices with their start and end apart: 20, of which 13 were waited for; matrix products, arithmetic and copies ran while one was open for 0% of the time, Pallas kernels for 0%

profile of v1, /device:TPU:0, one launch (start us, length us, event | category | flops | bytes accessed | tf_op | source)
XLA Modules:
  0.0 80.0 jit_solution(2775709745159586843)
XLA Ops:
  0.0 3.1 %edges.1 = (f32[512,128]{1,0:T(8,128)}, f32[160,128]{1,0:T(8,128)}, f32[160,128]{1,0:T(8,128)}, f32[96,128]{1,0:T(8,128)}, f32[96,128]{1,0:T(8,128)}) custom-call(f32[3072,128]{1,0:T(8,128)} %bitcast.7, s32[512,128]{1,0:T(8,128)} %bitcast.14, f32[16]{0:T(128)} %refs_2_.1), custom_call_target="tpu_custom_call" | custom-call | flops 1000 | bytes 1000 | tf_op jit(solution)/shard_map/edges/pallas_call | solution.py:495
  3.1 1.7 %collective-permute-start = (f32[160,128]{1,0:T(8,128)}, f32[160,128]{1,0:T(8,128)S(1)}, u32[]{:S(2)}, u32[]{:S(2)}) collective-permute-start(f32[160,128]{1,0:T(8,128)} %get-tuple-element.48), channel_id=1, source_target_pairs={{0,8},{8,16},{16,24},{24,32},{32,40},{40,48},{48,56},{56,64},{64,7... | collective-permute-start | bytes 245768 | tf_op jit(solution)/shard_map/ppermute | solution.py:515
  4.9 3.7 %collective-permute-start.1 = (f32[160,128]{1,0:T(8,128)}, f32[160,128]{1,0:T(8,128)S(1)}, u32[]{:S(2)}, u32[]{:S(2)}) collective-permute-start(f32[160,128]{1,0:T(8,128)} %get-tuple-element.49), channel_id=1, source_target_pairs={{0,120},{8,0},{16,8},{24,16},{32,24},{40,32},{48,40},{56,48},{64,5... | collective-permute-start | bytes 245768 | tf_op jit(solution)/shard_map/ppermute | solution.py:515
  8.6 0.0 collective-permute-start.2
  8.6 3.2 %collective-permute-start.3 = (f32[96,128]{1,0:T(8,128)}, f32[96,128]{1,0:T(8,128)S(1)}, u32[]{:S(2)}, u32[]{:S(2)}) collective-permute-start(f32[96,128]{1,0:T(8,128)} %get-tuple-element.51), channel_id=1, source_target_pairs={{0,7},{1,0},{2,1},{3,2},{4,3},{5,4},{6,5},{7,6},{8,15},{9,8},{10,9... | collective-permute-start | bytes 147464 | tf_op jit(solution)/shard_map/ppermute | solution.py:515
  11.8 2.0 %collective-permute-done.2.refs_4_ = f32[96,128]{1,0:T(8,128)S(1)} collective-permute-done((f32[96,128]{1,0:T(8,128)}, f32[96,128]{1,0:T(8,128)S(1)}, u32[]{:S(2)}, u32[]{:S(2)}) %collective-permute-start.2) | collective-permute-done | bytes 49184 | tf_op jit(solution)/shard_map/ppermute | solution.py:515
  13.7 0.1 collective-permute-done.3.refs_5_
  13.8 0.0 collective-permute-done.refs_2_
  13.8 0.0 collective-permute-done.1.refs_3_.refs_9_
  13.8 0.0 copy-start.2
  13.9 0.5 copy-done.12
  14.4 0.1 copy-done.13
  14.5 0.0 copy-done.11
  14.5 0.0 copy-done.2
  14.5 4.8 %one.1 = (f32[3328,128]{1,0:T(8,128)}, f32[512,128]{1,0:T(8,128)}, f32[640,128]{1,0:T(8,128)}, f32[640,128]{1,0:T(8,128)}, f32[640,128]{1,0:T(8,128)}, /*index=5...) custom-call(f32[3072,128]{1,0:T(8,128)} %bitcast.8, ...), custom_call_target="tpu_custom_call" | custom-call | flops 1000 | bytes 1000 | tf_op jit(solution)/shard_map/one/pallas_call | solution.py:495
  19.4 0.0 copy-start.3
  19.4 4.2 %all-to-all-start = ((f32[16,208,128]{2,1,0:T(8,128)}), f32[16,208,128]{2,1,0:T(8,128)S(1)}, u32[]{:S(2)}, u32[]{:S(2)}) async-start(f32[16,208,128]{2,1,0:T(8,128)} %bitcast.12), calls=%async_computation | async-start | bytes 3407872 | tf_op jit(solution)/shard_map/all_to_all | solution.py:520
  23.6 0.0 copy-done.3
  23.6 2.5 %collective-permute-start.10 = (f32[168,128]{1,0:T(8,128)S(1)}, f32[168,128]{1,0:T(8,128)S(1)}, u32[]{:S(2)}, u32[]{:S(2)}) collective-permute-start(f32[168,128]{1,0:T(8,128)S(1)} %copy-done.3), channel_id=1, source_target_pairs={{0,7},{1,0},{2,1},{3,2},{4,3},{5,4},{6,5},{7,6},{8,15},{9,8},{10,9... | collective-permute-start | bytes 258056 | tf_op jit(solution)/shard_map/ppermute | solution.py:515
  26.1 1.6 %collective-permute-start.9 = (f32[168,128]{1,0:T(8,128)S(1)}, f32[168,128]{1,0:T(8,128)S(1)}, u32[]{:S(2)}, u32[]{:S(2)}) collective-permute-start(f32[168,128]{1,0:T(8,128)S(1)} %copy-done.3), channel_id=1, source_target_pairs={{0,6},{1,7},{2,0},{3,1},{4,2},{5,3},{6,4},{7,5},{8,14},{9,15},{10,... | collective-permute-start | bytes 258056 | tf_op jit(solution)/shard_map/ppermute | solution.py:515
  27.8 0.0 collective-permute-start.8
  27.8 3.3 %collective-permute-start.7 = (f32[168,128]{1,0:T(8,128)S(1)}, f32[168,128]{1,0:T(8,128)S(1)}, u32[]{:S(2)}, u32[]{:S(2)}) collective-permute-start(f32[168,128]{1,0:T(8,128)S(1)} %copy-done.3), channel_id=1, source_target_pairs={{0,4},{1,5},{2,6},{3,7},{4,0},{5,1},{6,2},{7,3},{8,12},{9,13},{10,... | collective-permute-start | bytes 258056 | tf_op jit(solution)/shard_map/ppermute | solution.py:515
  31.1 0.0 collective-permute-start.6
  31.1 0.0 collective-permute-done.10.refs_7_
  31.1 0.1 collective-permute-start.5
  31.2 0.1 collective-permute-done.9.refs_6_
  31.3 0.9 %collective-permute-start.4 = (f32[168,128]{1,0:T(8,128)S(1)}, f32[168,128]{1,0:T(8,128)S(1)}, u32[]{:S(2)}, u32[]{:S(2)}) collective-permute-start(f32[168,128]{1,0:T(8,128)S(1)} %copy-done.3), channel_id=1, source_target_pairs={{0,1},{1,2},{2,3},{3,4},{4,5},{5,6},{6,7},{7,0},{8,9},{9,10},{10,1... | collective-permute-start | bytes 258056 | tf_op jit(solution)/shard_map/ppermute | solution.py:515
  32.2 0.4 collective-permute-done.8.refs_5_
  32.6 2.6 %collective-permute-done.7.refs_4_ = f32[168,128]{1,0:T(8,128)S(1)} collective-permute-done((f32[168,128]{1,0:T(8,128)S(1)}, f32[168,128]{1,0:T(8,128)S(1)}, u32[]{:S(2)}, u32[]{:S(2)}) %collective-permute-start.7) | collective-permute-done | bytes 86048 | tf_op jit(solution)/shard_map/ppermute | solution.py:515
  35.2 2.2 %collective-permute-done.6.refs_3_ = f32[168,128]{1,0:T(8,128)S(1)} collective-permute-done((f32[168,128]{1,0:T(8,128)S(1)}, f32[168,128]{1,0:T(8,128)S(1)}, u32[]{:S(2)}, u32[]{:S(2)}) %collective-permute-start.6) | collective-permute-done | bytes 86048 | tf_op jit(solution)/shard_map/ppermute | solution.py:515
  37.5 2.2 %collective-permute-done.5.refs_2_ = f32[168,128]{1,0:T(8,128)S(1)} collective-permute-done((f32[168,128]{1,0:T(8,128)S(1)}, f32[168,128]{1,0:T(8,128)S(1)}, u32[]{:S(2)}, u32[]{:S(2)}) %collective-permute-start.5) | collective-permute-done | bytes 86048 | tf_op jit(solution)/shard_map/ppermute | solution.py:515
  39.7 0.1 collective-permute-done.4.refs_1_
  39.8 10.7 %all-to-all-done = f32[16,208,128]{2,1,0:T(8,128)S(1)} async-done(((f32[16,208,128]{2,1,0:T(8,128)}), f32[16,208,128]{2,1,0:T(8,128)S(1)}, u32[]{:S(2)}, u32[]{:S(2)}) %all-to-all-start) | async-done | bytes 1703968 | tf_op jit(solution)/shard_map/all_to_all | solution.py:520
  50.4 0.0 copy-done.4
  50.4 0.0 copy-done.5
  50.4 0.0 copy-done.6
  50.5 0.0 copy-done.7
  50.5 0.0 copy-done.8
  50.5 0.0 copy-done.9
  50.5 0.0 copy-done.10
  50.5 1.2 %copy-done = f32[16,208,128]{2,1,0:T(8,128)} copy-done((f32[16,208,128]{2,1,0:T(8,128)}, f32[16,208,128]{2,1,0:T(8,128)S(1)}, u32[]{:S(2)}) %copy-start) | copy-done | bytes 1703960
  51.6 7.1 %two.1 = (f32[544,128]{1,0:T(8,128)}, f32[192,128]{1,0:T(8,128)}, f32[192,128]{1,0:T(8,128)}, f32[192,128]{1,0:T(8,128)}, f32[192,128]{1,0:T(8,128)}, /*index=5*...) custom-call(f32[168,128]{1,0:T(8,128)} %get-tuple-element.52.refs_0_, ...), custom_call_target="tpu_custom_call" | custom-call | flops 1000 | bytes 1000 | tf_op jit(solution)/shard_map/two/pallas_call | solution.py:495
  58.7 3.6 %all-to-all-start.1 = ((f32[16,64,128]{2,1,0:T(8,128)}), f32[16,64,128]{2,1,0:T(8,128)S(1)}, u32[]{:S(2)}, u32[]{:S(2)}) async-start(f32[16,64,128]{2,1,0:T(8,128)} %bitcast.13), calls=%async_computation.1 | async-start | bytes 1048576 | tf_op jit(solution)/shard_map/all_to_all | solution.py:520
  62.3 0.0 collective-permute-start.17
  62.3 1.8 %collective-permute-start.16 = (f32[48,128]{1,0:T(8,128)}, f32[48,128]{1,0:T(8,128)S(1)}, u32[]{:S(2)}, u32[]{:S(2)}) collective-permute-start(f32[48,128]{1,0:T(8,128)} %get-tuple-element.67.refs_0_), channel_id=1, source_target_pairs={{0,6},{1,7},{2,0},{3,1},{4,2},{5,3},{6,4},{7,5},{8,14},{9,15},{10,... | collective-permute-start | bytes 73736 | tf_op jit(solution)/shard_map/ppermute | solution.py:515
  64.2 1.9 %collective-permute-start.15 = (f32[48,128]{1,0:T(8,128)}, f32[48,128]{1,0:T(8,128)S(1)}, u32[]{:S(2)}, u32[]{:S(2)}) collective-permute-start(f32[48,128]{1,0:T(8,128)} %get-tuple-element.67.refs_0_), channel_id=1, source_target_pairs={{0,5},{1,6},{2,7},{3,0},{4,1},{5,2},{6,3},{7,4},{8,13},{9,14},{10,... | collective-permute-start | bytes 73736 | tf_op jit(solution)/shard_map/ppermute | solution.py:515
  66.1 1.4 %collective-permute-start.14 = (f32[48,128]{1,0:T(8,128)}, f32[48,128]{1,0:T(8,128)S(1)}, u32[]{:S(2)}, u32[]{:S(2)}) collective-permute-start(f32[48,128]{1,0:T(8,128)} %get-tuple-element.67.refs_0_), channel_id=1, source_target_pairs={{0,4},{1,5},{2,6},{3,7},{4,0},{5,1},{6,2},{7,3},{8,12},{9,13},{10,... | collective-permute-start | bytes 73736 | tf_op jit(solution)/shard_map/ppermute | solution.py:515
  67.5 0.0 collective-permute-start.13
  67.5 0.0 collective-permute-done.17.refs_7_
  67.5 1.4 %collective-permute-start.12 = (f32[48,128]{1,0:T(8,128)}, f32[48,128]{1,0:T(8,128)S(1)}, u32[]{:S(2)}, u32[]{:S(2)}) collective-permute-start(f32[48,128]{1,0:T(8,128)} %get-tuple-element.67.refs_0_), channel_id=1, source_target_pairs={{0,2},{1,3},{2,4},{3,5},{4,6},{5,7},{6,0},{7,1},{8,10},{9,11},{10,... | collective-permute-start | bytes 73736 | tf_op jit(solution)/shard_map/ppermute | solution.py:515
  68.9 0.0 collective-permute-done.16.refs_6_
  68.9 1.1 %collective-permute-start.11 = (f32[48,128]{1,0:T(8,128)}, f32[48,128]{1,0:T(8,128)S(1)}, u32[]{:S(2)}, u32[]{:S(2)}) collective-permute-start(f32[48,128]{1,0:T(8,128)} %get-tuple-element.67.refs_0_), channel_id=1, source_target_pairs={{0,1},{1,2},{2,3},{3,4},{4,5},{5,6},{6,7},{7,0},{8,9},{9,10},{10,1... | collective-permute-start | bytes 73736 | tf_op jit(solution)/shard_map/ppermute | solution.py:515
  70.0 0.0 collective-permute-done.15.refs_5_
  70.0 1.6 %collective-permute-done.14.refs_4_ = f32[48,128]{1,0:T(8,128)S(1)} collective-permute-done((f32[48,128]{1,0:T(8,128)}, f32[48,128]{1,0:T(8,128)S(1)}, u32[]{:S(2)}, u32[]{:S(2)}) %collective-permute-start.14) | collective-permute-done | bytes 24608 | tf_op jit(solution)/shard_map/ppermute | solution.py:515
  71.6 0.8 %collective-permute-done.13.refs_3_ = f32[48,128]{1,0:T(8,128)S(1)} collective-permute-done((f32[48,128]{1,0:T(8,128)}, f32[48,128]{1,0:T(8,128)S(1)}, u32[]{:S(2)}, u32[]{:S(2)}) %collective-permute-start.13) | collective-permute-done | bytes 24608 | tf_op jit(solution)/shard_map/ppermute | solution.py:515
  72.4 0.4 collective-permute-done.12.refs_2_
  72.8 1.5 %collective-permute-done.11.refs_1_ = f32[48,128]{1,0:T(8,128)S(1)} collective-permute-done((f32[48,128]{1,0:T(8,128)}, f32[48,128]{1,0:T(8,128)S(1)}, u32[]{:S(2)}, u32[]{:S(2)}) %collective-permute-start.11) | collective-permute-done | bytes 24608 | tf_op jit(solution)/shard_map/ppermute | solution.py:515
  74.2 0.0 all-to-all-done.1
  74.3 0.0 copy-done.14
  74.3 0.0 copy-done.15
  74.3 0.0 copy-done.16
  74.3 0.5 copy-done.20
  74.8 0.2 copy-done.1
  75.0 5.0 %three.1 = f32[3072,128]{1,0:T(8,128)} custom-call(f32[48,128]{1,0:T(8,128)} %get-tuple-element.67.refs_0_, f32[48,128]{1,0:T(8,128)} %copy-done.20, f32[48,128]{1,0:T(8,128)} %copy-done.19, f32[48,128]{1,0:T(8,128)} %copy-done.18, f32[48,128]{1,0:T(8,128)} %copy-done.17, f32[48,128]{1,0:T(8,128)} %copy-done.16, f32[48,128]{1,0:T(8,128)} %copy-done.15, ...), custom_call_target="tpu_custom_call" | custom-call | flops 1000 | bytes 1000 | tf_op jit(solution)/shard_map/three/pallas_call | solution.py:495
  (22 shorter events, 0.0 us)
Async XLA Ops:
  3.1 10.7 %collective-permute-start = (f32[160,128]{1,0:T(8,128)}, f32[160,128]{1,0:T(8,128)S(1)}, u32[]{:S(2)}, u32[]{:S(2)}) collective-permute-start(f32[160,128]{1,0:T(8,128)} %get-tuple-element.48), channel_id=1, source_target_pairs={{0,8},{8,16},{16,24},{24,32},{32,40},{40,48},{48,56},{56,64},{64,7... | collective-permute-start | bytes 245768 | tf_op jit(solution)/shard_map/ppermute | solution.py:515
  4.9 9.0 %collective-permute-start.1 = (f32[160,128]{1,0:T(8,128)}, f32[160,128]{1,0:T(8,128)S(1)}, u32[]{:S(2)}, u32[]{:S(2)}) collective-permute-start(f32[160,128]{1,0:T(8,128)} %get-tuple-element.49), channel_id=1, source_target_pairs={{0,120},{8,0},{16,8},{24,16},{32,24},{40,32},{48,40},{56,48},{64,5... | collective-permute-start | bytes 245768 | tf_op jit(solution)/shard_map/ppermute | solution.py:515
  8.6 5.2 %collective-permute-start.2 = (f32[96,128]{1,0:T(8,128)}, f32[96,128]{1,0:T(8,128)S(1)}, u32[]{:S(2)}, u32[]{:S(2)}) collective-permute-start(f32[96,128]{1,0:T(8,128)} %get-tuple-element.50), channel_id=1, source_target_pairs={{0,1},{1,2},{2,3},{3,4},{4,5},{5,6},{6,7},{7,0},{8,9},{9,10},{10,1... | collective-permute-start | bytes 147464 | tf_op jit(solution)/shard_map/ppermute | solution.py:515
  8.6 5.3 %collective-permute-start.3 = (f32[96,128]{1,0:T(8,128)}, f32[96,128]{1,0:T(8,128)S(1)}, u32[]{:S(2)}, u32[]{:S(2)}) collective-permute-start(f32[96,128]{1,0:T(8,128)} %get-tuple-element.51), channel_id=1, source_target_pairs={{0,7},{1,0},{2,1},{3,2},{4,3},{5,4},{6,5},{7,6},{8,15},{9,8},{10,9... | collective-permute-start | bytes 147464 | tf_op jit(solution)/shard_map/ppermute | solution.py:515
  13.7 0.6 copy-start.12
  13.8 0.6 copy-start.13
  13.8 0.6 copy-start.11
  13.8 0.7 copy-start.2
  19.4 4.2 %copy-start.3 = (f32[168,128]{1,0:T(8,128)S(1)}, f32[168,128]{1,0:T(8,128)}, u32[]{:S(2)}) copy-start(f32[168,128]{1,0:T(8,128)} %get-tuple-element.52.refs_0_) | copy-start | bytes 258052
  19.4 31.1 %all-to-all-start = ((f32[16,208,128]{2,1,0:T(8,128)}), f32[16,208,128]{2,1,0:T(8,128)S(1)}, u32[]{:S(2)}, u32[]{:S(2)}) async-start(f32[16,208,128]{2,1,0:T(8,128)} %bitcast.12), calls=%async_computation | async-start | bytes 3407872 | tf_op jit(solution)/shard_map/all_to_all | solution.py:520
  23.6 7.5 %collective-permute-start.10 = (f32[168,128]{1,0:T(8,128)S(1)}, f32[168,128]{1,0:T(8,128)S(1)}, u32[]{:S(2)}, u32[]{:S(2)}) collective-permute-start(f32[168,128]{1,0:T(8,128)S(1)} %copy-done.3), channel_id=1, source_target_pairs={{0,7},{1,0},{2,1},{3,2},{4,3},{5,4},{6,5},{7,6},{8,15},{9,8},{10,9... | collective-permute-start | bytes 258056 | tf_op jit(solution)/shard_map/ppermute | solution.py:515
  26.1 5.2 %collective-permute-start.9 = (f32[168,128]{1,0:T(8,128)S(1)}, f32[168,128]{1,0:T(8,128)S(1)}, u32[]{:S(2)}, u32[]{:S(2)}) collective-permute-start(f32[168,128]{1,0:T(8,128)S(1)} %copy-done.3), channel_id=1, source_target_pairs={{0,6},{1,7},{2,0},{3,1},{4,2},{5,3},{6,4},{7,5},{8,14},{9,15},{10,... | collective-permute-start | bytes 258056 | tf_op jit(solution)/shard_map/ppermute | solution.py:515
  27.8 4.8 %collective-permute-start.8 = (f32[168,128]{1,0:T(8,128)S(1)}, f32[168,128]{1,0:T(8,128)S(1)}, u32[]{:S(2)}, u32[]{:S(2)}) collective-permute-start(f32[168,128]{1,0:T(8,128)S(1)} %copy-done.3), channel_id=1, source_target_pairs={{0,5},{1,6},{2,7},{3,0},{4,1},{5,2},{6,3},{7,4},{8,13},{9,14},{10,... | collective-permute-start | bytes 258056 | tf_op jit(solution)/shard_map/ppermute | solution.py:515
  27.8 7.5 %collective-permute-start.7 = (f32[168,128]{1,0:T(8,128)S(1)}, f32[168,128]{1,0:T(8,128)S(1)}, u32[]{:S(2)}, u32[]{:S(2)}) collective-permute-start(f32[168,128]{1,0:T(8,128)S(1)} %copy-done.3), channel_id=1, source_target_pairs={{0,4},{1,5},{2,6},{3,7},{4,0},{5,1},{6,2},{7,3},{8,12},{9,13},{10,... | collective-permute-start | bytes 258056 | tf_op jit(solution)/shard_map/ppermute | solution.py:515
  31.1 6.4 %collective-permute-start.6 = (f32[168,128]{1,0:T(8,128)S(1)}, f32[168,128]{1,0:T(8,128)S(1)}, u32[]{:S(2)}, u32[]{:S(2)}) collective-permute-start(f32[168,128]{1,0:T(8,128)S(1)} %copy-done.3), channel_id=1, source_target_pairs={{0,3},{1,4},{2,5},{3,6},{4,7},{5,0},{6,1},{7,2},{8,11},{9,12},{10,... | collective-permute-start | bytes 258056 | tf_op jit(solution)/shard_map/ppermute | solution.py:515
  31.1 19.4 %copy-start.4 = (f32[168,128]{1,0:T(8,128)}, f32[168,128]{1,0:T(8,128)S(1)}, u32[]{:S(2)}) copy-start(f32[168,128]{1,0:T(8,128)S(1)} %collective-permute-done.10.refs_7_) | copy-start | bytes 258052
  31.1 8.6 %collective-permute-start.5 = (f32[168,128]{1,0:T(8,128)S(1)}, f32[168,128]{1,0:T(8,128)S(1)}, u32[]{:S(2)}, u32[]{:S(2)}) collective-permute-start(f32[168,128]{1,0:T(8,128)S(1)} %copy-done.3), channel_id=1, source_target_pairs={{0,2},{1,3},{2,4},{3,5},{4,6},{5,7},{6,0},{7,1},{8,10},{9,11},{10,... | collective-permute-start | bytes 258056 | tf_op jit(solution)/shard_map/ppermute | solution.py:515
  31.3 19.1 %copy-start.5 = (f32[168,128]{1,0:T(8,128)}, f32[168,128]{1,0:T(8,128)S(1)}, u32[]{:S(2)}) copy-start(f32[168,128]{1,0:T(8,128)S(1)} %collective-permute-done.9.refs_6_) | copy-start | bytes 258052
  31.3 8.5 %collective-permute-start.4 = (f32[168,128]{1,0:T(8,128)S(1)}, f32[168,128]{1,0:T(8,128)S(1)}, u32[]{:S(2)}, u32[]{:S(2)}) collective-permute-start(f32[168,128]{1,0:T(8,128)S(1)} %copy-done.3), channel_id=1, source_target_pairs={{0,1},{1,2},{2,3},{3,4},{4,5},{5,6},{6,7},{7,0},{8,9},{9,10},{10,1... | collective-permute-start | bytes 258056 | tf_op jit(solution)/shard_map/ppermute | solution.py:515
  32.6 17.8 %copy-start.6 = (f32[168,128]{1,0:T(8,128)}, f32[168,128]{1,0:T(8,128)S(1)}, u32[]{:S(2)}) copy-start(f32[168,128]{1,0:T(8,128)S(1)} %collective-permute-done.8.refs_5_) | copy-start | bytes 258052
  35.2 15.2 %copy-start.7 = (f32[168,128]{1,0:T(8,128)}, f32[168,128]{1,0:T(8,128)S(1)}, u32[]{:S(2)}) copy-start(f32[168,128]{1,0:T(8,128)S(1)} %collective-permute-done.7.refs_4_) | copy-start | bytes 258052
  37.5 13.0 %copy-start.8 = (f32[168,128]{1,0:T(8,128)}, f32[168,128]{1,0:T(8,128)S(1)}, u32[]{:S(2)}) copy-start(f32[168,128]{1,0:T(8,128)S(1)} %collective-permute-done.6.refs_3_) | copy-start | bytes 258052
  39.7 10.8 %copy-start.9 = (f32[168,128]{1,0:T(8,128)}, f32[168,128]{1,0:T(8,128)S(1)}, u32[]{:S(2)}) copy-start(f32[168,128]{1,0:T(8,128)S(1)} %collective-permute-done.5.refs_2_) | copy-start | bytes 258052
  39.8 10.7 %copy-start.10 = (f32[168,128]{1,0:T(8,128)}, f32[168,128]{1,0:T(8,128)S(1)}, u32[]{:S(2)}) copy-start(f32[168,128]{1,0:T(8,128)S(1)} %collective-permute-done.4.refs_1_) | copy-start | bytes 258052
  50.4 1.2 %copy-start = (f32[16,208,128]{2,1,0:T(8,128)}, f32[16,208,128]{2,1,0:T(8,128)S(1)}, u32[]{:S(2)}) copy-start(f32[16,208,128]{2,1,0:T(8,128)S(1)} %all-to-all-done) | copy-start | bytes 5111812
  58.7 15.5 %all-to-all-start.1 = ((f32[16,64,128]{2,1,0:T(8,128)}), f32[16,64,128]{2,1,0:T(8,128)S(1)}, u32[]{:S(2)}, u32[]{:S(2)}) async-start(f32[16,64,128]{2,1,0:T(8,128)} %bitcast.13), calls=%async_computation.1 | async-start | bytes 1048576 | tf_op jit(solution)/shard_map/all_to_all | solution.py:520
  62.3 5.1 %collective-permute-start.17 = (f32[48,128]{1,0:T(8,128)}, f32[48,128]{1,0:T(8,128)S(1)}, u32[]{:S(2)}, u32[]{:S(2)}) collective-permute-start(f32[48,128]{1,0:T(8,128)} %get-tuple-element.67.refs_0_), channel_id=1, source_target_pairs={{0,7},{1,0},{2,1},{3,2},{4,3},{5,4},{6,5},{7,6},{8,15},{9,8},{10,9... | collective-permute-start | bytes 73736 | tf_op jit(solution)/shard_map/ppermute | solution.py:515
  62.3 6.5 %collective-permute-start.16 = (f32[48,128]{1,0:T(8,128)}, f32[48,128]{1,0:T(8,128)S(1)}, u32[]{:S(2)}, u32[]{:S(2)}) collective-permute-start(f32[48,128]{1,0:T(8,128)} %get-tuple-element.67.refs_0_), channel_id=1, source_target_pairs={{0,6},{1,7},{2,0},{3,1},{4,2},{5,3},{6,4},{7,5},{8,14},{9,15},{10,... | collective-permute-start | bytes 73736 | tf_op jit(solution)/shard_map/ppermute | solution.py:515
  64.2 5.8 %collective-permute-start.15 = (f32[48,128]{1,0:T(8,128)}, f32[48,128]{1,0:T(8,128)S(1)}, u32[]{:S(2)}, u32[]{:S(2)}) collective-permute-start(f32[48,128]{1,0:T(8,128)} %get-tuple-element.67.refs_0_), channel_id=1, source_target_pairs={{0,5},{1,6},{2,7},{3,0},{4,1},{5,2},{6,3},{7,4},{8,13},{9,14},{10,... | collective-permute-start | bytes 73736 | tf_op jit(solution)/shard_map/ppermute | solution.py:515
  66.1 5.5 %collective-permute-start.14 = (f32[48,128]{1,0:T(8,128)}, f32[48,128]{1,0:T(8,128)S(1)}, u32[]{:S(2)}, u32[]{:S(2)}) collective-permute-start(f32[48,128]{1,0:T(8,128)} %get-tuple-element.67.refs_0_), channel_id=1, source_target_pairs={{0,4},{1,5},{2,6},{3,7},{4,0},{5,1},{6,2},{7,3},{8,12},{9,13},{10,... | collective-permute-start | bytes 73736 | tf_op jit(solution)/shard_map/ppermute | solution.py:515
  67.5 5.0 %collective-permute-start.13 = (f32[48,128]{1,0:T(8,128)}, f32[48,128]{1,0:T(8,128)S(1)}, u32[]{:S(2)}, u32[]{:S(2)}) collective-permute-start(f32[48,128]{1,0:T(8,128)} %get-tuple-element.67.refs_0_), channel_id=1, source_target_pairs={{0,3},{1,4},{2,5},{3,6},{4,7},{5,0},{6,1},{7,2},{8,11},{9,12},{10,... | collective-permute-start | bytes 73736 | tf_op jit(solution)/shard_map/ppermute | solution.py:515
  67.5 6.8 %copy-start.14 = (f32[48,128]{1,0:T(8,128)}, f32[48,128]{1,0:T(8,128)S(1)}, u32[]{:S(2)}) copy-start(f32[48,128]{1,0:T(8,128)S(1)} %collective-permute-done.17.refs_7_) | copy-start | bytes 73732
  67.5 5.3 %collective-permute-start.12 = (f32[48,128]{1,0:T(8,128)}, f32[48,128]{1,0:T(8,128)S(1)}, u32[]{:S(2)}, u32[]{:S(2)}) collective-permute-start(f32[48,128]{1,0:T(8,128)} %get-tuple-element.67.refs_0_), channel_id=1, source_target_pairs={{0,2},{1,3},{2,4},{3,5},{4,6},{5,7},{6,0},{7,1},{8,10},{9,11},{10,... | collective-permute-start | bytes 73736 | tf_op jit(solution)/shard_map/ppermute | solution.py:515
  68.9 5.4 %copy-start.15 = (f32[48,128]{1,0:T(8,128)}, f32[48,128]{1,0:T(8,128)S(1)}, u32[]{:S(2)}) copy-start(f32[48,128]{1,0:T(8,128)S(1)} %collective-permute-done.16.refs_6_) | copy-start | bytes 73732
  68.9 5.4 %collective-permute-start.11 = (f32[48,128]{1,0:T(8,128)}, f32[48,128]{1,0:T(8,128)S(1)}, u32[]{:S(2)}, u32[]{:S(2)}) collective-permute-start(f32[48,128]{1,0:T(8,128)} %get-tuple-element.67.refs_0_), channel_id=1, source_target_pairs={{0,1},{1,2},{2,3},{3,4},{4,5},{5,6},{6,7},{7,0},{8,9},{9,10},{10,1... | collective-permute-start | bytes 73736 | tf_op jit(solution)/shard_map/ppermute | solution.py:515
  70.0 4.3 %copy-start.16 = (f32[48,128]{1,0:T(8,128)}, f32[48,128]{1,0:T(8,128)S(1)}, u32[]{:S(2)}) copy-start(f32[48,128]{1,0:T(8,128)S(1)} %collective-permute-done.15.refs_5_) | copy-start | bytes 73732
  71.6 2.7 %copy-start.17 = (f32[48,128]{1,0:T(8,128)}, f32[48,128]{1,0:T(8,128)S(1)}, u32[]{:S(2)}) copy-start(f32[48,128]{1,0:T(8,128)S(1)} %collective-permute-done.14.refs_4_) | copy-start | bytes 73732
  72.4 1.9 %copy-start.18 = (f32[48,128]{1,0:T(8,128)}, f32[48,128]{1,0:T(8,128)S(1)}, u32[]{:S(2)}) copy-start(f32[48,128]{1,0:T(8,128)S(1)} %collective-permute-done.13.refs_3_) | copy-start | bytes 73732
  72.8 1.5 %copy-start.19 = (f32[48,128]{1,0:T(8,128)}, f32[48,128]{1,0:T(8,128)S(1)}, u32[]{:S(2)}) copy-start(f32[48,128]{1,0:T(8,128)S(1)} %collective-permute-done.12.refs_2_) | copy-start | bytes 73732
  74.2 0.6 copy-start.20
  74.3 0.8 copy-start.1

commit v2 on v1

--- a/solution.py
+++ b/solution.py
@@ -5,17 +5,31 @@
 from jax import lax
 from jax.experimental import pallas as pl
 from jax.experimental.pallas import tpu as pltpu
+from jax.sharding import Mesh
 from jax.sharding import PartitionSpec as P
 
 PX, PY, PZ = 16, 32, 128
 XR = 40
 YR = 24
 F32 = jnp.float32
+LIMIT = 30
 EX, EY, EZ, HX, HY, HZ = range(6)
 
 
-def lane():
-    return lax.broadcasted_iota(jnp.int32, (PY, PZ), 1)
+def x_index():
+    return lax.axis_index("ga") * lax.axis_size("gb") + lax.axis_index("gb")
+
+
+def y_index():
+    return lax.axis_index("gz") * lax.axis_size("gc") + lax.axis_index("gc")
+
+
+def y_size():
+    return lax.axis_size("gz") * lax.axis_size("gc")
+
+
+def x_size():
+    return lax.axis_size("ga") * lax.axis_size("gb")
 
 
 def sub():
@@ -70,26 +84,60 @@
     return level[0]
 
 
-def k_edges(f, reg, table, eps, xup, xdn, yup, ydn):
+def k_eps(reg, table, eps):
     tab = [table[i] for i in range(16)]
     for x in range(PX):
         put(eps, x, lookup(plane(reg, x), tab))
-    for i, c in enumerate((EX, EY, HY, HZ)):
-        put(xup, i, fplane(f, c, PX - 1))
-    put(xup, 4, plane(eps, PX - 1))
-    for i, c in enumerate((EY, EZ, HX, HZ)):
-        put(xdn, i, fplane(f, c, 0))
-    put(xdn, 4, plane(eps, 0))
-
-    def row(ref, base, y):
-        return ref[pl.ds(base * PX * PY + y, PX, stride=PY), :]
-
-    for i, (c, y) in enumerate(((EX, 31), (HY, 31), (EZ, 31), (HX, 31), (HX, 30))):
-        put(yup, i, row(f, c, y), PX)
-    put(yup, 5, row(eps, 0, PY - 1), PX)
-    for i, c in enumerate((EX, HY, EZ, HX)):
-        put(ydn, i, row(f, c, 0), PX)
-    put(ydn, 4, row(eps, 0, 0), PX)
+
+
+def k_edges(f, reg, table, xup, xdn, yup, ydn, tab, ends, low, high, rlow, rhigh, sems):
+    up, down = (EX, EY, HY, HZ), (EY, EZ, HX, HZ)
+    rows = (EX, HY, EZ, HX)
+    top = pl.ds(PY - 8, 8)
+    pairs = [(table, tab), (reg.at[PX - 1], ends.at[0]), (reg.at[0], ends.at[1])]
+    pairs += [(reg.at[:, top, :], rhigh), (reg.at[:, pl.ds(0, 8), :], rlow)]
+    for i in range(4):
+        pairs += [
+            (f.at[up[i], PX - 1], xup.at[pl.ds(i * PY, PY), :]),
+            (f.at[down[i], 0], xdn.at[pl.ds(i * PY, PY), :]),
+            (f.at[rows[i], :, top, :], high.at[i]),
+            (f.at[rows[i], :, pl.ds(0, 8), :], low.at[i]),
+        ]
+    copies = [pltpu.make_async_copy(p, q, sems.at[i]) for i, (p, q) in enumerate(pairs)]
+    for copy in copies:
+        copy.start()
+    for copy in copies:
+        copy.wait()
+    t = [tab[i] for i in range(16)]
+    put(xup, 4, lookup(ends[0], t))
+    put(xdn, 4, lookup(ends[1], t))
+    for i in range(4):
+        put(yup, i, high[i, :, 7, :], PX)
+        put(ydn, i, low[i, :, 0, :], PX)
+    put(yup, 4, high[3, :, 6, :], PX)
+    put(yup, 5, lookup(rhigh[:, 7, :], t), PX)
+    put(ydn, 4, lookup(rlow[:, 0, :], t), PX)
+
+
+def edges(fields, region, eps_table):
+    vmem, hbm = [pl.BlockSpec(memory_space=m) for m in (pltpu.VMEM, pltpu.HBM)]
+    return pl.pallas_call(
+        k_edges,
+        out_shape=[pltpu.VMEM((c, PZ), F32) for c in (5 * PY, 5 * PY, 6 * PX, 6 * PX)],
+        in_specs=[hbm] * 3,
+        out_specs=[vmem] * 4,
+        scratch_shapes=[
+            pltpu.SMEM((16,), F32),
+            pltpu.VMEM((2, PY, PZ), jnp.int32),
+            pltpu.VMEM((4, PX, 8, PZ), F32),
+            pltpu.VMEM((4, PX, 8, PZ), F32),
+            pltpu.VMEM((PX, 8, PZ), jnp.int32),
+            pltpu.VMEM((PX, 8, PZ), jnp.int32),
+            pltpu.SemaphoreType.DMA((21,)),
+        ],
+        cost_estimate=pl.CostEstimate(flops=1000, bytes_accessed=1000, transcendentals=0),
+        name="edges",
+    )(*[pltpu.with_memory_space_constraint(v, pltpu.HBM) for v in (fields, region, eps_table)])
 
 
 def factor(m_at, count, first, h, b, rows):
@@ -136,12 +184,11 @@
 
 
 def k_x1(f, eps, xl, xr, yl, yr, msg, q1, m, h, b, v, hb, r):
-    gx = lax.axis_index("gx")
-    gy = lax.axis_index("gy")
-    n = lax.axis_size("gx")
+    gx = x_index()
+    gy = y_index()
     xlo = gx > 0
     ylo = gy > 0
-    yhi = gy < lax.axis_size("gy") - 1
+    yhi = gy < y_size() - 1
     yin = jnp.where(ylo, 1.0, 0.0)
     yon = jnp.where(yhi, 1.0, 0.0)
     q1lo = yin * (plane(yl, 1, PX) - 0.5 * fz(plane(yl, 0, PX)))
@@ -181,16 +228,16 @@
     put(hb, 3, vn, XR)
     zq = jnp.zeros((6, PZ), F32)
     qq = jnp.concatenate([q1lo[PX - 1 :], q1hi[PX - 1 :], zq], 0) * (-1.0 / 32.0)
-    spread(msg, n, (pf, plast, a, bb, c, qq))
+    spread(msg, lax.axis_size("gb"), (pf, plast, a, bb, c, qq))
 
 
 def k_y1(f, eps, xl, xr, msg, p1, ey1, m, h, b, v, hb, r, ep):
-    gx = lax.axis_index("gx")
-    gy = lax.axis_index("gy")
-    n = lax.axis_size("gy")
+    gx = x_index()
+    gy = y_index()
+    n = y_size()
     xlo = gx > 0
     xin = jnp.where(xlo, 1.0, 0.0)
-    xon = jnp.where(gx < lax.axis_size("gx") - 1, 1.0, 0.0)
+    xon = jnp.where(gx < x_size() - 1, 1.0, 0.0)
     zero = jnp.zeros((1, PZ), F32)
     zeros = jnp.zeros((PY, PZ), F32)
     exl, eyl, hyl, hzl = [xin * plane(xl, i) for i in range(4)]
@@ -271,20 +318,27 @@
         put(dele, j, delta, rows)
 
 
-def interface(part, n, me, rows, tp, bp, ts, bs, bet, dele, al, ga, crows=None):
-    crows = crows or rows
-    zero = jnp.zeros((rows, PZ), F32)
+def chain(part, n, rows, crows, tp, bp, ts, bs, al, ga, start, stop):
     take = lambda ref, j: ref[pl.ds(j * crows, rows), :]
-    alpha = zero
-    put(al, 0, zero, rows)
-    gamma = zero
-    put(ga, n, zero, rows)
+    alpha, gamma = start, stop
+    put(al, 0, alpha, rows)
+    put(ga, n, gamma, rows)
     for j in range(n):
         k = n - 1 - j
         alpha = part(j, 1) + take(tp, j) * part(j, 0) + take(bp, j) * alpha
         gamma = part(k, 0) + take(ts, k) * part(k, 1) + take(bs, k) * gamma
         put(al, j + 1, alpha, rows)
         put(ga, k, gamma, rows)
+    return gamma, alpha
+
+
+def interface(part, n, me, rows, coefs, al, ga, start=None, stop=None, crows=None):
+    crows = crows or rows
+    tp, bp, ts, bs, bet, dele = coefs
+    zero = jnp.zeros((rows, PZ), F32)
+    start = zero if start is None else start
+    stop = zero if stop is None else stop
+    chain(part, n, rows, crows, tp, bp, ts, bs, al, ga, start, stop)
     at = lambda ref, d, size: ref[pl.ds(pl.multiple_of(d * size, 8), rows), :]
     a0, a1 = at(al, me, rows), at(al, me + 1, rows)
     g0, g1 = at(ga, me, rows), at(ga, me + 1, rows)
@@ -295,25 +349,61 @@
     return left, right
 
 
-def k_y2(msg, p1, h, b, v, hb, ex1, p2, elo, tp, bp, ts, bs, bet, dele, al, ga, dex):
-    n = lax.axis_size("gy")
-    me = lax.axis_index("gy")
-    block = 7 * YR
-    raw = lambda j, k: msg[pl.ds(j * block + k * YR, YR), :]
-    coefficients(raw, n, YR, tp, bp, ts, bs, bet, dele)
-
+XB = 5 * XR + 8
+
+
+def x_raw(msg):
+    return lambda j, k: msg[pl.ds(j * XB + k * XR, XR), :]
+
+
+def x_part(msg):
     def part(j, k):
-        own = raw(j, k)
         if j == 0:
-            return own
-        return own + raw(j, 2 + k) * raw(j - 1, 5)
-
-    left, right = interface(part, n, me, YR, tp, bp, ts, bs, bet, dele, al, ga)
-    prev = pl.multiple_of(jnp.maximum(me - 1, 0) * block, 8)
-    live = jnp.where(me > 0, 1.0, 0.0)
-    q = live * msg[pl.ds(prev + 5 * YR, YR), :]
-    elo[...] = live * msg[pl.ds(prev + 6 * YR, YR), :]
-    lw = (left + q) * plane(hb, 1, YR)
+            return x_raw(msg)(j, k)
+        own = msg[pl.ds(j * XB + k * XR, PY), :]
+        more = (
+            msg[pl.ds(j * XB + k * XR + PY, 8), :]
+            + msg[pl.ds(j * XB + (2 + k) * XR + PY, 8), :] * msg[pl.ds((j - 1) * XB + 5 * XR, 8), :]
+        )
+        return jnp.concatenate([own, more], 0)
+
+    return part
+
+
+def x_passed(msg, me):
+    prev = pl.multiple_of(jnp.maximum(me - 1, 0) * XB, 8)
+    return jnp.where(me > 0, msg[pl.ds(prev + 5 * XR, 8), :], 0.0)
+
+
+YB = 7 * YR
+
+
+def y_raw(msg):
+    return lambda j, k: msg[pl.ds(j * YB + k * YR, YR), :]
+
+
+def y_part(msg):
+    raw = y_raw(msg)
+    return lambda j, k: raw(j, k) + raw(j, 2 + k) * raw(j - 1, 5) if j else raw(j, k)
+
+
+def y_passed(msg, me, k):
+    prev = pl.multiple_of(jnp.maximum(me - 1, 0) * YB, 8)
+    return jnp.where(me > 0, msg[pl.ds(prev + k * YR, YR), :], 0.0)
+
+
+def k_y2(gi, go, p1, h, b, v, hb, ex1, p2, elo, *more):
+    coi, coo, (al, ga, dex) = more[:6], more[6:12], more[12:]
+    nz, nc = lax.axis_size("gz"), lax.axis_size("gc")
+    iz, ic = lax.axis_index("gz"), lax.axis_index("gc")
+    coefficients(y_raw(go), nz, YR, *coo)
+    coefficients(y_raw(gi), nc, YR, *coi)
+    left, right = interface(y_part(go), nz, iz, YR, coo, al, ga)
+    left = left + y_passed(go, iz, 5)
+    left, right = interface(y_part(gi), nc, ic, YR, coi, al, ga, left, right)
+    left = left + y_passed(gi, ic, 5)
+    elo[...] = jnp.where(ic > 0, y_passed(gi, ic, 6), y_passed(go, iz, 6))
+    lw = left * plane(hb, 1, YR)
     rw = (right - plane(hb, 3, YR)) * plane(hb, 0, YR)
     later = right
     for j in range(PY - 1, -1, -1):
@@ -321,35 +411,75 @@
         ex1[pl.ds(j, YR, stride=PY), :] = w
         dex[pl.ds(j, YR, stride=PY), :] = later - w
         later = w
-    live = jnp.where(lax.axis_index("gx") > 0, 1.0, 0.0)
+    live = jnp.where(x_index() > 0, 1.0, 0.0)
     for x in range(PX):
         put(p2, x, plane(p1, x) + 64.0 * plane(dex, x))
     put(p2, PX, live * (plane(p1, PX) + 64.0 * plane(dex, PX)))
 
 
-def k_x2(msg, f, eps, q1, ey1, p2, h, b, v, m, hb, ez1, hx1, msg2, v2, vn2, tp, bp, ts, bs, bet, dele, al, ga, r):
-    n = lax.axis_size("gx")
-    me = lax.axis_index("gx")
-    gy = lax.axis_index("gy")
-    yon = jnp.where(gy < lax.axis_size("gy") - 1, 1.0, 0.0)
-    block = 5 * XR + 8
-    raw = lambda j, k: msg[pl.ds(j * block + k * XR, XR), :]
-    coefficients(raw, n, XR, tp, bp, ts, bs, bet, dele)
-
-    def part(j, k):
-        if j == 0:
-            return raw(j, k)
-        own = msg[pl.ds(j * block + k * XR, PY), :]
-        more = (
-            msg[pl.ds(j * block + k * XR + PY, 8), :]
-            + msg[pl.ds(j * block + (2 + k) * XR + PY, 8), :] * msg[pl.ds((j - 1) * block + 5 * XR, 8), :]
-        )
-        return jnp.concatenate([own, more], 0)
-
-    left, right = interface(part, n, me, XR, tp, bp, ts, bs, bet, dele, al, ga)
-    prev = pl.multiple_of(jnp.maximum(me - 1, 0) * block, 8)
-    q = jnp.where(me > 0, 1.0, 0.0) * msg[pl.ds(prev + 5 * XR, 8), :]
-    left = jnp.concatenate([left[:PY], left[PY:] + q], 0)
+def join(part, raw, count):
+    pf, ph, a, b, c = part(0, 0), part(0, 1), raw(0, 2), raw(0, 3), raw(0, 4)
+    for j in range(1, count):
+        qf, qh, a2, b2, c2 = part(j, 0), part(j, 1), raw(j, 2), raw(j, 3), raw(j, 4)
+        den = 1.0 / (1.0 - c * a2)
+        low, high = b * den, b2 * den
+        pf, ph = pf + low * (qf + a2 * ph), qh + high * (ph + c * qf)
+        a, b, c = a + low * b * a2, low * b2, c2 + high * b2 * c
+    return pf, ph, a, b, c
+
+
+def k_join_y(gi, msg):
+    nc = lax.axis_size("gc")
+    raw = y_raw(gi)
+    spread(msg, 1, join(y_part(gi), raw, nc) + (raw(nc - 1, 5), raw(nc - 1, 6)))
+
+
+def k_join_x(gi, msg, inner):
+    inner[...] = gi[...]
+    nb = lax.axis_size("gb")
+    last = gi[pl.ds((nb - 1) * XB + 5 * XR, 8), :]
+    spread(msg, lax.axis_size("ga"), join(x_part(gi), x_raw(gi), nb) + (last,))
+
+
+def shares(pf, ph, coefs, count, me, rows, crows):
+    tp, bp, ts, bs = coefs[:4]
+    low = high = jnp.ones((rows, PZ), F32)
+    for k in range(count):
+        low = jnp.where(k < me, low * bs[pl.ds(k * crows, rows), :], low)
+        high = jnp.where(k > me, high * bp[pl.ds(k * crows, rows), :], high)
+    mine = pl.ds(pl.multiple_of(me * crows, 8), rows)
+    return low * (pf + ts[mine, :] * ph), high * (ph + tp[mine, :] * pf)
+
+
+def gathered(msg, n, m, ia, ib, rows, crows, coi, coo, al, ga):
+    zero = jnp.zeros((rows, PZ), F32)
+
+    def inside(j, k):
+        at = pl.multiple_of(((ia * m + j) * 2 + k) * rows, 8)
+        return msg[pl.ds(at, rows), :]
+
+    whole = chain(inside, m, rows, crows, *coi[:4], al, ga, zero, zero)
+
+    def group(j, k):
+        total = sum(msg[pl.ds(((j * m + i) * 2 + k) * rows, rows), :] for i in range(m))
+        return jnp.where(ia == j, whole[k], total)
+
+    left, right = interface(group, n, ia, rows, coo, al, ga, crows=crows)
+    return interface(inside, m, ib, rows, coi, al, ga, left, right, crows)
+
+
+def k_x2(gi, go, f, q1, ey1, p2, h, b, v, m, hb, ez1, hx1, msg2, v2, vn2, *more):
+    coi, coo, (al, ga, r) = more[:6], more[6:12], more[12:]
+    na, nb = lax.axis_size("ga"), lax.axis_size("gb")
+    ia, ib = lax.axis_index("ga"), lax.axis_index("gb")
+    gy = y_index()
+    yon = jnp.where(gy < y_size() - 1, 1.0, 0.0)
+    coefficients(x_raw(go), na, XR, *coo)
+    coefficients(x_raw(gi), nb, XR, *coi)
+    left, right = interface(x_part(go), na, ia, XR, coo, al, ga)
+    left = jnp.concatenate([left[:PY], left[PY:] + x_passed(go, ia)], 0)
+    left, right = interface(x_part(gi), nb, ib, XR, coi, al, ga, left, right)
+    left = jnp.concatenate([left[:PY], left[PY:] + x_passed(gi, ib)], 0)
     lw = left * plane(hb, 1, XR)
     rw = (right - plane(hb, 3, XR)) * plane(hb, 0, XR)
     for x in range(PX):
@@ -363,18 +493,21 @@
         t = fplane(f, HX, x) - 32.0 * (y_next(z, z32) - z) + 0.5 * fz(ey)
         put(hx1, x, t)
         p = plane(p2, x)
-        ie = 1.0 / plane(eps, x)
+        ie = 1.0 / (m[pl.ds(x * XR, PY), :] * 1024.0)
         put(r, x, ey + (0.5 * ie) * bz(t) - (32.0 * ie) * (p - before))
         before = p
     last, vn = sweep(lambda i: m[pl.ds(i * XR, PY), :], lambda i: plane(r, i), PX, v2, PY)
     vn2[...] = vn
     pf, plast = ends(last, vn, hb[pl.ds(0, PY), :], hb[pl.ds(2 * XR, PY), :])
-    spread(msg2, n, (pf, plast))
-
-
-def k_y3(f, xr, q1, eps, ey1, ez1, hx1, ex1, elo, m, hb, msg2, v2, vn2, ex2, hy1, q2, r):
-    n = lax.axis_size("gy")
-    gy = lax.axis_index("gy")
+    share = shares(pf, plast, coi, nb, ib, PY, XR)
+    for k in range(na * nb):
+        for i, (own, joined) in enumerate(zip((pf, plast), share)):
+            put(msg2, 2 * k + i, jnp.where(ia == k // nb, own, joined))
+
+
+def k_y3(f, xr, q1, mx, ey1, ez1, hx1, ex1, elo, m, hb, tp, bp, ts, bs, msg2, part2, v2, vn2, ex2, hy1, q2, r):
+    n = y_size()
+    gy = y_index()
     yon = jnp.where(gy < n - 1, 1.0, 0.0)
     yin = jnp.where(gy > 0, 1.0, 0.0)
     zeros = jnp.zeros((PY, PZ), F32)
@@ -391,7 +524,7 @@
         k = x if x < PX else PX + 1
         dlo = yin * (32.0 * (z[:1] - zlo) - elo[pl.ds(k, 1), :])
         ez = fplane(f, EZ, x) if x < PX else plane(xr, 1)
-        e = plane(eps, x) if x < PX else plane(xr, 4)
+        e = mx[pl.ds(at, PY), :] * 1024.0 if x < PX else plane(xr, 4)
         ie = 1.0 / e
         put(r, k, 2.0 * z - ez + (32.0 * ie) * (d - y_prev(d, dlo)))
         if x < PX:
@@ -404,13 +537,15 @@
     vn2[...] = vn
     pf, plast = ends(last, vn, plane(hb, 0, YR), plane(hb, 2, YR))
     spread(msg2, 1, (pf, plast))
-
-
-def k_y4(msg, h, b, v2, vn2, hb, tp, bp, ts, bs, bet, dele, ex2, hy1, q2, out, al, ga, w2, dw):
-    n = lax.axis_size("gy")
-    me = lax.axis_index("gy")
-    part = lambda j, k: msg[pl.ds((2 * j + k) * YR, YR), :]
-    left, right = interface(part, n, me, YR, tp, bp, ts, bs, bet, dele, al, ga)
+    nc, ic = lax.axis_size("gc"), lax.axis_index("gc")
+    spread(part2, 1, shares(pf, plast, (tp, bp, ts, bs), nc, ic, YR, YR))
+
+
+def k_y4(msg, h, b, v2, vn2, hb, *more):
+    coi, coo, (ex2, hy1, q2, out, al, ga, w2, dw) = more[:6], more[6:12], more[12:]
+    nz, nc = lax.axis_size("gz"), lax.axis_size("gc")
+    iz, ic = lax.axis_index("gz"), lax.axis_index("gc")
+    left, right = gathered(msg, nz, nc, iz, ic, YR, YR, coi, coo, al, ga)
     lw = left * plane(hb, 1, YR)
     rw = (right - vn2[...]) * plane(hb, 0, YR)
     later = right
@@ -419,7 +554,7 @@
         w2[pl.ds(j, YR, stride=PY), :] = w
         dw[pl.ds(j, YR, stride=PY), :] = later - w
         later = w
-    xon = jnp.where(lax.axis_index("gx") < lax.axis_size("gx") - 1, 1.0, 0.0)
+    xon = jnp.where(x_index() < x_size() - 1, 1.0, 0.0)
     for x in range(PX):
         w = plane(w2, x)
         nxt = plane(w2, x + 1) if x < PX - 1 else xon * plane(w2, PX + 1)
@@ -430,11 +565,11 @@
         put(out, HY * PX + x, plane(hy1, x) - 0.5 * fz(e2) + 32.0 * (nxt - w))
 
 
-def k_x4(msg, h, b, v2, vn2, hb, tp, bp, ts, bs, bet, dele, p2, out, al, ga):
-    n = lax.axis_size("gx")
-    me = lax.axis_index("gx")
-    part = lambda j, k: msg[pl.ds((2 * j + k) * PY, PY), :]
-    left, right = interface(part, n, me, PY, tp, bp, ts, bs, bet, dele, al, ga, XR)
+def k_x4(msg, h, b, v2, vn2, hb, *more):
+    coi, coo, (p2, out, al, ga) = more[:6], more[6:12], more[12:]
+    na, nb = lax.axis_size("ga"), lax.axis_size("gb")
+    ia, ib = lax.axis_index("ga"), lax.axis_index("gb")
+    left, right = gathered(msg, na, nb, ia, ib, PY, XR, coi, coo, al, ga)
     lw = left * hb[pl.ds(XR, PY), :]
     rw = (right - vn2[...]) * hb[pl.ds(0, PY), :]
     later = right
@@ -445,13 +580,14 @@
         later = w
 
 
-def call(name, parts, args, outs, scratch=(), smem=(), into=(), flush=()):
+def call(name, parts, args, outs, scratch=(), smem=(), into=(), flush=(), near=()):
     into, flush, scratch = dict(into), dict(flush), dict(scratch)
-    moved = [k for k in args if k not in smem]
+    moved = [k for k in args if k not in smem and (k not in near or k in into)]
     pieces = {k for group in flush.values() for k, _, _ in group}
     last = {k: max(i for i, (_, used) in enumerate(parts) if k in used) for k in outs}
     leave = [
-        [(k, 0, outs[k]) for k in outs if last[k] == i and k not in pieces] + list(flush.get(i, ()))
+        [(k, 0, outs[k]) for k in outs if last[k] == i and k not in pieces and k not in near]
+        + list(flush.get(i, ()))
         for i in range(len(parts))
     ]
     own = [k for k in moved if k not in into]
@@ -461,9 +597,9 @@
         hbm = {k: next(take) for k in args}
         results = {k: next(take) for k in outs}
         env = {k: next(take) for k in own}
-        env.update({k: next(take) for k in outs})
+        env.update({k: results[k] if k in near else next(take) for k in outs})
         env.update({k: next(take) for k in scratch})
-        env.update({k: hbm[k] for k in smem})
+        env.update({k: hbm[k] for k in args if k not in moved})
         sem_in, sem_out = next(take), next(take)
         pending = {}
         for i, k in enumerate(moved):
@@ -490,23 +626,25 @@
         for copy in sent:
             copy.wait()
 
-    anywhere = pl.BlockSpec(memory_space=pl.ANY)
-    scalars = pl.BlockSpec(memory_space=pltpu.SMEM)
+    far, close, scalars = [
+        pl.BlockSpec(memory_space=m) for m in (pltpu.HBM, pltpu.VMEM, pltpu.SMEM)
+    ]
     got = pl.pallas_call(
         body,
-        out_shape=[jax.ShapeDtypeStruct((c, PZ), F32) for c in outs.values()],
-        in_specs=[scalars if k in smem else anywhere for k in args],
-        out_specs=[anywhere] * len(outs),
+        out_shape=[(pltpu.VMEM if k in near else pltpu.HBM)((c, PZ), F32) for k, c in outs.items()],
+        in_specs=[scalars if k in smem else close if k in near else far for k in args],
+        out_specs=[close if k in near else far for k in outs],
         scratch_shapes=[pltpu.VMEM(args[k].shape, args[k].dtype) for k in own]
-        + [pltpu.VMEM((c, PZ), F32) for c in list(outs.values()) + list(scratch.values())]
+        + [pltpu.VMEM((c, PZ), F32) for k, c in outs.items() if k not in near]
+        + [pltpu.VMEM((c, PZ), F32) for c in scratch.values()]
         + [
             pltpu.SemaphoreType.DMA((len(moved),)),
-            pltpu.SemaphoreType.DMA((sum(len(group) for group in leave),)),
+            pltpu.SemaphoreType.DMA((max(1, sum(len(group) for group in leave)),)),
         ],
-        compiler_params=pltpu.CompilerParams(vmem_limit_bytes=56 * 1024 * 1024),
+        compiler_params=pltpu.CompilerParams(vmem_limit_bytes=LIMIT * 1024 * 1024),
         cost_estimate=pl.CostEstimate(flops=1000, bytes_accessed=1000, transcendentals=0),
         name=name,
-    )(*args.values())
+    )(*[a if k in smem else pltpu.with_memory_space_constraint(a, pltpu.VMEM if k in near else pltpu.HBM) for k, a in args.items()])
     return dict(zip(outs, got))
 
 
@@ -536,86 +674,125 @@
     return args, into
 
 
+def from_groups(own, share, buffer):
+    nz, nc = lax.axis_size("gz"), lax.axis_size("gc")
+    rows = own.shape[0]
+    args, into = {}, {}
+    for z in range(nz):
+        for c in range(nc):
+            k = buffer + str(z * nc + c)
+            route = [
+                (i * nc + j, (i + z) % nz * nc + (j + c) % nc) for i in range(nz) for j in range(nc)
+            ]
+            sent = share if z else own
+            args[k] = lax.ppermute(sent, ("gz", "gc"), route) if z or c else own
+
+            def row(z=z, c=c):
+                iz = lax.rem(lax.axis_index("gz") - z + nz, nz)
+                ic = lax.rem(lax.axis_index("gc") - c + nc, nc)
+                return pl.multiple_of((iz * nc + ic) * rows, 8)
+
+            into[k] = (buffer, row)
+    return args, into
+
+
 def local(fields, region, eps_table):
-    nx = lax.axis_size("gx")
-    ny = lax.axis_size("gy")
+    na, nb = lax.axis_size("ga"), lax.axis_size("gb")
+    along_x, along_y = ("ga", "gb"), ("gz", "gc")
+    nz, nc = lax.axis_size("gz"), lax.axis_size("gc")
+    ny = nz * nc
+    ey = (max(nz, nc) + 1) * YR
     cells = PX * PY
     nxl, nyl = PX * XR, PY * YR
     f = fields.reshape(6 * cells, PZ)
     reg = region.reshape(cells, PZ)
-    halo = ("xup", "xdn", "yup", "ydn")
-    got = call(
-        "edges",
-        [(k_edges, ("f", "reg", "table", "eps") + halo)],
-        dict(f=f, reg=reg, table=eps_table),
-        dict(eps=cells, xup=5 * PY, xdn=5 * PY, yup=6 * PX, ydn=6 * PX),
-        smem=("table",),
-    )
-    base = dict(f=f, eps=got["eps"])
-    xl = ring(got["xup"], "gx", 1)
-    xr = ring(got["xdn"], "gx", -1)
-    yl = ring(got["yup"], "gy", 1)
-    yr = ring(got["ydn"], "gy", -1)
+    xup, xdn, yup, ydn = edges(fields, region, eps_table)
+    xl = ring(xup, along_x, 1)
+    xr = ring(xdn, along_x, -1)
+    yl = ring(yup, along_y, 1)
+    yr = ring(ydn, along_y, -1)
     linex = ("mx", "hx", "bx", "vx", "hbx")
     liney = ("my", "hy", "by", "vy", "hby")
     one = call(
         "one",
         [
+            (k_eps, ("reg", "table", "eps")),
             (k_x1, ("f", "eps", "xl", "xr", "yl", "yr", "msgx", "q1") + linex + ("r",)),
             (k_y1, ("f", "eps", "xl", "xr", "msgy", "p1", "ey1") + liney + ("rt", "ep")),
         ],
-        dict(base, xl=xl, xr=xr, yl=yl, yr=yr),
+        dict(reg=reg, f=f, xl=xl, xr=xr, yl=yl, yr=yr, table=eps_table),
         dict(
             zip(
                 ("msgx", "q1") + linex + ("msgy", "p1", "ey1") + liney,
-                (nx * (5 * XR + 8), cells, nxl, nxl, nxl, nxl, 4 * XR)
+                (nb * XB, cells, nxl, nxl, nxl, nxl, 4 * XR)
                 + (7 * YR, cells + PY, cells + PY, nyl, nyl, nyl, nyl, 4 * YR),
             )
         ),
-        dict(r=nxl, rt=YR * PY, ep=YR * PY),
+        dict(eps=cells, r=nxl, rt=YR * PY, ep=YR * PY),
+        smem=("table",),
+        near=("xl", "xr", "yl", "yr", "msgy"),
     )
-    gotx = swap(one["msgx"], "gx")
-    argy, into = from_all(one["msgy"], "gy", "gy")
+    pair, into = from_all(one["msgy"], "gc", "gyi")
+    group = call(
+        "group",
+        [
+            (k_join_y, ("gyi", "msgyo")),
+            (k_join_x, ("gi", "msgo", "inner")),
+        ],
+        dict(pair, gi=swap(one["msgx"], "gb")),
+        dict(msgyo=YB, msgo=na * XB, inner=nb * XB),
+        dict(gyi=nc * YB),
+        into=into,
+        near=("gi", "msgyo") + tuple(pair),
+    )
+    goto = swap(group["msgo"], "ga")
+    argy, into_o = from_all(group["msgyo"], "gz", "gyo")
+    argy.update(pair)
+    into.update(into_o)
     chains = ("tp", "bp", "ts", "bs", "bet", "del")
-    cx, cy = [tuple(k + a for k in chains) for a in "xy"]
+    ci, co, cyi, cyo = [tuple(k + a for k in chains) for a in ("i", "o", "yi", "yo")]
+    cx, cy = ci + co, cyi + cyo
     size = lambda n, rows: (n * rows,) * 4 + ((n + 1) * rows,) * 2
     keep = {k: one[k] for k in ("q1", "p1", "ey1") + linex + liney}
     two = call(
         "two",
         [
-            (k_y2, ("gy", "p1", "hy", "by", "vy", "hby", "ex1", "p2", "elo") + cy + ("aly", "gay", "dex")),
+            (k_y2, ("gyi", "gyo", "p1", "hy", "by", "vy", "hby", "ex1", "p2", "elo") + cy + ("aly", "gay", "dex")),
             (
                 k_x2,
-                ("gx", "f", "eps", "q1", "ey1", "p2", "hx", "bx", "vx", "mx", "hbx")
+                ("gi", "go", "f", "q1", "ey1", "p2", "hx", "bx", "vx", "mx", "hbx")
                 + ("ez1", "hx1", "msgx2", "vx2", "vnx2")
                 + cx
                 + ("alx", "gax", "r"),
             ),
             (
                 k_y3,
-                ("f", "xr", "q1", "eps", "ey1", "ez1", "hx1", "ex1", "elo", "my", "hby")
-                + ("msgy2", "vy2", "vny2", "ex2", "hy1", "q2", "rt"),
+                ("f", "xr", "q1", "mx", "ey1", "ez1", "hx1", "ex1", "elo", "my", "hby")
+                + cyi[:4] + ("msgy2", "party2", "vy2", "vny2", "ex2", "hy1", "q2", "rt"),
             ),
         ],
-        dict(argy, gx=gotx, xr=xr, **base, **keep),
+        dict(argy, gi=group["inner"], go=goto, xr=xr, f=f, **keep),
         dict(
             zip(
-                ("p2",) + cy + ("msgx2", "vx2", "vnx2") + cx + ("msgy2", "vy2", "vny2", "ex2", "hy1", "q2"),
+                ("p2",) + cy + ("msgx2", "vx2", "vnx2") + cx + ("msgy2", "party2", "vy2", "vny2", "ex2", "hy1", "q2"),
                 (cells + PY,)
-                + size(ny, YR)
-                + (nx * 2 * PY, cells, PY)
-                + size(nx, XR)
-                + (2 * YR, nyl, YR, cells, cells, cells),
+                + size(nc, YR)
+                + size(nz, YR)
+                + (na * nb * 2 * PY, cells, PY)
+                + size(nb, XR)
+                + size(na, XR)
+                + (2 * YR, 2 * YR, nyl, YR, cells, cells, cells),
             )
         ),
         dict(
-            gy=ny * 7 * YR, ex1=YR * PY, elo=YR, aly=(ny + 1) * YR, gay=(ny + 1) * YR, dex=YR * PY,
-            ez1=nxl + XR, hx1=cells, alx=(nx + 1) * XR, gax=(nx + 1) * XR, r=cells, rt=YR * PY,
+            gyi=nc * YB, gyo=nz * YB, ex1=YR * PY, elo=YR, aly=ey, gay=ey, dex=YR * PY,
+            ez1=nxl + XR, hx1=cells, alx=(max(na, nb) + 1) * XR, gax=(max(na, nb) + 1) * XR, r=cells, rt=YR * PY,
         ),
         into=into,
+        near=("go", "msgy2", "party2") + tuple(k for k in argy if k not in pair),
     )
-    gotx = swap(two["msgx2"], "gx")
-    argy, into = from_all(two["msgy2"], "gy", "gy")
+    gotx = swap(two["msgx2"], along_x)
+    argy, into = from_groups(two["msgy2"], two["party2"], "gy")
     need = {k: one[k] for k in ("hx", "bx", "hbx", "hy", "by", "hby")}
     need.update({k: two[k] for k in ("p2",) + cy + cx + ("vx2", "vnx2", "vy2", "vny2", "ex2", "hy1", "q2")})
     three = call(
@@ -631,10 +808,11 @@
         dict(argy, gx=gotx, **need),
         dict(out=6 * cells),
         dict(
-            gy=ny * 2 * YR, aly=(ny + 1) * YR, gay=(ny + 1) * YR, w2=YR * PY, dw=YR * PY,
-            alx=(nx + 1) * PY, gax=(nx + 1) * PY,
+            gy=ny * 2 * YR, aly=ey, gay=ey, w2=YR * PY, dw=YR * PY,
+            alx=(max(na, nb) + 1) * PY, gax=(max(na, nb) + 1) * PY,
         ),
         into=into,
+        near=("gx",) + tuple(argy),
         flush={
             0: [("out", EX * cells, cells), ("out", EZ * cells, 3 * cells)],
             1: [("out", EY * cells, cells), ("out", HZ * cells, cells)],
@@ -644,10 +822,15 @@
 
 
 def solution(mesh):
+    nx, ny = mesh.devices.shape
+    nb = max(d for d in range(1, nx + 1) if nx % d == 0 and d * d <= nx)
+    shape = (nx // nb, nb, ny // 2, 2)
+    grid = Mesh(mesh.devices.reshape(shape), ("ga", "gb", "gz", "gc"))
+    columns = P(("ga", "gb"), ("gz", "gc"), None)
     return jax.shard_map(
         local,
-        mesh=mesh,
-        in_specs=(P(None, "gx", "gy", None), P("gx", "gy", None), P()),
-        out_specs=P(None, "gx", "gy", None),
+        mesh=grid,
+        in_specs=(P(None, *columns), columns, P()),
+        out_specs=P(None, *columns),
         check_vma=False,
     )

time: 80.9 us -> 72.8 us (0.90)
  waiting for transfers between devices: 24.8 us -> 19.8 us
  local copies, waits for them, and re-layouts: 2.6 us -> 0.02 us
  Pallas kernels: 20 us -> 19 us
    ppermute x18 -> x8, starting transfers between devices: 24.7 us -> 13.7 us  [ring(): return lax.ppermute(block, axis, [(i, (i + step) % n) for i in range(n)])]
    ppermute x0 -> x7, starting transfers between devices: none -> 7.22 us  [from_groups(): args[k] = lax.ppermute(sent, ('gz', 'gc'), route) if z or c else own]
    ppermute x18 -> x8, waiting for transfers between devices: 14.1 us -> 8.45 us  [ring(): return lax.ppermute(block, axis, [(i, (i + step) % n) for i in range(n)])]
    all_to_all x2 -> x3, starting transfers between devices: 7.77 us -> 12.1 us  [swap(): got = lax.all_to_all(msg.reshape(n, -1, PZ), axis, 0, 0, tiled=True)]
    ppermute x0 -> x7, waiting for transfers between devices: none -> 3.58 us  [from_groups(): args[k] = lax.ppermute(sent, ('gz', 'gc'), route) if z or c else own]
    all_to_all x2 -> x3, waiting for transfers between devices: 10.7 us -> 7.83 us  [swap(): got = lax.all_to_all(msg.reshape(n, -1, PZ), axis, 0, 0, tiled=True)]
    unnamed x42 -> x8, local copies, waits for them, and re-layouts: 2.6 us -> 0.02 us
    pallas_call x4 -> x5, Pallas kernels: 20 us -> 19 us  [the longest x4 17.4 us: call(): pl.pallas_call(body, out_shape=[(pltpu.VMEM if k in near else pltpu.HBM)(...]
  transfers between devices with their start and end apart: 20 -> 18, of which waited for: 13 -> 8; matrix products, arithmetic and copies ran while one was open for 0% -> 0% of each run, Pallas kernels for 0% -> 0%
where the time goes in v2:
time: 72.8 us; the launch traced here: 72.1 us
  starting transfers between devices  33 us (45%)
  waiting for transfers between devices  19.8 us (27%)
  Pallas kernels  19 us (26%)
    pallas_call x4, Pallas kernels, call(): pl.pallas_call(body, out_shape=[(pltpu.VMEM if k in near else pltpu.HBM)(...  17.4 us
    ppermute x8, starting transfers between devices, ring(): return lax.ppermute(block, axis, [(i, (i + step) % n) for i in range(n)])  13.7 us
    all_to_all x3, starting transfers between devices, swap(): got = lax.all_to_all(msg.reshape(n, -1, PZ), axis, 0, 0, tiled=True)  12.1 us
    ppermute x8, waiting for transfers between devices, ring(): return lax.ppermute(block, axis, [(i, (i + step) % n) for i in range(n)])  8.45 us
    all_to_all x3, waiting for transfers between devices, swap(): got = lax.all_to_all(msg.reshape(n, -1, PZ), axis, 0, 0, tiled=True)  7.83 us
    ppermute x7, starting transfers between devices, from_groups(): args[k] = lax.ppermute(sent, ('gz', 'gc'), route) if z or c else own  7.22 us
    ppermute x7, waiting for transfers between devices, from_groups(): args[k] = lax.ppermute(sent, ('gz', 'gc'), route) if z or c else own  3.58 us
    pallas_call x1, Pallas kernels, edges(): pl.pallas_call(k_edges, out_shape=[pltpu.VMEM((c, PZ), F32) for c in (5 *...  1.58 us
  transfers between devices with their start and end apart: 18, of which 8 were waited for; matrix products, arithmetic and copies ran while one was open for 0% of the time, Pallas kernels for 0%

profile of v2, /device:TPU:0, one launch (start us, length us, event | category | flops | bytes accessed | tf_op | source)
XLA Modules:
  0.0 72.1 jit_solution(12708223337762942186)
XLA Ops:
  0.0 0.0 copy-start.3
  0.0 1.6 %edges.1 = (f32[160,128]{1,0:T(8,128)S(1)}, f32[160,128]{1,0:T(8,128)S(1)}, f32[96,128]{1,0:T(8,128)S(1)}, f32[96,128]{1,0:T(8,128)S(1)}) custom-call(f32[6,16,32,128]{3,2,1,0:T(8,128)} %f.1, s32[16,32,128]{2,1,0:T(8,128)} %reg.1, f32[16]{0:T(128)} %refs_6_.1), custom_call_target="tpu_custom_call" | custom-call | flops 1000 | bytes 1000 | tf_op jit(solution)/shard_map/edges/pallas_call | solution.py:124
  1.6 1.7 %collective-permute-start = (f32[160,128]{1,0:T(8,128)S(1)}, f32[160,128]{1,0:T(8,128)S(1)}, u32[]{:S(2)}, u32[]{:S(2)}) collective-permute-start(f32[160,128]{1,0:T(8,128)S(1)} %get-tuple-element.62), channel_id=1, source_target_pairs={{0,8},{8,16},{16,24},{24,32},{32,40},{40,48},{48,56},{56,64},{64,7... | collective-permute-start | bytes 245768 | tf_op jit(solution)/shard_map/ppermute | solution.py:653
  3.3 3.7 %collective-permute-start.1 = (f32[160,128]{1,0:T(8,128)S(1)}, f32[160,128]{1,0:T(8,128)S(1)}, u32[]{:S(2)}, u32[]{:S(2)}) collective-permute-start(f32[160,128]{1,0:T(8,128)S(1)} %get-tuple-element.63), channel_id=1, source_target_pairs={{0,120},{8,0},{16,8},{24,16},{32,24},{40,32},{48,40},{56,48},{64,5... | collective-permute-start | bytes 245768 | tf_op jit(solution)/shard_map/ppermute | solution.py:653
  7.0 0.0 collective-permute-start.2
  7.0 3.2 %collective-permute-start.3 = (f32[96,128]{1,0:T(8,128)S(1)}, f32[96,128]{1,0:T(8,128)S(1)}, u32[]{:S(2)}, u32[]{:S(2)}) collective-permute-start(f32[96,128]{1,0:T(8,128)S(1)} %get-tuple-element.65), channel_id=1, source_target_pairs={{0,7},{1,0},{2,1},{3,2},{4,3},{5,4},{6,5},{7,6},{8,15},{9,8},{10,9... | collective-permute-start | bytes 147464 | tf_op jit(solution)/shard_map/ppermute | solution.py:653
  10.2 1.8 %collective-permute-done.2.refs_4_ = f32[96,128]{1,0:T(8,128)S(1)} collective-permute-done((f32[96,128]{1,0:T(8,128)S(1)}, f32[96,128]{1,0:T(8,128)S(1)}, u32[]{:S(2)}, u32[]{:S(2)}) %collective-permute-start.2) | collective-permute-done | bytes 49184 | tf_op jit(solution)/shard_map/ppermute | solution.py:653
  12.0 0.0 collective-permute-done.3.refs_5_
  12.0 0.0 collective-permute-done.refs_2_
  12.0 0.0 collective-permute-done.1.refs_3_.refs_8_
  12.0 0.0 copy-start.2
  12.0 0.0 copy-done.3
  12.0 4.9 %one.1 = (f32[832,128]{1,0:T(8,128)}, f32[512,128]{1,0:T(8,128)}, f32[640,128]{1,0:T(8,128)}, f32[640,128]{1,0:T(8,128)}, f32[640,128]{1,0:T(8,128)}, /*index=5*...) custom-call(s32[512,128]{1,0:T(8,128)} %bitcast.14, ...), custom_call_target="tpu_custom_call" | custom-call | flops 1000 | bytes 1000 | tf_op jit(solution)/shard_map/one/pallas_call | solution.py:632
  16.9 0.0 copy-start
  16.9 3.5 %all-to-all-start = ((f32[4,208,128]{2,1,0:T(8,128)}), f32[4,208,128]{2,1,0:T(8,128)S(1)}, u32[]{:S(2)}, u32[]{:S(2)}) async-start(f32[4,208,128]{2,1,0:T(8,128)} %bitcast.16), calls=%async_computation | async-start | bytes 851968 | tf_op jit(solution)/shard_map/all_to_all | solution.py:658
  20.4 0.7 collective-permute-start.4
  21.1 0.9 %collective-permute-done.4.refs_1_.refs_5_ = f32[168,128]{1,0:T(8,128)S(1)} collective-permute-done((f32[168,128]{1,0:T(8,128)S(1)}, f32[168,128]{1,0:T(8,128)S(1)}, u32[]{:S(2)}, u32[]{:S(2)}) %collective-permute-start.4) | collective-permute-done | bytes 86048 | tf_op jit(solution)/shard_map/ppermute | solution.py:653
  22.1 0.0 copy-start.1
  22.1 7.8 %all-to-all-done = f32[4,208,128]{2,1,0:T(8,128)S(1)} async-done(((f32[4,208,128]{2,1,0:T(8,128)}), f32[4,208,128]{2,1,0:T(8,128)S(1)}, u32[]{:S(2)}, u32[]{:S(2)}) %all-to-all-start) | async-done | bytes 426016 | tf_op jit(solution)/shard_map/all_to_all | solution.py:658
  29.9 1.2 %group.1 = (f32[168,128]{1,0:T(8,128)S(1)}, f32[832,128]{1,0:T(8,128)}, f32[832,128]{1,0:T(8,128)}) custom-call(f32[168,128]{1,0:T(8,128)S(1)} %get-tuple-element.66.refs_0_.refs_4_, f32[168,128]{1,0:T(8,128)S(1)} %collective-permute-done.4.refs_1_.refs_5_, f32[832,128]{1,0:T(8,128)S(1)} %bitcast.10), custom_call_target="tpu_custom_call" | custom-call | flops 1000 | bytes 1000 | tf_op jit(solution)/shard_map/group/pallas_call | solution.py:632
  31.1 0.0 copy-done.2
  31.1 3.5 %all-to-all-start.1 = ((f32[4,208,128]{2,1,0:T(8,128)}), f32[4,208,128]{2,1,0:T(8,128)S(1)}, u32[]{:S(2)}, u32[]{:S(2)}) async-start(f32[4,208,128]{2,1,0:T(8,128)} %bitcast.17), calls=%async_computation.1 | async-start | bytes 851968 | tf_op jit(solution)/shard_map/all_to_all | solution.py:658
  34.6 2.8 %collective-permute-start.7 = (f32[168,128]{1,0:T(8,128)S(1)}, f32[168,128]{1,0:T(8,128)S(1)}, u32[]{:S(2)}, u32[]{:S(2)}) collective-permute-start(f32[168,128]{1,0:T(8,128)S(1)} %get-tuple-element.68.refs_0_), channel_id=1, source_target_pairs={{0,6},{2,0},{4,2},{6,4},{1,7},{3,1},{5,3},{7,5},{8,14},{10,8},{12,... | collective-permute-start | bytes 258056 | tf_op jit(solution)/shard_map/ppermute | solution.py:653
  37.4 0.5 collective-permute-start.6
  37.9 1.0 %collective-permute-start.5 = (f32[168,128]{1,0:T(8,128)S(1)}, f32[168,128]{1,0:T(8,128)S(1)}, u32[]{:S(2)}, u32[]{:S(2)}) collective-permute-start(f32[168,128]{1,0:T(8,128)S(1)} %get-tuple-element.68.refs_0_), channel_id=1, source_target_pairs={{0,2},{2,4},{4,6},{6,0},{1,3},{3,5},{5,7},{7,1},{8,10},{10,12},{12... | collective-permute-start | bytes 258056 | tf_op jit(solution)/shard_map/ppermute | solution.py:653
  38.9 2.1 %collective-permute-done.7.refs_3_ = f32[168,128]{1,0:T(8,128)S(1)} collective-permute-done((f32[168,128]{1,0:T(8,128)S(1)}, f32[168,128]{1,0:T(8,128)S(1)}, u32[]{:S(2)}, u32[]{:S(2)}) %collective-permute-start.7) | collective-permute-done | bytes 86048 | tf_op jit(solution)/shard_map/ppermute | solution.py:653
  41.0 2.8 %collective-permute-done.6.refs_2_ = f32[168,128]{1,0:T(8,128)S(1)} collective-permute-done((f32[168,128]{1,0:T(8,128)S(1)}, f32[168,128]{1,0:T(8,128)S(1)}, u32[]{:S(2)}, u32[]{:S(2)}) %collective-permute-start.6) | collective-permute-done | bytes 86048 | tf_op jit(solution)/shard_map/ppermute | solution.py:653
  43.9 0.8 %collective-permute-done.5.refs_1_ = f32[168,128]{1,0:T(8,128)S(1)} collective-permute-done((f32[168,128]{1,0:T(8,128)S(1)}, f32[168,128]{1,0:T(8,128)S(1)}, u32[]{:S(2)}, u32[]{:S(2)}) %collective-permute-start.5) | collective-permute-done | bytes 86048 | tf_op jit(solution)/shard_map/ppermute | solution.py:653
  44.7 0.0 all-to-all-done.1
  44.7 0.0 copy-done
  44.7 0.0 copy-done.1
  44.7 6.6 %two.1 = (f32[544,128]{1,0:T(8,128)}, f32[48,128]{1,0:T(8,128)}, f32[48,128]{1,0:T(8,128)}, f32[48,128]{1,0:T(8,128)}, f32[48,128]{1,0:T(8,128)}, /*index=5*/f32...) custom-call(f32[168,128]{1,0:T(8,128)S(1)} %get-tuple-element.68.ref, ...), custom_call_target="tpu_custom_call" | custom-call | flops 1000 | bytes 1000 | tf_op jit(solution)/shard_map/two/pallas_call | solution.py:632
  51.3 5.2 %all-to-all-start.2 = ((f32[16,64,128]{2,1,0:T(8,128)}), f32[16,64,128]{2,1,0:T(8,128)S(1)}, u32[]{:S(2)}, u32[]{:S(2)}) async-start(f32[16,64,128]{2,1,0:T(8,128)} %bitcast.15), calls=%async_computation.2 | async-start | bytes 1048576 | tf_op jit(solution)/shard_map/all_to_all | solution.py:658
  56.5 0.1 collective-permute-start.8
  56.6 0.7 collective-permute-start.14
  57.3 0.9 %collective-permute-start.13 = (f32[48,128]{1,0:T(8,128)S(1)}, f32[48,128]{1,0:T(8,128)S(1)}, u32[]{:S(2)}, u32[]{:S(2)}) collective-permute-start(f32[48,128]{1,0:T(8,128)S(1)} %get-tuple-element.85), channel_id=1, source_target_pairs={{0,6},{1,7},{2,0},{3,1},{4,2},{5,3},{6,4},{7,5},{8,14},{9,15},{10,... | collective-permute-start | bytes 73736 | tf_op jit(solution)/shard_map/ppermute | solution.py:688
  58.2 2.0 %collective-permute-start.12 = (f32[48,128]{1,0:T(8,128)S(1)}, f32[48,128]{1,0:T(8,128)S(1)}, u32[]{:S(2)}, u32[]{:S(2)}) collective-permute-start(f32[48,128]{1,0:T(8,128)S(1)} %get-tuple-element.85), channel_id=1, source_target_pairs={{0,5},{1,4},{2,7},{3,6},{4,1},{5,0},{6,3},{7,2},{8,13},{9,12},{10,... | collective-permute-start | bytes 73736 | tf_op jit(solution)/shard_map/ppermute | solution.py:688
  60.2 0.9 %collective-permute-start.11 = (f32[48,128]{1,0:T(8,128)S(1)}, f32[48,128]{1,0:T(8,128)S(1)}, u32[]{:S(2)}, u32[]{:S(2)}) collective-permute-start(f32[48,128]{1,0:T(8,128)S(1)} %get-tuple-element.85), channel_id=1, source_target_pairs={{0,4},{1,5},{2,6},{3,7},{4,0},{5,1},{6,2},{7,3},{8,12},{9,13},{10,... | collective-permute-start | bytes 73736 | tf_op jit(solution)/shard_map/ppermute | solution.py:688
  61.1 0.0 collective-permute-done.8.refs_1_
  61.1 1.1 %collective-permute-start.10 = (f32[48,128]{1,0:T(8,128)S(1)}, f32[48,128]{1,0:T(8,128)S(1)}, u32[]{:S(2)}, u32[]{:S(2)}) collective-permute-start(f32[48,128]{1,0:T(8,128)S(1)} %get-tuple-element.85), channel_id=1, source_target_pairs={{0,3},{1,2},{2,5},{3,4},{4,7},{5,6},{6,1},{7,0},{8,11},{9,10},{10,... | collective-permute-start | bytes 73736 | tf_op jit(solution)/shard_map/ppermute | solution.py:688
  62.3 0.0 collective-permute-done.14.refs_7_
  62.3 1.5 %collective-permute-start.9 = (f32[48,128]{1,0:T(8,128)S(1)}, f32[48,128]{1,0:T(8,128)S(1)}, u32[]{:S(2)}, u32[]{:S(2)}) collective-permute-start(f32[48,128]{1,0:T(8,128)S(1)} %get-tuple-element.85), channel_id=1, source_target_pairs={{0,2},{1,3},{2,4},{3,5},{4,6},{5,7},{6,0},{7,1},{8,10},{9,11},{10,... | collective-permute-start | bytes 73736 | tf_op jit(solution)/shard_map/ppermute | solution.py:688
  63.7 0.0 collective-permute-done.13.refs_6_
  63.7 0.0 collective-permute-done.12.refs_5_
  63.7 2.0 %collective-permute-done.11.refs_4_ = f32[48,128]{1,0:T(8,128)S(1)} collective-permute-done((f32[48,128]{1,0:T(8,128)S(1)}, f32[48,128]{1,0:T(8,128)S(1)}, u32[]{:S(2)}, u32[]{:S(2)}) %collective-permute-start.11) | collective-permute-done | bytes 24608 | tf_op jit(solution)/shard_map/ppermute | solution.py:688
  65.8 0.0 collective-permute-done.10.refs_3_
  65.8 1.5 %collective-permute-done.9.refs_2_ = f32[48,128]{1,0:T(8,128)S(1)} collective-permute-done((f32[48,128]{1,0:T(8,128)S(1)}, f32[48,128]{1,0:T(8,128)S(1)}, u32[]{:S(2)}, u32[]{:S(2)}) %collective-permute-start.9) | collective-permute-done | bytes 24608 | tf_op jit(solution)/shard_map/ppermute | solution.py:688
  67.3 0.0 all-to-all-done.2
  67.3 4.7 %three.1 = f32[3072,128]{1,0:T(8,128)} custom-call(f32[48,128]{1,0:T(8,128)S(1)} %get-tuple-element.84.refs_0_, f32[48,128]{1,0:T(8,128)S(1)} %collective-permute-done.8.refs_1_, f32[48,128]{1,0:T(8,128)S(1)} %collective-permute-done.9.refs_2_, f32[48,128]{1,0:T(8,128)S(1)} %collective-permute-done.10.refs_3_, ...), custom_call_target="tpu_custom_call" | custom-call | flops 1000 | bytes 1000 | tf_op jit(solution)/shard_map/three/pallas_call | solution.py:632
Async XLA Ops:
  0.0 12.0 %copy-start.3 = (f32[16]{0:T(128)S(1)}, f32[16]{0:T(128)}, u32[]{:S(2)}) copy-start(f32[16]{0:T(128)} %refs_6_.1) | copy-start | bytes 196
  1.6 10.4 %collective-permute-start = (f32[160,128]{1,0:T(8,128)S(1)}, f32[160,128]{1,0:T(8,128)S(1)}, u32[]{:S(2)}, u32[]{:S(2)}) collective-permute-start(f32[160,128]{1,0:T(8,128)S(1)} %get-tuple-element.62), channel_id=1, source_target_pairs={{0,8},{8,16},{16,24},{24,32},{32,40},{40,48},{48,56},{56,64},{64,7... | collective-permute-start | bytes 245768 | tf_op jit(solution)/shard_map/ppermute | solution.py:653
  3.3 8.7 %collective-permute-start.1 = (f32[160,128]{1,0:T(8,128)S(1)}, f32[160,128]{1,0:T(8,128)S(1)}, u32[]{:S(2)}, u32[]{:S(2)}) collective-permute-start(f32[160,128]{1,0:T(8,128)S(1)} %get-tuple-element.63), channel_id=1, source_target_pairs={{0,120},{8,0},{16,8},{24,16},{32,24},{40,32},{48,40},{56,48},{64,5... | collective-permute-start | bytes 245768 | tf_op jit(solution)/shard_map/ppermute | solution.py:653
  7.0 5.0 %collective-permute-start.2 = (f32[96,128]{1,0:T(8,128)S(1)}, f32[96,128]{1,0:T(8,128)S(1)}, u32[]{:S(2)}, u32[]{:S(2)}) collective-permute-start(f32[96,128]{1,0:T(8,128)S(1)} %get-tuple-element.64), channel_id=1, source_target_pairs={{0,1},{1,2},{2,3},{3,4},{4,5},{5,6},{6,7},{7,0},{8,9},{9,10},{10,1... | collective-permute-start | bytes 147464 | tf_op jit(solution)/shard_map/ppermute | solution.py:653
  7.0 5.0 %collective-permute-start.3 = (f32[96,128]{1,0:T(8,128)S(1)}, f32[96,128]{1,0:T(8,128)S(1)}, u32[]{:S(2)}, u32[]{:S(2)}) collective-permute-start(f32[96,128]{1,0:T(8,128)S(1)} %get-tuple-element.65), channel_id=1, source_target_pairs={{0,7},{1,0},{2,1},{3,2},{4,3},{5,4},{6,5},{7,6},{8,15},{9,8},{10,9... | collective-permute-start | bytes 147464 | tf_op jit(solution)/shard_map/ppermute | solution.py:653
  12.0 19.1 %copy-start.2 = (f32[160,128]{1,0:T(8,128)}, f32[160,128]{1,0:T(8,128)S(1)}, u32[]{:S(2)}) copy-start(f32[160,128]{1,0:T(8,128)S(1)} %collective-permute-done.1.refs_3_.refs_8_) | copy-start | bytes 245764
  16.9 27.8 %copy-start = (f32[168,128]{1,0:T(8,128)}, f32[168,128]{1,0:T(8,128)S(1)}, u32[]{:S(2)}) copy-start(f32[168,128]{1,0:T(8,128)S(1)} %get-tuple-element.66.refs_0_.refs_4_) | copy-start | bytes 258052
  16.9 12.9 %all-to-all-start = ((f32[4,208,128]{2,1,0:T(8,128)}), f32[4,208,128]{2,1,0:T(8,128)S(1)}, u32[]{:S(2)}, u32[]{:S(2)}) async-start(f32[4,208,128]{2,1,0:T(8,128)} %bitcast.16), calls=%async_computation | async-start | bytes 851968 | tf_op jit(solution)/shard_map/all_to_all | solution.py:658
  20.4 1.6 %collective-permute-start.4 = (f32[168,128]{1,0:T(8,128)S(1)}, f32[168,128]{1,0:T(8,128)S(1)}, u32[]{:S(2)}, u32[]{:S(2)}) collective-permute-start(f32[168,128]{1,0:T(8,128)S(1)} %get-tuple-element.66.refs_0_.refs_4_), channel_id=1, source_target_pairs={{0,1},{1,0},{2,3},{3,2},{4,5},{5,4},{6,7},{7,6},{8,9},{9,8},{10,11... | collective-permute-start | bytes 258056 | tf_op jit(solution)/shard_map/ppermute | solution.py:653
  22.1 22.6 %copy-start.1 = (f32[168,128]{1,0:T(8,128)}, f32[168,128]{1,0:T(8,128)S(1)}, u32[]{:S(2)}) copy-start(f32[168,128]{1,0:T(8,128)S(1)} %collective-permute-done.4.refs_1_.refs_5_) | copy-start | bytes 258052
  31.1 13.6 %all-to-all-start.1 = ((f32[4,208,128]{2,1,0:T(8,128)}), f32[4,208,128]{2,1,0:T(8,128)S(1)}, u32[]{:S(2)}, u32[]{:S(2)}) async-start(f32[4,208,128]{2,1,0:T(8,128)} %bitcast.17), calls=%async_computation.1 | async-start | bytes 851968 | tf_op jit(solution)/shard_map/all_to_all | solution.py:658
  34.6 6.5 %collective-permute-start.7 = (f32[168,128]{1,0:T(8,128)S(1)}, f32[168,128]{1,0:T(8,128)S(1)}, u32[]{:S(2)}, u32[]{:S(2)}) collective-permute-start(f32[168,128]{1,0:T(8,128)S(1)} %get-tuple-element.68.refs_0_), channel_id=1, source_target_pairs={{0,6},{2,0},{4,2},{6,4},{1,7},{3,1},{5,3},{7,5},{8,14},{10,8},{12,... | collective-permute-start | bytes 258056 | tf_op jit(solution)/shard_map/ppermute | solution.py:653
  37.4 6.5 %collective-permute-start.6 = (f32[168,128]{1,0:T(8,128)S(1)}, f32[168,128]{1,0:T(8,128)S(1)}, u32[]{:S(2)}, u32[]{:S(2)}) collective-permute-start(f32[168,128]{1,0:T(8,128)S(1)} %get-tuple-element.68.refs_0_), channel_id=1, source_target_pairs={{0,4},{2,6},{4,0},{6,2},{1,5},{3,7},{5,1},{7,3},{8,12},{10,14},{12... | collective-permute-start | bytes 258056 | tf_op jit(solution)/shard_map/ppermute | solution.py:653
  37.9 6.8 %collective-permute-start.5 = (f32[168,128]{1,0:T(8,128)S(1)}, f32[168,128]{1,0:T(8,128)S(1)}, u32[]{:S(2)}, u32[]{:S(2)}) collective-permute-start(f32[168,128]{1,0:T(8,128)S(1)} %get-tuple-element.68.refs_0_), channel_id=1, source_target_pairs={{0,2},{2,4},{4,6},{6,0},{1,3},{3,5},{5,7},{7,1},{8,10},{10,12},{12... | collective-permute-start | bytes 258056 | tf_op jit(solution)/shard_map/ppermute | solution.py:653
  51.3 16.0 %all-to-all-start.2 = ((f32[16,64,128]{2,1,0:T(8,128)}), f32[16,64,128]{2,1,0:T(8,128)S(1)}, u32[]{:S(2)}, u32[]{:S(2)}) async-start(f32[16,64,128]{2,1,0:T(8,128)} %bitcast.15), calls=%async_computation.2 | async-start | bytes 1048576 | tf_op jit(solution)/shard_map/all_to_all | solution.py:658
  56.5 4.6 %collective-permute-start.8 = (f32[48,128]{1,0:T(8,128)S(1)}, f32[48,128]{1,0:T(8,128)S(1)}, u32[]{:S(2)}, u32[]{:S(2)}) collective-permute-start(f32[48,128]{1,0:T(8,128)S(1)} %get-tuple-element.84.refs_0_), channel_id=1, source_target_pairs={{0,1},{1,0},{2,3},{3,2},{4,5},{5,4},{6,7},{7,6},{8,9},{9,8},{10,11... | collective-permute-start | bytes 73736 | tf_op jit(solution)/shard_map/ppermute | solution.py:688
  56.6 5.7 %collective-permute-start.14 = (f32[48,128]{1,0:T(8,128)S(1)}, f32[48,128]{1,0:T(8,128)S(1)}, u32[]{:S(2)}, u32[]{:S(2)}) collective-permute-start(f32[48,128]{1,0:T(8,128)S(1)} %get-tuple-element.85), channel_id=1, source_target_pairs={{0,7},{1,6},{2,1},{3,0},{4,3},{5,2},{6,5},{7,4},{8,15},{9,14},{10,... | collective-permute-start | bytes 73736 | tf_op jit(solution)/shard_map/ppermute | solution.py:688
  57.3 6.5 %collective-permute-start.13 = (f32[48,128]{1,0:T(8,128)S(1)}, f32[48,128]{1,0:T(8,128)S(1)}, u32[]{:S(2)}, u32[]{:S(2)}) collective-permute-start(f32[48,128]{1,0:T(8,128)S(1)} %get-tuple-element.85), channel_id=1, source_target_pairs={{0,6},{1,7},{2,0},{3,1},{4,2},{5,3},{6,4},{7,5},{8,14},{9,15},{10,... | collective-permute-start | bytes 73736 | tf_op jit(solution)/shard_map/ppermute | solution.py:688
  58.2 5.5 %collective-permute-start.12 = (f32[48,128]{1,0:T(8,128)S(1)}, f32[48,128]{1,0:T(8,128)S(1)}, u32[]{:S(2)}, u32[]{:S(2)}) collective-permute-start(f32[48,128]{1,0:T(8,128)S(1)} %get-tuple-element.85), channel_id=1, source_target_pairs={{0,5},{1,4},{2,7},{3,6},{4,1},{5,0},{6,3},{7,2},{8,13},{9,12},{10,... | collective-permute-start | bytes 73736 | tf_op jit(solution)/shard_map/ppermute | solution.py:688
  60.2 5.6 %collective-permute-start.11 = (f32[48,128]{1,0:T(8,128)S(1)}, f32[48,128]{1,0:T(8,128)S(1)}, u32[]{:S(2)}, u32[]{:S(2)}) collective-permute-start(f32[48,128]{1,0:T(8,128)S(1)} %get-tuple-element.85), channel_id=1, source_target_pairs={{0,4},{1,5},{2,6},{3,7},{4,0},{5,1},{6,2},{7,3},{8,12},{9,13},{10,... | collective-permute-start | bytes 73736 | tf_op jit(solution)/shard_map/ppermute | solution.py:688
  61.1 4.7 %collective-permute-start.10 = (f32[48,128]{1,0:T(8,128)S(1)}, f32[48,128]{1,0:T(8,128)S(1)}, u32[]{:S(2)}, u32[]{:S(2)}) collective-permute-start(f32[48,128]{1,0:T(8,128)S(1)} %get-tuple-element.85), channel_id=1, source_target_pairs={{0,3},{1,2},{2,5},{3,4},{4,7},{5,6},{6,1},{7,0},{8,11},{9,10},{10,... | collective-permute-start | bytes 73736 | tf_op jit(solution)/shard_map/ppermute | solution.py:688
  62.3 5.0 %collective-permute-start.9 = (f32[48,128]{1,0:T(8,128)S(1)}, f32[48,128]{1,0:T(8,128)S(1)}, u32[]{:S(2)}, u32[]{:S(2)}) collective-permute-start(f32[48,128]{1,0:T(8,128)S(1)} %get-tuple-element.85), channel_id=1, source_target_pairs={{0,2},{1,3},{2,4},{3,5},{4,6},{5,7},{6,0},{7,1},{8,10},{9,11},{10,... | collective-permute-start | bytes 73736 | tf_op jit(solution)/shard_map/ppermute | solution.py:688

commit v3 on v2

--- a/solution.py
+++ b/solution.py
@@ -13,6 +13,7 @@
 YR = 24
 F32 = jnp.float32
 LIMIT = 30
+NEAR = ()
 EX, EY, EZ, HX, HY, HZ = range(6)
 
 
@@ -505,7 +506,7 @@
             put(msg2, 2 * k + i, jnp.where(ia == k // nb, own, joined))
 
 
-def k_y3(f, xr, q1, mx, ey1, ez1, hx1, ex1, elo, m, hb, tp, bp, ts, bs, msg2, part2, v2, vn2, ex2, hy1, q2, r):
+def k_y3(f, xr, q1, mx, ey1, ez1, hx1, ex1, elo, ex2, hy1, q2, r):
     n = y_size()
     gy = y_index()
     yon = jnp.where(gy < n - 1, 1.0, 0.0)
@@ -532,20 +533,32 @@
             put(hy1, x, t)
             put(ex2, x, 2.0 * plane(ex1, x) - fplane(f, EX, x) + (0.5 * ie) * bz(fplane(f, HY, x) - t))
             put(q2, x, plane(hx1, x) + 0.5 * fe)
+
+
+def k_y3_sweep(r, m, hb, msg2, v2, vn2):
     m_at = lambda j: plane(m, j, YR)
     last, vn = sweep(m_at, lambda j: r[pl.ds(j, YR, stride=PY), :], PY, v2, YR)
     vn2[...] = vn
     pf, plast = ends(last, vn, plane(hb, 0, YR), plane(hb, 2, YR))
     spread(msg2, 1, (pf, plast))
-    nc, ic = lax.axis_size("gc"), lax.axis_index("gc")
-    spread(part2, 1, shares(pf, plast, (tp, bp, ts, bs), nc, ic, YR, YR))
-
-
-def k_y4(msg, h, b, v2, vn2, hb, *more):
+
+
+def y_ends(msg):
+    return lambda j, k: msg[pl.ds((2 * j + k) * YR, YR), :]
+
+
+def k_join_ends(gi, tp, bp, ts, bs, msg, al, ga):
+    nc = lax.axis_size("gc")
+    zero = jnp.zeros((YR, PZ), F32)
+    spread(msg, 1, chain(y_ends(gi), nc, YR, YR, tp, bp, ts, bs, al, ga, zero, zero))
+
+
+def k_y4(gi, go, h, b, v2, vn2, hb, *more):
     coi, coo, (ex2, hy1, q2, out, al, ga, w2, dw) = more[:6], more[6:12], more[12:]
     nz, nc = lax.axis_size("gz"), lax.axis_size("gc")
     iz, ic = lax.axis_index("gz"), lax.axis_index("gc")
-    left, right = gathered(msg, nz, nc, iz, ic, YR, YR, coi, coo, al, ga)
+    left, right = interface(y_ends(go), nz, iz, YR, coo, al, ga)
+    left, right = interface(y_ends(gi), nc, ic, YR, coi, al, ga, left, right)
     lw = left * plane(hb, 1, YR)
     rw = (right - vn2[...]) * plane(hb, 0, YR)
     later = right
@@ -580,8 +593,8 @@
         later = w
 
 
-def call(name, parts, args, outs, scratch=(), smem=(), into=(), flush=(), near=()):
-    into, flush, scratch = dict(into), dict(flush), dict(scratch)
+def call(name, parts, args, outs, scratch=(), smem=(), into=(), flush=(), near=(), only=()):
+    into, flush, scratch, only = dict(into), dict(flush), dict(scratch), dict(only)
     moved = [k for k in args if k not in smem and (k not in near or k in into)]
     pieces = {k for group in flush.values() for k, _, _ in group}
     last = {k: max(i for i, (_, used) in enumerate(parts) if k in used) for k in outs}
@@ -602,14 +615,20 @@
         env.update({k: hbm[k] for k in args if k not in moved})
         sem_in, sem_out = next(take), next(take)
         pending = {}
-        for i, k in enumerate(moved):
-            where = env.get(k)
+        count = 0
+        for k in moved:
+            pairs = [(hbm[k], env.get(k))]
             if k in into:
                 buffer, row = into[k]
-                where = env[buffer].at[pl.ds(row(), args[k].shape[0]), :]
-            copy = pltpu.make_async_copy(hbm[k], where, sem_in.at[i])
-            copy.start()
-            pending.setdefault(into[k][0] if k in into else k, []).append(copy)
+                pairs = [(hbm[k], env[buffer].at[pl.ds(row(), args[k].shape[0]), :])]
+            elif k in only:
+                windows = [pl.ds(at, rows) for at, rows in only[k]]
+                pairs = [(hbm[k].at[w, :], env[k].at[w, :]) for w in windows]
+            for source, where in pairs:
+                copy = pltpu.make_async_copy(source, where, sem_in.at[count])
+                copy.start()
+                count += 1
+                pending.setdefault(into[k][0] if k in into else k, []).append(copy)
         sent = []
         for i, (function, used) in enumerate(parts):
             for k in used:
@@ -638,7 +657,7 @@
         + [pltpu.VMEM((c, PZ), F32) for k, c in outs.items() if k not in near]
         + [pltpu.VMEM((c, PZ), F32) for c in scratch.values()]
         + [
-            pltpu.SemaphoreType.DMA((len(moved),)),
+            pltpu.SemaphoreType.DMA((sum(len(only.get(k, (0,))) for k in moved),)),
             pltpu.SemaphoreType.DMA((max(1, sum(len(group) for group in leave)),)),
         ],
         compiler_params=pltpu.CompilerParams(vmem_limit_bytes=LIMIT * 1024 * 1024),
@@ -671,28 +690,6 @@
             return pl.multiple_of(lax.rem(lax.axis_index(axis) - step + n, n) * rows, 8)
 
         into[k] = (buffer, row)
-    return args, into
-
-
-def from_groups(own, share, buffer):
-    nz, nc = lax.axis_size("gz"), lax.axis_size("gc")
-    rows = own.shape[0]
-    args, into = {}, {}
-    for z in range(nz):
-        for c in range(nc):
-            k = buffer + str(z * nc + c)
-            route = [
-                (i * nc + j, (i + z) % nz * nc + (j + c) % nc) for i in range(nz) for j in range(nc)
-            ]
-            sent = share if z else own
-            args[k] = lax.ppermute(sent, ("gz", "gc"), route) if z or c else own
-
-            def row(z=z, c=c):
-                iz = lax.rem(lax.axis_index("gz") - z + nz, nz)
-                ic = lax.rem(lax.axis_index("gc") - c + nc, nc)
-                return pl.multiple_of((iz * nc + ic) * rows, 8)
-
-            into[k] = (buffer, row)
     return args, into
 
 
@@ -714,24 +711,34 @@
     linex = ("mx", "hx", "bx", "vx", "hbx")
     liney = ("my", "hy", "by", "vy", "hby")
     one = call(
-        "one",
+        "onex",
         [
             (k_eps, ("reg", "table", "eps")),
             (k_x1, ("f", "eps", "xl", "xr", "yl", "yr", "msgx", "q1") + linex + ("r",)),
-            (k_y1, ("f", "eps", "xl", "xr", "msgy", "p1", "ey1") + liney + ("rt", "ep")),
         ],
-        dict(reg=reg, f=f, xl=xl, xr=xr, yl=yl, yr=yr, table=eps_table),
+        dict(xl=xl, xr=xr, yl=yl, yr=yr, reg=reg, f=f, table=eps_table),
+        dict(zip(("eps", "q1") + linex + ("msgx",), (cells, cells, nxl, nxl, nxl, nxl, 4 * XR, nb * XB))),
+        dict(r=nxl),
+        smem=("table",),
+        near=("xl", "xr", "yl", "yr") + NEAR,
+        flush={0: [("eps", 0, cells)]},
+        only=dict(f=[(EX * cells, cells), (EZ * cells, 3 * cells)]),
+    )
+    oney = call(
+        "oney",
+        [(k_y1, ("f", "eps", "xl", "xr", "msgy", "p1", "ey1") + liney + ("rt", "ep"))],
+        dict(f=f, eps=one["eps"], xl=xl, xr=xr),
         dict(
             zip(
-                ("msgx", "q1") + linex + ("msgy", "p1", "ey1") + liney,
-                (nb * XB, cells, nxl, nxl, nxl, nxl, 4 * XR)
-                + (7 * YR, cells + PY, cells + PY, nyl, nyl, nyl, nyl, 4 * YR),
+                ("msgy", "p1", "ey1") + liney,
+                (7 * YR, cells + PY, cells + PY, nyl, nyl, nyl, nyl, 4 * YR),
             )
         ),
-        dict(eps=cells, r=nxl, rt=YR * PY, ep=YR * PY),
-        smem=("table",),
-        near=("xl", "xr", "yl", "yr", "msgy"),
+        dict(rt=YR * PY, ep=YR * PY),
+        near=("msgy",),
+        only=dict(f=[(EX * cells, 2 * cells), (HX * cells, 3 * cells)]),
     )
+    one.update(oney)
     pair, into = from_all(one["msgy"], "gc", "gyi")
     group = call(
         "group",
@@ -743,7 +750,7 @@
         dict(msgyo=YB, msgo=na * XB, inner=nb * XB),
         dict(gyi=nc * YB),
         into=into,
-        near=("gi", "msgyo") + tuple(pair),
+        near=("gi", "msgyo") + NEAR + tuple(pair),
     )
     goto = swap(group["msgo"], "ga")
     argy, into_o = from_all(group["msgyo"], "gz", "gyo")
@@ -767,21 +774,21 @@
             ),
             (
                 k_y3,
-                ("f", "xr", "q1", "mx", "ey1", "ez1", "hx1", "ex1", "elo", "my", "hby")
-                + cyi[:4] + ("msgy2", "party2", "vy2", "vny2", "ex2", "hy1", "q2", "rt"),
+                ("f", "xr", "q1", "mx", "ey1", "ez1", "hx1", "ex1", "elo", "ex2", "hy1", "q2", "rt"),
             ),
+            (k_y3_sweep, ("rt", "my", "hby", "msgy2", "vy2", "vny2")),
         ],
-        dict(argy, gi=group["inner"], go=goto, xr=xr, f=f, **keep),
+        dict(argy, **{k: keep[k] for k in ("hby", "vy", "by", "hy", "p1")}, gi=group["inner"], go=goto, f=f, xr=xr, **{k: keep[k] for k in linex + ("ey1", "q1", "my")}),
         dict(
             zip(
-                ("p2",) + cy + ("msgx2", "vx2", "vnx2") + cx + ("msgy2", "party2", "vy2", "vny2", "ex2", "hy1", "q2"),
+                ("p2",) + cy + ("msgx2", "vx2", "vnx2") + cx + ("msgy2", "vy2", "vny2", "ex2", "hy1", "q2"),
                 (cells + PY,)
                 + size(nc, YR)
                 + size(nz, YR)
                 + (na * nb * 2 * PY, cells, PY)
                 + size(nb, XR)
                 + size(na, XR)
-                + (2 * YR, 2 * YR, nyl, YR, cells, cells, cells),
+                + (2 * YR, nyl, YR, cells, cells, cells),
             )
         ),
         dict(
@@ -789,18 +796,32 @@
             ez1=nxl + XR, hx1=cells, alx=(max(na, nb) + 1) * XR, gax=(max(na, nb) + 1) * XR, r=cells, rt=YR * PY,
         ),
         into=into,
-        near=("go", "msgy2", "party2") + tuple(k for k in argy if k not in pair),
+        near=("go", "msgy2", "party2") + NEAR + tuple(k for k in argy if k not in pair),
+        flush={0: [("p2", 0, cells + PY)] + [(k, 0, c) for k, c in zip(cy, size(nc, YR) + size(nz, YR))]},
+        only=dict(f=[(EX * cells, cells), (EZ * cells, 3 * cells)]),
     )
     gotx = swap(two["msgx2"], along_x)
-    argy, into = from_groups(two["msgy2"], two["party2"], "gy")
-    need = {k: one[k] for k in ("hx", "bx", "hbx", "hy", "by", "hby")}
-    need.update({k: two[k] for k in ("p2",) + cy + cx + ("vx2", "vnx2", "vy2", "vny2", "ex2", "hy1", "q2")})
+    pair, into = from_all(two["msgy2"], "gc", "gyi")
+    group = call(
+        "ends",
+        [(k_join_ends, ("gyi",) + cyi[:4] + ("msg", "aly", "gay"))],
+        dict(pair, **{k: two[k] for k in cyi[:4]}),
+        dict(msg=2 * YR),
+        dict(gyi=nc * 2 * YR, aly=ey, gay=ey),
+        into=into,
+        near=tuple(pair) + ("msg",),
+    )
+    argy, into_o = from_all(group["msg"], "gz", "gyo")
+    argy.update(pair)
+    into.update(into_o)
+    order = cy + ("hby", "vny2", "vy2", "by", "hy", "ex2", "q2", "hy1") + cx + ("hbx", "vnx2", "vx2", "bx", "hx", "p2")
+    need = {k: two.get(k, one.get(k)) for k in order}
     three = call(
         "three",
         [
             (
                 k_y4,
-                ("gy", "hy", "by", "vy2", "vny2", "hby") + cy + ("ex2", "hy1", "q2", "out")
+                ("gyi", "gyo", "hy", "by", "vy2", "vny2", "hby") + cy + ("ex2", "hy1", "q2", "out")
                 + ("aly", "gay", "w2", "dw"),
             ),
             (k_x4, ("gx", "hx", "bx", "vx2", "vnx2", "hbx") + cx + ("p2", "out", "alx", "gax")),
@@ -808,7 +829,7 @@
         dict(argy, gx=gotx, **need),
         dict(out=6 * cells),
         dict(
-            gy=ny * 2 * YR, aly=ey, gay=ey, w2=YR * PY, dw=YR * PY,
+            gyi=nc * 2 * YR, gyo=nz * 2 * YR, aly=ey, gay=ey, w2=YR * PY, dw=YR * PY,
             alx=(max(na, nb) + 1) * PY, gax=(max(na, nb) + 1) * PY,
         ),
         into=into,

time: 72.8 us -> 68.9 us (0.946)
  starting transfers between devices: 33 us -> 28.3 us
  Pallas kernels: 19 us -> 20.5 us
    ppermute x7 -> x0, starting transfers between devices: 7.22 us -> none  [from_groups(): args[k] = lax.ppermute(sent, ('gz', 'gc'), route) if z or c else own]
    ppermute x8 -> x12, waiting for transfers between devices: 8.45 us -> 13.8 us  [ring(): return lax.ppermute(block, axis, [(i, (i + step) % n) for i in range(n)])]
    ppermute x7 -> x0, waiting for transfers between devices: 3.58 us -> none  [from_groups(): args[k] = lax.ppermute(sent, ('gz', 'gc'), route) if z or c else own]
    ppermute x8 -> x12, starting transfers between devices: 13.7 us -> 16.2 us  [ring(): return lax.ppermute(block, axis, [(i, (i + step) % n) for i in range(n)])]
    all_to_all x3, waiting for transfers between devices: 7.83 us -> 5.57 us  [swap(): got = lax.all_to_all(msg.reshape(n, -1, PZ), axis, 0, 0, tiled=True)]
    pallas_call x4 -> x6, Pallas kernels: 17.4 us -> 19 us  [call(): pl.pallas_call(body, out_shape=[(pltpu.VMEM if k in near else pltpu.HBM)(...]
  transfers between devices with their start and end apart: 18 -> 15, of which waited for: 8 -> 11; matrix products, arithmetic and copies ran while one was open for 0% -> 0% of each run, Pallas kernels for 0% -> 7%
where the time goes in v3:
time: 68.9 us; the launch traced here: 68.4 us
  starting transfers between devices  28.3 us (41%)
  Pallas kernels  20.5 us (30%)
  waiting for transfers between devices  19.3 us (28%)
    pallas_call x6, Pallas kernels, call(): pl.pallas_call(body, out_shape=[(pltpu.VMEM if k in near else pltpu.HBM)(...  19 us
    ppermute x12, starting transfers between devices, ring(): return lax.ppermute(block, axis, [(i, (i + step) % n) for i in range(n)])  16.2 us
    ppermute x12, waiting for transfers between devices, ring(): return lax.ppermute(block, axis, [(i, (i + step) % n) for i in range(n)])  13.8 us
    all_to_all x3, starting transfers between devices, swap(): got = lax.all_to_all(msg.reshape(n, -1, PZ), axis, 0, 0, tiled=True)  12.1 us
    all_to_all x3, waiting for transfers between devices, swap(): got = lax.all_to_all(msg.reshape(n, -1, PZ), axis, 0, 0, tiled=True)  5.57 us
    pallas_call x1, Pallas kernels, edges(): pl.pallas_call(k_edges, out_shape=[pltpu.VMEM((c, PZ), F32) for c in (5 *...  1.58 us
  transfers between devices with their start and end apart: 15, of which 11 were waited for; matrix products, arithmetic and copies ran while one was open for 0% of the time, Pallas kernels for 7%

profile of v3, /device:TPU:0, one launch (start us, length us, event | category | flops | bytes accessed | tf_op | source)
XLA Modules:
  0.0 68.4 jit_solution(18321360960548056751)
XLA Ops:
  0.0 0.0 copy-start.4
  0.0 1.6 %edges.1 = (f32[160,128]{1,0:T(8,128)S(1)}, f32[160,128]{1,0:T(8,128)S(1)}, f32[96,128]{1,0:T(8,128)S(1)}, f32[96,128]{1,0:T(8,128)S(1)}) custom-call(f32[6,16,32,128]{3,2,1,0:T(8,128)} %f.1, s32[16,32,128]{2,1,0:T(8,128)} %reg.1, f32[16]{0:T(128)} %refs_6_.1), custom_call_target="tpu_custom_call" | custom-call | flops 1000 | bytes 1000 | tf_op jit(solution)/shard_map/edges/pallas_call | solution.py:125
  1.6 1.7 %collective-permute-start = (f32[160,128]{1,0:T(8,128)S(1)}, f32[160,128]{1,0:T(8,128)S(1)}, u32[]{:S(2)}, u32[]{:S(2)}) collective-permute-start(f32[160,128]{1,0:T(8,128)S(1)} %get-tuple-element.62), channel_id=1, source_target_pairs={{0,8},{8,16},{16,24},{24,32},{32,40},{40,48},{48,56},{56,64},{64,7... | collective-permute-start | bytes 245768 | tf_op jit(solution)/shard_map/ppermute | solution.py:672
  3.3 3.7 %collective-permute-start.1 = (f32[160,128]{1,0:T(8,128)S(1)}, f32[160,128]{1,0:T(8,128)S(1)}, u32[]{:S(2)}, u32[]{:S(2)}) collective-permute-start(f32[160,128]{1,0:T(8,128)S(1)} %get-tuple-element.63), channel_id=1, source_target_pairs={{0,120},{8,0},{16,8},{24,16},{32,24},{40,32},{48,40},{56,48},{64,5... | collective-permute-start | bytes 245768 | tf_op jit(solution)/shard_map/ppermute | solution.py:672
  7.0 0.0 collective-permute-start.2
  7.0 3.2 %collective-permute-start.3 = (f32[96,128]{1,0:T(8,128)S(1)}, f32[96,128]{1,0:T(8,128)S(1)}, u32[]{:S(2)}, u32[]{:S(2)}) collective-permute-start(f32[96,128]{1,0:T(8,128)S(1)} %get-tuple-element.65), channel_id=1, source_target_pairs={{0,7},{1,0},{2,1},{3,2},{4,3},{5,4},{6,5},{7,6},{8,15},{9,8},{10,9... | collective-permute-start | bytes 147464 | tf_op jit(solution)/shard_map/ppermute | solution.py:672
  10.2 1.8 %collective-permute-done.2.refs_2_ = f32[96,128]{1,0:T(8,128)S(1)} collective-permute-done((f32[96,128]{1,0:T(8,128)S(1)}, f32[96,128]{1,0:T(8,128)S(1)}, u32[]{:S(2)}, u32[]{:S(2)}) %collective-permute-start.2) | collective-permute-done | bytes 49184 | tf_op jit(solution)/shard_map/ppermute | solution.py:672
  12.0 0.0 collective-permute-done.3.refs_3_
  12.0 0.0 collective-permute-done.refs_0_.refs_2_
  12.0 0.0 copy-start.3
  12.0 0.0 collective-permute-done.1.refs_1_.refs_3_.refs_14_
  12.0 0.0 copy-start
  12.0 0.0 copy-done.4
  12.0 3.5 %onex.1 = (f32[512,128]{1,0:T(8,128)}, f32[512,128]{1,0:T(8,128)}, f32[640,128]{1,0:T(8,128)}, f32[640,128]{1,0:T(8,128)}, f32[640,128]{1,0:T(8,128)}, /*index=5...) custom-call(f32[160,128]{1,0:T(8,128)S(1)} %collective-permute-done.refs_0_.refs_2_, ...), custom_call_target="tpu_custom_call" | custom-call | flops 1000 | bytes 1000 | tf_op jit(solution)/shard_map/onex/pallas_call | solution.py:651
  15.6 3.5 %all-to-all-start = ((f32[4,208,128]{2,1,0:T(8,128)}), f32[4,208,128]{2,1,0:T(8,128)S(1)}, u32[]{:S(2)}, u32[]{:S(2)}) async-start(f32[4,208,128]{2,1,0:T(8,128)} %bitcast.17), calls=%async_computation | async-start | bytes 851968 | tf_op jit(solution)/shard_map/all_to_all | solution.py:677
  19.0 0.0 copy-done.3
  19.1 0.0 copy-done
  19.1 3.6 %oney.1 = (f32[168,128]{1,0:T(8,128)S(1)}, f32[544,128]{1,0:T(8,128)}, f32[544,128]{1,0:T(8,128)}, f32[768,128]{1,0:T(8,128)}, f32[768,128]{1,0:T(8,128)}, /*ind...) custom-call(f32[3072,128]{1,0:T(8,128)} %bitcast.13, f32[512,128]{1,0:T(8,128)} %get-tuple-element.66.refs_1_, ...), custom_call_target="tpu_custom_call" | custom-call | flops 1000 | bytes 1000 | tf_op jit(solution)/shard_map/oney/pallas_call | solution.py:651
  22.6 0.0 copy-start.1
  22.6 0.7 %collective-permute-start.4 = (f32[168,128]{1,0:T(8,128)S(1)}, f32[168,128]{1,0:T(8,128)S(1)}, u32[]{:S(2)}, u32[]{:S(2)}) collective-permute-start(f32[168,128]{1,0:T(8,128)S(1)} %get-tuple-element.67.refs_0_.refs_4_), channel_id=1, source_target_pairs={{0,1},{1,0},{2,3},{3,2},{4,5},{5,4},{6,7},{7,6},{8,9},{9,8},{10,11... | collective-permute-start | bytes 258056 | tf_op jit(solution)/shard_map/ppermute | solution.py:672
  23.3 0.9 %collective-permute-done.4.refs_1_.refs_5_ = f32[168,128]{1,0:T(8,128)S(1)} collective-permute-done((f32[168,128]{1,0:T(8,128)S(1)}, f32[168,128]{1,0:T(8,128)S(1)}, u32[]{:S(2)}, u32[]{:S(2)}) %collective-permute-start.4) | collective-permute-done | bytes 86048 | tf_op jit(solution)/shard_map/ppermute | solution.py:672
  24.3 0.0 copy-start.2
  24.3 4.2 %all-to-all-done = f32[4,208,128]{2,1,0:T(8,128)S(1)} async-done(((f32[4,208,128]{2,1,0:T(8,128)}), f32[4,208,128]{2,1,0:T(8,128)S(1)}, u32[]{:S(2)}, u32[]{:S(2)}) %all-to-all-start) | async-done | bytes 426016 | tf_op jit(solution)/shard_map/all_to_all | solution.py:677
  28.5 1.2 %group.1 = (f32[168,128]{1,0:T(8,128)S(1)}, f32[832,128]{1,0:T(8,128)}, f32[832,128]{1,0:T(8,128)}) custom-call(f32[168,128]{1,0:T(8,128)S(1)} %get-tuple-element.67.refs_0_.refs_4_, f32[168,128]{1,0:T(8,128)S(1)} %collective-permute-done.4.refs_1_.refs_5_, f32[832,128]{1,0:T(8,128)S(1)} %bitcast.10), custom_call_target="tpu_custom_call" | custom-call | flops 1000 | bytes 1000 | tf_op jit(solution)/shard_map/group/pallas_call | solution.py:651
  29.7 3.5 %all-to-all-start.1 = ((f32[4,208,128]{2,1,0:T(8,128)}), f32[4,208,128]{2,1,0:T(8,128)S(1)}, u32[]{:S(2)}, u32[]{:S(2)}) async-start(f32[4,208,128]{2,1,0:T(8,128)} %bitcast.18), calls=%async_computation.1 | async-start | bytes 851968 | tf_op jit(solution)/shard_map/all_to_all | solution.py:677
  33.2 2.8 %collective-permute-start.7 = (f32[168,128]{1,0:T(8,128)S(1)}, f32[168,128]{1,0:T(8,128)S(1)}, u32[]{:S(2)}, u32[]{:S(2)}) collective-permute-start(f32[168,128]{1,0:T(8,128)S(1)} %get-tuple-element.69.refs_0_), channel_id=1, source_target_pairs={{0,6},{2,0},{4,2},{6,4},{1,7},{3,1},{5,3},{7,5},{8,14},{10,8},{12,... | collective-permute-start | bytes 258056 | tf_op jit(solution)/shard_map/ppermute | solution.py:672
  36.0 0.5 collective-permute-start.6
  36.5 1.0 %collective-permute-start.5 = (f32[168,128]{1,0:T(8,128)S(1)}, f32[168,128]{1,0:T(8,128)S(1)}, u32[]{:S(2)}, u32[]{:S(2)}) collective-permute-start(f32[168,128]{1,0:T(8,128)S(1)} %get-tuple-element.69.refs_0_), channel_id=1, source_target_pairs={{0,2},{2,4},{4,6},{6,0},{1,3},{3,5},{5,7},{7,1},{8,10},{10,12},{12... | collective-permute-start | bytes 258056 | tf_op jit(solution)/shard_map/ppermute | solution.py:672
  37.6 2.1 %collective-permute-done.7.refs_3_ = f32[168,128]{1,0:T(8,128)S(1)} collective-permute-done((f32[168,128]{1,0:T(8,128)S(1)}, f32[168,128]{1,0:T(8,128)S(1)}, u32[]{:S(2)}, u32[]{:S(2)}) %collective-permute-start.7) | collective-permute-done | bytes 86048 | tf_op jit(solution)/shard_map/ppermute | solution.py:672
  39.7 2.8 %collective-permute-done.6.refs_2_ = f32[168,128]{1,0:T(8,128)S(1)} collective-permute-done((f32[168,128]{1,0:T(8,128)S(1)}, f32[168,128]{1,0:T(8,128)S(1)}, u32[]{:S(2)}, u32[]{:S(2)}) %collective-permute-start.6) | collective-permute-done | bytes 86048 | tf_op jit(solution)/shard_map/ppermute | solution.py:672
  42.5 0.8 %collective-permute-done.5.refs_1_ = f32[168,128]{1,0:T(8,128)S(1)} collective-permute-done((f32[168,128]{1,0:T(8,128)S(1)}, f32[168,128]{1,0:T(8,128)S(1)}, u32[]{:S(2)}, u32[]{:S(2)}) %collective-permute-start.5) | collective-permute-done | bytes 86048 | tf_op jit(solution)/shard_map/ppermute | solution.py:672
  43.3 0.0 all-to-all-done.1
  43.3 0.0 copy-done.1
  43.3 0.0 copy-done.2
  43.3 5.7 %two.1 = (f32[544,128]{1,0:T(8,128)}, f32[48,128]{1,0:T(8,128)}, f32[48,128]{1,0:T(8,128)}, f32[48,128]{1,0:T(8,128)}, f32[48,128]{1,0:T(8,128)}, /*index=5*/f32...) custom-call(f32[168,128]{1,0:T(8,128)S(1)} %get-tuple-element.69.ref, ...), custom_call_target="tpu_custom_call" | custom-call | flops 1000 | bytes 1000 | tf_op jit(solution)/shard_map/two/pallas_call | solution.py:651
  49.1 5.2 %all-to-all-start.2 = ((f32[16,64,128]{2,1,0:T(8,128)}), f32[16,64,128]{2,1,0:T(8,128)S(1)}, u32[]{:S(2)}, u32[]{:S(2)}) async-start(f32[16,64,128]{2,1,0:T(8,128)} %bitcast.16), calls=%async_computation.2 | async-start | bytes 1048576 | tf_op jit(solution)/shard_map/all_to_all | solution.py:677
  54.2 0.1 collective-permute-start.8
  54.3 1.2 %collective-permute-done.8.refs_1_.refs_5_ = f32[48,128]{1,0:T(8,128)S(1)} collective-permute-done((f32[48,128]{1,0:T(8,128)S(1)}, f32[48,128]{1,0:T(8,128)S(1)}, u32[]{:S(2)}, u32[]{:S(2)}) %collective-permute-start.8) | collective-permute-done | bytes 24608 | tf_op jit(solution)/shard_map/ppermute | solution.py:672
  55.5 0.9 %ends.1.refs_0_ = f32[48,128]{1,0:T(8,128)S(1)} custom-call(f32[48,128]{1,0:T(8,128)S(1)} %get-tuple-element.85.refs_0_.refs_4_, f32[48,128]{1,0:T(8,128)S(1)} %collective-permute-done.8.refs_1_.refs_5_, f32[48,128]{1,0:T(8,128)} %get-tuple-element.86.refs_2_.refs_7_, f32[48,128]{1,0:T(8,128)} %get-tuple-element.87.refs_3_.refs_8_, ...), custom_call_target="tpu_custom_call" | custom-call | flops 1000 | bytes 1000 | tf_op jit(solution)/shard_map/ends/pallas_call | solution.py:651
  56.4 0.6 collective-permute-start.11
  57.1 0.6 collective-permute-start.10
  57.7 1.2 %collective-permute-start.9 = (f32[48,128]{1,0:T(8,128)S(1)}, f32[48,128]{1,0:T(8,128)S(1)}, u32[]{:S(2)}, u32[]{:S(2)}) collective-permute-start(f32[48,128]{1,0:T(8,128)S(1)} %ends.1.refs_0_), channel_id=1, source_target_pairs={{0,2},{2,4},{4,6},{6,0},{1,3},{3,5},{5,7},{7,1},{8,10},{10,12},{12... | collective-permute-start | bytes 73736 | tf_op jit(solution)/shard_map/ppermute | solution.py:672
  58.9 1.5 %collective-permute-done.11.refs_3_ = f32[48,128]{1,0:T(8,128)S(1)} collective-permute-done((f32[48,128]{1,0:T(8,128)S(1)}, f32[48,128]{1,0:T(8,128)S(1)}, u32[]{:S(2)}, u32[]{:S(2)}) %collective-permute-start.11) | collective-permute-done | bytes 24608 | tf_op jit(solution)/shard_map/ppermute | solution.py:672
  60.3 2.1 %collective-permute-done.10.refs_2_ = f32[48,128]{1,0:T(8,128)S(1)} collective-permute-done((f32[48,128]{1,0:T(8,128)S(1)}, f32[48,128]{1,0:T(8,128)S(1)}, u32[]{:S(2)}, u32[]{:S(2)}) %collective-permute-start.10) | collective-permute-done | bytes 24608 | tf_op jit(solution)/shard_map/ppermute | solution.py:672
  62.4 0.6 collective-permute-done.9.refs_1_
  63.0 1.3 %all-to-all-done.2 = f32[16,64,128]{2,1,0:T(8,128)S(1)} async-done(((f32[16,64,128]{2,1,0:T(8,128)}), f32[16,64,128]{2,1,0:T(8,128)S(1)}, u32[]{:S(2)}, u32[]{:S(2)}) %all-to-all-start.2) | async-done | bytes 524320 | tf_op jit(solution)/shard_map/all_to_all | solution.py:677
  64.3 4.1 %three.1 = f32[3072,128]{1,0:T(8,128)} custom-call(f32[48,128]{1,0:T(8,128)S(1)} %ends.1.refs_0_, f32[48,128]{1,0:T(8,128)S(1)} %collective-permute-done.9.refs_1_, f32[48,128]{1,0:T(8,128)S(1)} %collective-permute-done.10.refs_2_, f32[48,128]{1,0:T(8,128)S(1)} %collective-permute-done.11.refs_3_, f32[48,128]{1,0:T(8,128)S(1)} %get-tuple-element.85.refs_0_.refs_4_, ...), custom_call_target="tpu_custom_call" | custom-call | flops 1000 | bytes 1000 | tf_op jit(solution)/shard_map/three/pallas_call | solution.py:651
Async XLA Ops:
  0.0 12.0 %copy-start.4 = (f32[16]{0:T(128)S(1)}, f32[16]{0:T(128)}, u32[]{:S(2)}) copy-start(f32[16]{0:T(128)} %refs_6_.1) | copy-start | bytes 196
  1.6 10.4 %collective-permute-start = (f32[160,128]{1,0:T(8,128)S(1)}, f32[160,128]{1,0:T(8,128)S(1)}, u32[]{:S(2)}, u32[]{:S(2)}) collective-permute-start(f32[160,128]{1,0:T(8,128)S(1)} %get-tuple-element.62), channel_id=1, source_target_pairs={{0,8},{8,16},{16,24},{24,32},{32,40},{40,48},{48,56},{56,64},{64,7... | collective-permute-start | bytes 245768 | tf_op jit(solution)/shard_map/ppermute | solution.py:672
  3.3 8.7 %collective-permute-start.1 = (f32[160,128]{1,0:T(8,128)S(1)}, f32[160,128]{1,0:T(8,128)S(1)}, u32[]{:S(2)}, u32[]{:S(2)}) collective-permute-start(f32[160,128]{1,0:T(8,128)S(1)} %get-tuple-element.63), channel_id=1, source_target_pairs={{0,120},{8,0},{16,8},{24,16},{32,24},{40,32},{48,40},{56,48},{64,5... | collective-permute-start | bytes 245768 | tf_op jit(solution)/shard_map/ppermute | solution.py:672
  7.0 5.0 %collective-permute-start.2 = (f32[96,128]{1,0:T(8,128)S(1)}, f32[96,128]{1,0:T(8,128)S(1)}, u32[]{:S(2)}, u32[]{:S(2)}) collective-permute-start(f32[96,128]{1,0:T(8,128)S(1)} %get-tuple-element.64), channel_id=1, source_target_pairs={{0,1},{1,2},{2,3},{3,4},{4,5},{5,6},{6,7},{7,0},{8,9},{9,10},{10,1... | collective-permute-start | bytes 147464 | tf_op jit(solution)/shard_map/ppermute | solution.py:672
  7.0 5.0 %collective-permute-start.3 = (f32[96,128]{1,0:T(8,128)S(1)}, f32[96,128]{1,0:T(8,128)S(1)}, u32[]{:S(2)}, u32[]{:S(2)}) collective-permute-start(f32[96,128]{1,0:T(8,128)S(1)} %get-tuple-element.65), channel_id=1, source_target_pairs={{0,7},{1,0},{2,1},{3,2},{4,3},{5,4},{6,5},{7,6},{8,15},{9,8},{10,9... | collective-permute-start | bytes 147464 | tf_op jit(solution)/shard_map/ppermute | solution.py:672
  12.0 7.0 %copy-start.3 = (f32[160,128]{1,0:T(8,128)}, f32[160,128]{1,0:T(8,128)S(1)}, u32[]{:S(2)}) copy-start(f32[160,128]{1,0:T(8,128)S(1)} %collective-permute-done.refs_0_.refs_2_) | copy-start | bytes 245764
  12.0 7.0 %copy-start = (f32[160,128]{1,0:T(8,128)}, f32[160,128]{1,0:T(8,128)S(1)}, u32[]{:S(2)}) copy-start(f32[160,128]{1,0:T(8,128)S(1)} %collective-permute-done.1.refs_1_.refs_3_.refs_14_) | copy-start | bytes 245764
  15.6 12.9 %all-to-all-start = ((f32[4,208,128]{2,1,0:T(8,128)}), f32[4,208,128]{2,1,0:T(8,128)S(1)}, u32[]{:S(2)}, u32[]{:S(2)}) async-start(f32[4,208,128]{2,1,0:T(8,128)} %bitcast.17), calls=%async_computation | async-start | bytes 851968 | tf_op jit(solution)/shard_map/all_to_all | solution.py:677
  22.6 20.7 %copy-start.1 = (f32[168,128]{1,0:T(8,128)}, f32[168,128]{1,0:T(8,128)S(1)}, u32[]{:S(2)}) copy-start(f32[168,128]{1,0:T(8,128)S(1)} %get-tuple-element.67.refs_0_.refs_4_) | copy-start | bytes 258052
  22.6 1.6 %collective-permute-start.4 = (f32[168,128]{1,0:T(8,128)S(1)}, f32[168,128]{1,0:T(8,128)S(1)}, u32[]{:S(2)}, u32[]{:S(2)}) collective-permute-start(f32[168,128]{1,0:T(8,128)S(1)} %get-tuple-element.67.refs_0_.refs_4_), channel_id=1, source_target_pairs={{0,1},{1,0},{2,3},{3,2},{4,5},{5,4},{6,7},{7,6},{8,9},{9,8},{10,11... | collective-permute-start | bytes 258056 | tf_op jit(solution)/shard_map/ppermute | solution.py:672
  24.3 19.0 %copy-start.2 = (f32[168,128]{1,0:T(8,128)}, f32[168,128]{1,0:T(8,128)S(1)}, u32[]{:S(2)}) copy-start(f32[168,128]{1,0:T(8,128)S(1)} %collective-permute-done.4.refs_1_.refs_5_) | copy-start | bytes 258052
  29.7 13.6 %all-to-all-start.1 = ((f32[4,208,128]{2,1,0:T(8,128)}), f32[4,208,128]{2,1,0:T(8,128)S(1)}, u32[]{:S(2)}, u32[]{:S(2)}) async-start(f32[4,208,128]{2,1,0:T(8,128)} %bitcast.18), calls=%async_computation.1 | async-start | bytes 851968 | tf_op jit(solution)/shard_map/all_to_all | solution.py:677
  33.2 6.5 %collective-permute-start.7 = (f32[168,128]{1,0:T(8,128)S(1)}, f32[168,128]{1,0:T(8,128)S(1)}, u32[]{:S(2)}, u32[]{:S(2)}) collective-permute-start(f32[168,128]{1,0:T(8,128)S(1)} %get-tuple-element.69.refs_0_), channel_id=1, source_target_pairs={{0,6},{2,0},{4,2},{6,4},{1,7},{3,1},{5,3},{7,5},{8,14},{10,8},{12,... | collective-permute-start | bytes 258056 | tf_op jit(solution)/shard_map/ppermute | solution.py:672
  36.0 6.5 %collective-permute-start.6 = (f32[168,128]{1,0:T(8,128)S(1)}, f32[168,128]{1,0:T(8,128)S(1)}, u32[]{:S(2)}, u32[]{:S(2)}) collective-permute-start(f32[168,128]{1,0:T(8,128)S(1)} %get-tuple-element.69.refs_0_), channel_id=1, source_target_pairs={{0,4},{2,6},{4,0},{6,2},{1,5},{3,7},{5,1},{7,3},{8,12},{10,14},{12... | collective-permute-start | bytes 258056 | tf_op jit(solution)/shard_map/ppermute | solution.py:672
  36.5 6.8 %collective-permute-start.5 = (f32[168,128]{1,0:T(8,128)S(1)}, f32[168,128]{1,0:T(8,128)S(1)}, u32[]{:S(2)}, u32[]{:S(2)}) collective-permute-start(f32[168,128]{1,0:T(8,128)S(1)} %get-tuple-element.69.refs_0_), channel_id=1, source_target_pairs={{0,2},{2,4},{4,6},{6,0},{1,3},{3,5},{5,7},{7,1},{8,10},{10,12},{12... | collective-permute-start | bytes 258056 | tf_op jit(solution)/shard_map/ppermute | solution.py:672
  49.1 15.3 %all-to-all-start.2 = ((f32[16,64,128]{2,1,0:T(8,128)}), f32[16,64,128]{2,1,0:T(8,128)S(1)}, u32[]{:S(2)}, u32[]{:S(2)}) async-start(f32[16,64,128]{2,1,0:T(8,128)} %bitcast.16), calls=%async_computation.2 | async-start | bytes 1048576 | tf_op jit(solution)/shard_map/all_to_all | solution.py:677
  54.2 1.3 %collective-permute-start.8 = (f32[48,128]{1,0:T(8,128)S(1)}, f32[48,128]{1,0:T(8,128)S(1)}, u32[]{:S(2)}, u32[]{:S(2)}) collective-permute-start(f32[48,128]{1,0:T(8,128)S(1)} %get-tuple-element.85.refs_0_.refs_4_), channel_id=1, source_target_pairs={{0,1},{1,0},{2,3},{3,2},{4,5},{5,4},{6,7},{7,6},{8,9},{9,8},{10,11... | collective-permute-start | bytes 73736 | tf_op jit(solution)/shard_map/ppermute | solution.py:672
  56.4 3.9 %collective-permute-start.11 = (f32[48,128]{1,0:T(8,128)S(1)}, f32[48,128]{1,0:T(8,128)S(1)}, u32[]{:S(2)}, u32[]{:S(2)}) collective-permute-start(f32[48,128]{1,0:T(8,128)S(1)} %ends.1.refs_0_), channel_id=1, source_target_pairs={{0,6},{2,0},{4,2},{6,4},{1,7},{3,1},{5,3},{7,5},{8,14},{10,8},{12,... | collective-permute-start | bytes 73736 | tf_op jit(solution)/shard_map/ppermute | solution.py:672
  57.1 5.3 %collective-permute-start.10 = (f32[48,128]{1,0:T(8,128)S(1)}, f32[48,128]{1,0:T(8,128)S(1)}, u32[]{:S(2)}, u32[]{:S(2)}) collective-permute-start(f32[48,128]{1,0:T(8,128)S(1)} %ends.1.refs_0_), channel_id=1, source_target_pairs={{0,4},{2,6},{4,0},{6,2},{1,5},{3,7},{5,1},{7,3},{8,12},{10,14},{12... | collective-permute-start | bytes 73736 | tf_op jit(solution)/shard_map/ppermute | solution.py:672
  57.7 5.3 %collective-permute-start.9 = (f32[48,128]{1,0:T(8,128)S(1)}, f32[48,128]{1,0:T(8,128)S(1)}, u32[]{:S(2)}, u32[]{:S(2)}) collective-permute-start(f32[48,128]{1,0:T(8,128)S(1)} %ends.1.refs_0_), channel_id=1, source_target_pairs={{0,2},{2,4},{4,6},{6,0},{1,3},{3,5},{5,7},{7,1},{8,10},{10,12},{12... | collective-permute-start | bytes 73736 | tf_op jit(solution)/shard_map/ppermute | solution.py:672

commit v4 on v3

--- a/solution.py
+++ b/solution.py
@@ -9,12 +9,14 @@
 from jax.sharding import PartitionSpec as P
 
 PX, PY, PZ = 16, 32, 128
+XL, YL = PY + 2, PX + 2
 XR = 40
 YR = 24
 F32 = jnp.float32
 LIMIT = 30
 NEAR = ()
 EX, EY, EZ, HX, HY, HZ = range(6)
+XB, YB = 5 * XL + 6, 7 * YL + 2
 
 
 def x_index():
@@ -83,6 +85,12 @@
         on = (region & (1 << bit)) != 0
         level = [jnp.where(on, level[2 * i + 1], level[2 * i]) for i in range(len(level) // 2)]
     return level[0]
+
+
+def packed(values, lines, more, rows):
+    parts = [v[:lines] for v in values] + list(more)
+    pad = rows - sum(v.shape[0] for v in parts)
+    return (jnp.concatenate(parts + [jnp.zeros((pad, PZ), F32)], 0),)
 
 
 def k_eps(reg, table, eps):
@@ -227,9 +235,8 @@
     put(hb, 1, bn, XR)
     put(hb, 2, c, XR)
     put(hb, 3, vn, XR)
-    zq = jnp.zeros((6, PZ), F32)
-    qq = jnp.concatenate([q1lo[PX - 1 :], q1hi[PX - 1 :], zq], 0) * (-1.0 / 32.0)
-    spread(msg, lax.axis_size("gb"), (pf, plast, a, bb, c, qq))
+    qq = jnp.concatenate([q1lo[PX - 1 :], q1hi[PX - 1 :]], 0) * (-1.0 / 32.0)
+    spread(msg, lax.axis_size("gb"), packed((pf, plast, a, bb, c), XL, (qq,), XB))
 
 
 def k_y1(f, eps, xl, xr, msg, p1, ey1, m, h, b, v, hb, r, ep):
@@ -292,7 +299,7 @@
     qq = jnp.concatenate([lastrow(p1, 0, PX), lastrow(p1, PX, 1), tail], 0) * (-1.0 / 32.0)
     tail = jnp.zeros((6, PZ), F32)
     ee = fz(jnp.concatenate([lastrow(ey1, 0, PX), zero, lastrow(ey1, PX, 1), tail], 0))
-    spread(msg, 1, (pf, plast, a, bb, c, qq, ee))
+    spread(msg, 1, packed((pf, plast, a, bb, c, qq, ee), YL, (), YB))
 
 
 def coefficients(part, n, rows, tp, bp, ts, bs, bet, dele):
@@ -350,21 +357,22 @@
     return left, right
 
 
-XB = 5 * XR + 8
-
-
 def x_raw(msg):
-    return lambda j, k: msg[pl.ds(j * XB + k * XR, XR), :]
+    return lambda j, k: msg[pl.ds(j * XB + k * XL, XR), :]
+
+
+def x_late(msg, at):
+    return pltpu.roll(msg[pl.ds(at + XB - 8, 8), :], 6, 0)
 
 
 def x_part(msg):
     def part(j, k):
         if j == 0:
             return x_raw(msg)(j, k)
-        own = msg[pl.ds(j * XB + k * XR, PY), :]
+        own = msg[pl.ds(j * XB + k * XL, PY), :]
         more = (
-            msg[pl.ds(j * XB + k * XR + PY, 8), :]
-            + msg[pl.ds(j * XB + (2 + k) * XR + PY, 8), :] * msg[pl.ds((j - 1) * XB + 5 * XR, 8), :]
+            msg[pl.ds(j * XB + k * XL + PY, 8), :]
+            + msg[pl.ds(j * XB + (2 + k) * XL + PY, 8), :] * x_late(msg, (j - 1) * XB)
         )
         return jnp.concatenate([own, more], 0)
 
@@ -373,14 +381,11 @@
 
 def x_passed(msg, me):
     prev = pl.multiple_of(jnp.maximum(me - 1, 0) * XB, 8)
-    return jnp.where(me > 0, msg[pl.ds(prev + 5 * XR, 8), :], 0.0)
-
-
-YB = 7 * YR
+    return jnp.where(me > 0, x_late(msg, prev), 0.0)
 
 
 def y_raw(msg):
-    return lambda j, k: msg[pl.ds(j * YB + k * YR, YR), :]
+    return lambda j, k: msg[pl.ds(j * YB + k * YL, YR), :]
 
 
 def y_part(msg):
@@ -389,8 +394,9 @@
 
 
 def y_passed(msg, me, k):
-    prev = pl.multiple_of(jnp.maximum(me - 1, 0) * YB, 8)
-    return jnp.where(me > 0, msg[pl.ds(prev + k * YR, YR), :], 0.0)
+    skip = k * YL % 8
+    prev = pl.multiple_of(jnp.maximum(me - 1, 0) * YB + k * YL - skip, 8)
+    return jnp.where(me > 0, pltpu.roll(msg[pl.ds(prev, YR), :], YR - skip, 0), 0.0)
 
 
 def k_y2(gi, go, p1, h, b, v, hb, ex1, p2, elo, *more):
@@ -432,14 +438,16 @@
 def k_join_y(gi, msg):
     nc = lax.axis_size("gc")
     raw = y_raw(gi)
-    spread(msg, 1, join(y_part(gi), raw, nc) + (raw(nc - 1, 5), raw(nc - 1, 6)))
+    values = join(y_part(gi), raw, nc)
+    more = gi[pl.ds((nc - 1) * YB + 5 * YL, 2 * YL), :]
+    spread(msg, 1, packed(values, YL, (more,), YB))
 
 
 def k_join_x(gi, msg, inner):
     inner[...] = gi[...]
     nb = lax.axis_size("gb")
-    last = gi[pl.ds((nb - 1) * XB + 5 * XR, 8), :]
-    spread(msg, lax.axis_size("ga"), join(x_part(gi), x_raw(gi), nb) + (last,))
+    last = x_late(gi, (nb - 1) * XB)[:2]
+    spread(msg, lax.axis_size("ga"), packed(join(x_part(gi), x_raw(gi), nb), XL, (last,), XB))
 
 
 def shares(pf, ph, coefs, count, me, rows, crows):
@@ -731,7 +739,7 @@
         dict(
             zip(
                 ("msgy", "p1", "ey1") + liney,
-                (7 * YR, cells + PY, cells + PY, nyl, nyl, nyl, nyl, 4 * YR),
+                (YB, cells + PY, cells + PY, nyl, nyl, nyl, nyl, 4 * YR),
             )
         ),
         dict(rt=YR * PY, ep=YR * PY),

time: 68.9 us -> 67.3 us (0.977)
  waiting for transfers between devices: 19.3 us -> 17.6 us
  starting transfers between devices: 28.3 us -> 29 us
    ppermute x12, waiting for transfers between devices: 13.8 us -> 12.6 us  [ring(): return lax.ppermute(block, axis, [(i, (i + step) % n) for i in range(n)])]
  transfers between devices with their start and end apart: 15 -> 15, of which waited for: 11 -> 11; matrix products, arithmetic and copies ran while one was open for 0% -> 0% of each run, Pallas kernels for 7% -> 6%
where the time goes in v4:
time: 67.3 us; the launch traced here: 66.8 us
  starting transfers between devices  29 us (43%)
  Pallas kernels  20.1 us (30%)
  waiting for transfers between devices  17.6 us (26%)
    pallas_call x6, Pallas kernels, call(): pl.pallas_call(body, out_shape=[(pltpu.VMEM if k in near else pltpu.HBM)(...  18.5 us
    ppermute x12, starting transfers between devices, ring(): return lax.ppermute(block, axis, [(i, (i + step) % n) for i in range(n)])  16.6 us
    ppermute x12, waiting for transfers between devices, ring(): return lax.ppermute(block, axis, [(i, (i + step) % n) for i in range(n)])  12.6 us
    all_to_all x3, starting transfers between devices, swap(): got = lax.all_to_all(msg.reshape(n, -1, PZ), axis, 0, 0, tiled=True)  12.4 us
    all_to_all x3, waiting for transfers between devices, swap(): got = lax.all_to_all(msg.reshape(n, -1, PZ), axis, 0, 0, tiled=True)  4.97 us
    pallas_call x1, Pallas kernels, edges(): pl.pallas_call(k_edges, out_shape=[pltpu.VMEM((c, PZ), F32) for c in (5 *...  1.58 us
  transfers between devices with their start and end apart: 15, of which 11 were waited for; matrix products, arithmetic and copies ran while one was open for 0% of the time, Pallas kernels for 6%

profile of v4, /device:TPU:0, one launch (start us, length us, event | category | flops | bytes accessed | tf_op | source)
XLA Modules:
  0.0 66.8 jit_solution(11683237579611570310)
XLA Ops:
  0.0 0.0 copy-start.4
  0.0 1.6 %edges.1 = (f32[160,128]{1,0:T(8,128)S(1)}, f32[160,128]{1,0:T(8,128)S(1)}, f32[96,128]{1,0:T(8,128)S(1)}, f32[96,128]{1,0:T(8,128)S(1)}) custom-call(f32[6,16,32,128]{3,2,1,0:T(8,128)} %f.1, s32[16,32,128]{2,1,0:T(8,128)} %reg.1, f32[16]{0:T(128)} %refs_6_.1), custom_call_target="tpu_custom_call" | custom-call | flops 1000 | bytes 1000 | tf_op jit(solution)/shard_map/edges/pallas_call | solution.py:133
  1.6 1.7 %collective-permute-start = (f32[160,128]{1,0:T(8,128)S(1)}, f32[160,128]{1,0:T(8,128)S(1)}, u32[]{:S(2)}, u32[]{:S(2)}) collective-permute-start(f32[160,128]{1,0:T(8,128)S(1)} %get-tuple-element.62), channel_id=1, source_target_pairs={{0,8},{8,16},{16,24},{24,32},{32,40},{40,48},{48,56},{56,64},{64,7... | collective-permute-start | bytes 245768 | tf_op jit(solution)/shard_map/ppermute | solution.py:680
  3.3 3.7 %collective-permute-start.1 = (f32[160,128]{1,0:T(8,128)S(1)}, f32[160,128]{1,0:T(8,128)S(1)}, u32[]{:S(2)}, u32[]{:S(2)}) collective-permute-start(f32[160,128]{1,0:T(8,128)S(1)} %get-tuple-element.63), channel_id=1, source_target_pairs={{0,120},{8,0},{16,8},{24,16},{32,24},{40,32},{48,40},{56,48},{64,5... | collective-permute-start | bytes 245768 | tf_op jit(solution)/shard_map/ppermute | solution.py:680
  7.0 0.0 collective-permute-start.2
  7.0 3.2 %collective-permute-start.3 = (f32[96,128]{1,0:T(8,128)S(1)}, f32[96,128]{1,0:T(8,128)S(1)}, u32[]{:S(2)}, u32[]{:S(2)}) collective-permute-start(f32[96,128]{1,0:T(8,128)S(1)} %get-tuple-element.65), channel_id=1, source_target_pairs={{0,7},{1,0},{2,1},{3,2},{4,3},{5,4},{6,5},{7,6},{8,15},{9,8},{10,9... | collective-permute-start | bytes 147464 | tf_op jit(solution)/shard_map/ppermute | solution.py:680
  10.2 1.8 %collective-permute-done.2.refs_2_ = f32[96,128]{1,0:T(8,128)S(1)} collective-permute-done((f32[96,128]{1,0:T(8,128)S(1)}, f32[96,128]{1,0:T(8,128)S(1)}, u32[]{:S(2)}, u32[]{:S(2)}) %collective-permute-start.2) | collective-permute-done | bytes 49184 | tf_op jit(solution)/shard_map/ppermute | solution.py:680
  12.0 0.0 collective-permute-done.3.refs_3_
  12.0 0.0 collective-permute-done.refs_0_.refs_2_
  12.0 0.0 copy-start.1
  12.0 0.0 collective-permute-done.1.refs_1_.refs_3_.refs_14_
  12.0 0.0 copy-start
  12.0 0.0 copy-done.4
  12.0 3.5 %onex.1 = (f32[512,128]{1,0:T(8,128)}, f32[512,128]{1,0:T(8,128)}, f32[640,128]{1,0:T(8,128)}, f32[640,128]{1,0:T(8,128)}, f32[640,128]{1,0:T(8,128)}, /*index=5...) custom-call(f32[160,128]{1,0:T(8,128)S(1)} %collective-permute-done.refs_0_.refs_2_, ...), custom_call_target="tpu_custom_call" | custom-call | flops 1000 | bytes 1000 | tf_op jit(solution)/shard_map/onex/pallas_call | solution.py:659
  15.5 3.5 %all-to-all-start = ((f32[4,176,128]{2,1,0:T(8,128)}), f32[4,176,128]{2,1,0:T(8,128)S(1)}, u32[]{:S(2)}, u32[]{:S(2)}) async-start(f32[4,176,128]{2,1,0:T(8,128)} %bitcast.17), calls=%async_computation | async-start | bytes 720896 | tf_op jit(solution)/shard_map/all_to_all | solution.py:685
  19.0 0.0 copy-done.1
  19.0 0.0 copy-done
  19.0 3.4 %oney.1 = (f32[128,128]{1,0:T(8,128)S(1)}, f32[544,128]{1,0:T(8,128)}, f32[544,128]{1,0:T(8,128)}, f32[768,128]{1,0:T(8,128)}, f32[768,128]{1,0:T(8,128)}, /*ind...) custom-call(f32[3072,128]{1,0:T(8,128)} %bitcast.13, f32[512,128]{1,0:T(8,128)} %get-tuple-element.66.refs_1_, ...), custom_call_target="tpu_custom_call" | custom-call | flops 1000 | bytes 1000 | tf_op jit(solution)/shard_map/oney/pallas_call | solution.py:659
  22.5 0.0 copy-start.2
  22.5 0.7 %collective-permute-start.4 = (f32[128,128]{1,0:T(8,128)S(1)}, f32[128,128]{1,0:T(8,128)S(1)}, u32[]{:S(2)}, u32[]{:S(2)}) collective-permute-start(f32[128,128]{1,0:T(8,128)S(1)} %get-tuple-element.67.refs_0_.refs_4_), channel_id=1, source_target_pairs={{0,1},{1,0},{2,3},{3,2},{4,5},{5,4},{6,7},{7,6},{8,9},{9,8},{10,11... | collective-permute-start | bytes 196616 | tf_op jit(solution)/shard_map/ppermute | solution.py:680
  23.2 0.9 %collective-permute-done.4.refs_1_.refs_5_ = f32[128,128]{1,0:T(8,128)S(1)} collective-permute-done((f32[128,128]{1,0:T(8,128)S(1)}, f32[128,128]{1,0:T(8,128)S(1)}, u32[]{:S(2)}, u32[]{:S(2)}) %collective-permute-start.4) | collective-permute-done | bytes 65568 | tf_op jit(solution)/shard_map/ppermute | solution.py:680
  24.1 0.0 copy-start.3
  24.1 3.7 %all-to-all-done = f32[4,176,128]{2,1,0:T(8,128)S(1)} async-done(((f32[4,176,128]{2,1,0:T(8,128)}), f32[4,176,128]{2,1,0:T(8,128)S(1)}, u32[]{:S(2)}, u32[]{:S(2)}) %all-to-all-start) | async-done | bytes 360480 | tf_op jit(solution)/shard_map/all_to_all | solution.py:685
  27.8 1.1 %group.1 = (f32[128,128]{1,0:T(8,128)S(1)}, f32[704,128]{1,0:T(8,128)}, f32[704,128]{1,0:T(8,128)}) custom-call(f32[128,128]{1,0:T(8,128)S(1)} %get-tuple-element.67.refs_0_.refs_4_, f32[128,128]{1,0:T(8,128)S(1)} %collective-permute-done.4.refs_1_.refs_5_, f32[704,128]{1,0:T(8,128)S(1)} %bitcast.10), custom_call_target="tpu_custom_call" | custom-call | flops 1000 | bytes 1000 | tf_op jit(solution)/shard_map/group/pallas_call | solution.py:659
  28.9 3.5 %all-to-all-start.1 = ((f32[4,176,128]{2,1,0:T(8,128)}), f32[4,176,128]{2,1,0:T(8,128)S(1)}, u32[]{:S(2)}, u32[]{:S(2)}) async-start(f32[4,176,128]{2,1,0:T(8,128)} %bitcast.18), calls=%async_computation.1 | async-start | bytes 720896 | tf_op jit(solution)/shard_map/all_to_all | solution.py:685
  32.3 2.8 %collective-permute-start.7 = (f32[128,128]{1,0:T(8,128)S(1)}, f32[128,128]{1,0:T(8,128)S(1)}, u32[]{:S(2)}, u32[]{:S(2)}) collective-permute-start(f32[128,128]{1,0:T(8,128)S(1)} %get-tuple-element.69.refs_0_), channel_id=1, source_target_pairs={{0,6},{2,0},{4,2},{6,4},{1,7},{3,1},{5,3},{7,5},{8,14},{10,8},{12,... | collective-permute-start | bytes 196616 | tf_op jit(solution)/shard_map/ppermute | solution.py:680
  35.1 0.6 collective-permute-start.6
  35.7 1.0 %collective-permute-start.5 = (f32[128,128]{1,0:T(8,128)S(1)}, f32[128,128]{1,0:T(8,128)S(1)}, u32[]{:S(2)}, u32[]{:S(2)}) collective-permute-start(f32[128,128]{1,0:T(8,128)S(1)} %get-tuple-element.69.refs_0_), channel_id=1, source_target_pairs={{0,2},{2,4},{4,6},{6,0},{1,3},{3,5},{5,7},{7,1},{8,10},{10,12},{12... | collective-permute-start | bytes 196616 | tf_op jit(solution)/shard_map/ppermute | solution.py:680
  36.7 0.5 collective-permute-done.7.refs_3_
  37.2 3.7 %collective-permute-done.6.refs_2_ = f32[128,128]{1,0:T(8,128)S(1)} collective-permute-done((f32[128,128]{1,0:T(8,128)S(1)}, f32[128,128]{1,0:T(8,128)S(1)}, u32[]{:S(2)}, u32[]{:S(2)}) %collective-permute-start.6) | collective-permute-done | bytes 65568 | tf_op jit(solution)/shard_map/ppermute | solution.py:680
  40.9 0.7 collective-permute-done.5.refs_1_
  41.6 0.0 all-to-all-done.1
  41.6 0.0 copy-done.2
  41.6 0.0 copy-done.3
  41.6 5.6 %two.1 = (f32[544,128]{1,0:T(8,128)}, f32[48,128]{1,0:T(8,128)}, f32[48,128]{1,0:T(8,128)}, f32[48,128]{1,0:T(8,128)}, f32[48,128]{1,0:T(8,128)}, /*index=5*/f32...) custom-call(f32[128,128]{1,0:T(8,128)S(1)} %get-tuple-element.69.ref, ...), custom_call_target="tpu_custom_call" | custom-call | flops 1000 | bytes 1000 | tf_op jit(solution)/shard_map/two/pallas_call | solution.py:659
  47.2 5.4 %all-to-all-start.2 = ((f32[16,64,128]{2,1,0:T(8,128)}), f32[16,64,128]{2,1,0:T(8,128)S(1)}, u32[]{:S(2)}, u32[]{:S(2)}) async-start(f32[16,64,128]{2,1,0:T(8,128)} %bitcast.16), calls=%async_computation.2 | async-start | bytes 1048576 | tf_op jit(solution)/shard_map/all_to_all | solution.py:685
  52.6 0.1 collective-permute-start.8
  52.7 1.2 %collective-permute-done.8.refs_1_.refs_5_ = f32[48,128]{1,0:T(8,128)S(1)} collective-permute-done((f32[48,128]{1,0:T(8,128)S(1)}, f32[48,128]{1,0:T(8,128)S(1)}, u32[]{:S(2)}, u32[]{:S(2)}) %collective-permute-start.8) | collective-permute-done | bytes 24608 | tf_op jit(solution)/shard_map/ppermute | solution.py:680
  53.9 0.9 %ends.1.refs_0_ = f32[48,128]{1,0:T(8,128)S(1)} custom-call(f32[48,128]{1,0:T(8,128)S(1)} %get-tuple-element.85.refs_0_.refs_4_, f32[48,128]{1,0:T(8,128)S(1)} %collective-permute-done.8.refs_1_.refs_5_, f32[48,128]{1,0:T(8,128)} %get-tuple-element.86.refs_2_.refs_7_, f32[48,128]{1,0:T(8,128)} %get-tuple-element.87.refs_3_.refs_8_, ...), custom_call_target="tpu_custom_call" | custom-call | flops 1000 | bytes 1000 | tf_op jit(solution)/shard_map/ends/pallas_call | solution.py:659
  54.8 0.6 collective-permute-start.11
  55.5 1.0 %collective-permute-start.10 = (f32[48,128]{1,0:T(8,128)S(1)}, f32[48,128]{1,0:T(8,128)S(1)}, u32[]{:S(2)}, u32[]{:S(2)}) collective-permute-start(f32[48,128]{1,0:T(8,128)S(1)} %ends.1.refs_0_), channel_id=1, source_target_pairs={{0,4},{2,6},{4,0},{6,2},{1,5},{3,7},{5,1},{7,3},{8,12},{10,14},{12... | collective-permute-start | bytes 73736 | tf_op jit(solution)/shard_map/ppermute | solution.py:680
  56.4 1.2 %collective-permute-start.9 = (f32[48,128]{1,0:T(8,128)S(1)}, f32[48,128]{1,0:T(8,128)S(1)}, u32[]{:S(2)}, u32[]{:S(2)}) collective-permute-start(f32[48,128]{1,0:T(8,128)S(1)} %ends.1.refs_0_), channel_id=1, source_target_pairs={{0,2},{2,4},{4,6},{6,0},{1,3},{3,5},{5,7},{7,1},{8,10},{10,12},{12... | collective-permute-start | bytes 73736 | tf_op jit(solution)/shard_map/ppermute | solution.py:680
  57.6 1.1 %collective-permute-done.11.refs_3_ = f32[48,128]{1,0:T(8,128)S(1)} collective-permute-done((f32[48,128]{1,0:T(8,128)S(1)}, f32[48,128]{1,0:T(8,128)S(1)}, u32[]{:S(2)}, u32[]{:S(2)}) %collective-permute-start.11) | collective-permute-done | bytes 24608 | tf_op jit(solution)/shard_map/ppermute | solution.py:680
  58.7 2.1 %collective-permute-done.10.refs_2_ = f32[48,128]{1,0:T(8,128)S(1)} collective-permute-done((f32[48,128]{1,0:T(8,128)S(1)}, f32[48,128]{1,0:T(8,128)S(1)}, u32[]{:S(2)}, u32[]{:S(2)}) %collective-permute-start.10) | collective-permute-done | bytes 24608 | tf_op jit(solution)/shard_map/ppermute | solution.py:680
  60.8 0.7 %collective-permute-done.9.refs_1_ = f32[48,128]{1,0:T(8,128)S(1)} collective-permute-done((f32[48,128]{1,0:T(8,128)S(1)}, f32[48,128]{1,0:T(8,128)S(1)}, u32[]{:S(2)}, u32[]{:S(2)}) %collective-permute-start.9) | collective-permute-done | bytes 24608 | tf_op jit(solution)/shard_map/ppermute | solution.py:680
  61.5 1.3 %all-to-all-done.2 = f32[16,64,128]{2,1,0:T(8,128)S(1)} async-done(((f32[16,64,128]{2,1,0:T(8,128)}), f32[16,64,128]{2,1,0:T(8,128)S(1)}, u32[]{:S(2)}, u32[]{:S(2)}) %all-to-all-start.2) | async-done | bytes 524320 | tf_op jit(solution)/shard_map/all_to_all | solution.py:685
  62.7 4.1 %three.1 = f32[3072,128]{1,0:T(8,128)} custom-call(f32[48,128]{1,0:T(8,128)S(1)} %ends.1.refs_0_, f32[48,128]{1,0:T(8,128)S(1)} %collective-permute-done.9.refs_1_, f32[48,128]{1,0:T(8,128)S(1)} %collective-permute-done.10.refs_2_, f32[48,128]{1,0:T(8,128)S(1)} %collective-permute-done.11.refs_3_, f32[48,128]{1,0:T(8,128)S(1)} %get-tuple-element.85.refs_0_.refs_4_, ...), custom_call_target="tpu_custom_call" | custom-call | flops 1000 | bytes 1000 | tf_op jit(solution)/shard_map/three/pallas_call | solution.py:659
Async XLA Ops:
  0.0 12.0 %copy-start.4 = (f32[16]{0:T(128)S(1)}, f32[16]{0:T(128)}, u32[]{:S(2)}) copy-start(f32[16]{0:T(128)} %refs_6_.1) | copy-start | bytes 196
  1.6 10.4 %collective-permute-start = (f32[160,128]{1,0:T(8,128)S(1)}, f32[160,128]{1,0:T(8,128)S(1)}, u32[]{:S(2)}, u32[]{:S(2)}) collective-permute-start(f32[160,128]{1,0:T(8,128)S(1)} %get-tuple-element.62), channel_id=1, source_target_pairs={{0,8},{8,16},{16,24},{24,32},{32,40},{40,48},{48,56},{56,64},{64,7... | collective-permute-start | bytes 245768 | tf_op jit(solution)/shard_map/ppermute | solution.py:680
  3.3 8.7 %collective-permute-start.1 = (f32[160,128]{1,0:T(8,128)S(1)}, f32[160,128]{1,0:T(8,128)S(1)}, u32[]{:S(2)}, u32[]{:S(2)}) collective-permute-start(f32[160,128]{1,0:T(8,128)S(1)} %get-tuple-element.63), channel_id=1, source_target_pairs={{0,120},{8,0},{16,8},{24,16},{32,24},{40,32},{48,40},{56,48},{64,5... | collective-permute-start | bytes 245768 | tf_op jit(solution)/shard_map/ppermute | solution.py:680
  7.0 5.0 %collective-permute-start.2 = (f32[96,128]{1,0:T(8,128)S(1)}, f32[96,128]{1,0:T(8,128)S(1)}, u32[]{:S(2)}, u32[]{:S(2)}) collective-permute-start(f32[96,128]{1,0:T(8,128)S(1)} %get-tuple-element.64), channel_id=1, source_target_pairs={{0,1},{1,2},{2,3},{3,4},{4,5},{5,6},{6,7},{7,0},{8,9},{9,10},{10,1... | collective-permute-start | bytes 147464 | tf_op jit(solution)/shard_map/ppermute | solution.py:680
  7.0 5.0 %collective-permute-start.3 = (f32[96,128]{1,0:T(8,128)S(1)}, f32[96,128]{1,0:T(8,128)S(1)}, u32[]{:S(2)}, u32[]{:S(2)}) collective-permute-start(f32[96,128]{1,0:T(8,128)S(1)} %get-tuple-element.65), channel_id=1, source_target_pairs={{0,7},{1,0},{2,1},{3,2},{4,3},{5,4},{6,5},{7,6},{8,15},{9,8},{10,9... | collective-permute-start | bytes 147464 | tf_op jit(solution)/shard_map/ppermute | solution.py:680
  12.0 7.0 %copy-start.1 = (f32[160,128]{1,0:T(8,128)}, f32[160,128]{1,0:T(8,128)S(1)}, u32[]{:S(2)}) copy-start(f32[160,128]{1,0:T(8,128)S(1)} %collective-permute-done.refs_0_.refs_2_) | copy-start | bytes 245764
  12.0 7.0 %copy-start = (f32[160,128]{1,0:T(8,128)}, f32[160,128]{1,0:T(8,128)S(1)}, u32[]{:S(2)}) copy-start(f32[160,128]{1,0:T(8,128)S(1)} %collective-permute-done.1.refs_1_.refs_3_.refs_14_) | copy-start | bytes 245764
  15.5 12.2 %all-to-all-start = ((f32[4,176,128]{2,1,0:T(8,128)}), f32[4,176,128]{2,1,0:T(8,128)S(1)}, u32[]{:S(2)}, u32[]{:S(2)}) async-start(f32[4,176,128]{2,1,0:T(8,128)} %bitcast.17), calls=%async_computation | async-start | bytes 720896 | tf_op jit(solution)/shard_map/all_to_all | solution.py:685
  22.5 19.2 %copy-start.2 = (f32[128,128]{1,0:T(8,128)}, f32[128,128]{1,0:T(8,128)S(1)}, u32[]{:S(2)}) copy-start(f32[128,128]{1,0:T(8,128)S(1)} %get-tuple-element.67.refs_0_.refs_4_) | copy-start | bytes 196612
  22.5 1.6 %collective-permute-start.4 = (f32[128,128]{1,0:T(8,128)S(1)}, f32[128,128]{1,0:T(8,128)S(1)}, u32[]{:S(2)}, u32[]{:S(2)}) collective-permute-start(f32[128,128]{1,0:T(8,128)S(1)} %get-tuple-element.67.refs_0_.refs_4_), channel_id=1, source_target_pairs={{0,1},{1,0},{2,3},{3,2},{4,5},{5,4},{6,7},{7,6},{8,9},{9,8},{10,11... | collective-permute-start | bytes 196616 | tf_op jit(solution)/shard_map/ppermute | solution.py:680
  24.1 17.5 %copy-start.3 = (f32[128,128]{1,0:T(8,128)}, f32[128,128]{1,0:T(8,128)S(1)}, u32[]{:S(2)}) copy-start(f32[128,128]{1,0:T(8,128)S(1)} %collective-permute-done.4.refs_1_.refs_5_) | copy-start | bytes 196612
  28.9 12.7 %all-to-all-start.1 = ((f32[4,176,128]{2,1,0:T(8,128)}), f32[4,176,128]{2,1,0:T(8,128)S(1)}, u32[]{:S(2)}, u32[]{:S(2)}) async-start(f32[4,176,128]{2,1,0:T(8,128)} %bitcast.18), calls=%async_computation.1 | async-start | bytes 720896 | tf_op jit(solution)/shard_map/all_to_all | solution.py:685
  32.3 4.9 %collective-permute-start.7 = (f32[128,128]{1,0:T(8,128)S(1)}, f32[128,128]{1,0:T(8,128)S(1)}, u32[]{:S(2)}, u32[]{:S(2)}) collective-permute-start(f32[128,128]{1,0:T(8,128)S(1)} %get-tuple-element.69.refs_0_), channel_id=1, source_target_pairs={{0,6},{2,0},{4,2},{6,4},{1,7},{3,1},{5,3},{7,5},{8,14},{10,8},{12,... | collective-permute-start | bytes 196616 | tf_op jit(solution)/shard_map/ppermute | solution.py:680
  35.1 5.8 %collective-permute-start.6 = (f32[128,128]{1,0:T(8,128)S(1)}, f32[128,128]{1,0:T(8,128)S(1)}, u32[]{:S(2)}, u32[]{:S(2)}) collective-permute-start(f32[128,128]{1,0:T(8,128)S(1)} %get-tuple-element.69.refs_0_), channel_id=1, source_target_pairs={{0,4},{2,6},{4,0},{6,2},{1,5},{3,7},{5,1},{7,3},{8,12},{10,14},{12... | collective-permute-start | bytes 196616 | tf_op jit(solution)/shard_map/ppermute | solution.py:680
  35.7 5.9 %collective-permute-start.5 = (f32[128,128]{1,0:T(8,128)S(1)}, f32[128,128]{1,0:T(8,128)S(1)}, u32[]{:S(2)}, u32[]{:S(2)}) collective-permute-start(f32[128,128]{1,0:T(8,128)S(1)} %get-tuple-element.69.refs_0_), channel_id=1, source_target_pairs={{0,2},{2,4},{4,6},{6,0},{1,3},{3,5},{5,7},{7,1},{8,10},{10,12},{12... | collective-permute-start | bytes 196616 | tf_op jit(solution)/shard_map/ppermute | solution.py:680
  47.2 15.5 %all-to-all-start.2 = ((f32[16,64,128]{2,1,0:T(8,128)}), f32[16,64,128]{2,1,0:T(8,128)S(1)}, u32[]{:S(2)}, u32[]{:S(2)}) async-start(f32[16,64,128]{2,1,0:T(8,128)} %bitcast.16), calls=%async_computation.2 | async-start | bytes 1048576 | tf_op jit(solution)/shard_map/all_to_all | solution.py:685
  52.6 1.3 %collective-permute-start.8 = (f32[48,128]{1,0:T(8,128)S(1)}, f32[48,128]{1,0:T(8,128)S(1)}, u32[]{:S(2)}, u32[]{:S(2)}) collective-permute-start(f32[48,128]{1,0:T(8,128)S(1)} %get-tuple-element.85.refs_0_.refs_4_), channel_id=1, source_target_pairs={{0,1},{1,0},{2,3},{3,2},{4,5},{5,4},{6,7},{7,6},{8,9},{9,8},{10,11... | collective-permute-start | bytes 73736 | tf_op jit(solution)/shard_map/ppermute | solution.py:680
  54.8 3.9 %collective-permute-start.11 = (f32[48,128]{1,0:T(8,128)S(1)}, f32[48,128]{1,0:T(8,128)S(1)}, u32[]{:S(2)}, u32[]{:S(2)}) collective-permute-start(f32[48,128]{1,0:T(8,128)S(1)} %ends.1.refs_0_), channel_id=1, source_target_pairs={{0,6},{2,0},{4,2},{6,4},{1,7},{3,1},{5,3},{7,5},{8,14},{10,8},{12,... | collective-permute-start | bytes 73736 | tf_op jit(solution)/shard_map/ppermute | solution.py:680
  55.5 5.3 %collective-permute-start.10 = (f32[48,128]{1,0:T(8,128)S(1)}, f32[48,128]{1,0:T(8,128)S(1)}, u32[]{:S(2)}, u32[]{:S(2)}) collective-permute-start(f32[48,128]{1,0:T(8,128)S(1)} %ends.1.refs_0_), channel_id=1, source_target_pairs={{0,4},{2,6},{4,0},{6,2},{1,5},{3,7},{5,1},{7,3},{8,12},{10,14},{12... | collective-permute-start | bytes 73736 | tf_op jit(solution)/shard_map/ppermute | solution.py:680
  56.4 5.0 %collective-permute-start.9 = (f32[48,128]{1,0:T(8,128)S(1)}, f32[48,128]{1,0:T(8,128)S(1)}, u32[]{:S(2)}, u32[]{:S(2)}) collective-permute-start(f32[48,128]{1,0:T(8,128)S(1)} %ends.1.refs_0_), channel_id=1, source_target_pairs={{0,2},{2,4},{4,6},{6,0},{1,3},{3,5},{5,7},{7,1},{8,10},{10,12},{12... | collective-permute-start | bytes 73736 | tf_op jit(solution)/shard_map/ppermute | solution.py:680

commit v5 on v4

--- a/solution.py
+++ b/solution.py
@@ -601,11 +601,13 @@
         later = w
 
 
-def call(name, parts, args, outs, scratch=(), smem=(), into=(), flush=(), near=(), only=()):
+def call(name, parts, args, outs, scratch=(), smem=(), into=(), flush=(), near=(), only=(), views=()):
     into, flush, scratch, only = dict(into), dict(flush), dict(scratch), dict(only)
+    views = dict(views)
+    touched = [list(used) + [views[k][0] for k in used if k in views] for _, used in parts]
     moved = [k for k in args if k not in smem and (k not in near or k in into)]
     pieces = {k for group in flush.values() for k, _, _ in group}
-    last = {k: max(i for i, (_, used) in enumerate(parts) if k in used) for k in outs}
+    last = {k: max(i for i, used in enumerate(touched) if k in used) for k in outs}
     leave = [
         [(k, 0, outs[k]) for k in outs if last[k] == i and k not in pieces and k not in near]
         + list(flush.get(i, ()))
@@ -621,6 +623,7 @@
         env.update({k: results[k] if k in near else next(take) for k in outs})
         env.update({k: next(take) for k in scratch})
         env.update({k: hbm[k] for k in args if k not in moved})
+        env.update({k: env[b].at[pl.ds(at, rows), :] for k, (b, at, rows) in views.items()})
         sem_in, sem_out = next(take), next(take)
         pending = {}
         count = 0
@@ -639,7 +642,7 @@
                 pending.setdefault(into[k][0] if k in into else k, []).append(copy)
         sent = []
         for i, (function, used) in enumerate(parts):
-            for k in used:
+            for k in touched[i]:
                 for copy in pending.pop(k, ()):
                     copy.wait()
             function(*[env[k] for k in used])
@@ -675,6 +678,10 @@
     return dict(zip(outs, got))
 
 
+def stacked(buffer, names, rows):
+    return {k: (buffer, sum(rows[:i]), rows[i]) for i, k in enumerate(names)}
+
+
 def ring(block, axis, step):
     n = lax.axis_size(axis)
     return lax.ppermute(block, axis, [(i, (i + step) % n) for i in range(n)])
@@ -718,6 +725,12 @@
     yr = ring(ydn, along_y, -1)
     linex = ("mx", "hx", "bx", "vx", "hbx")
     liney = ("my", "hy", "by", "vy", "hby")
+    lines_x, lines_y = 4 * nxl + 4 * XR, 4 * nyl + 4 * YR
+    lines = {
+        **stacked("lx", ("mx", "vx", "hx", "bx", "hbx"), (nxl,) * 4 + (4 * XR,)),
+        **stacked("ly", ("my", "vy", "hy", "by", "hby"), (nyl,) * 4 + (4 * YR,)),
+    }
+    of = lambda names: {k: lines[k] for k in names}
     one = call(
         "onex",
         [
@@ -725,25 +738,22 @@
             (k_x1, ("f", "eps", "xl", "xr", "yl", "yr", "msgx", "q1") + linex + ("r",)),
         ],
         dict(xl=xl, xr=xr, yl=yl, yr=yr, reg=reg, f=f, table=eps_table),
-        dict(zip(("eps", "q1") + linex + ("msgx",), (cells, cells, nxl, nxl, nxl, nxl, 4 * XR, nb * XB))),
+        dict(eps=cells, q1=cells, lx=lines_x, msgx=nb * XB),
         dict(r=nxl),
         smem=("table",),
         near=("xl", "xr", "yl", "yr") + NEAR,
         flush={0: [("eps", 0, cells)]},
+        views=of(linex),
         only=dict(f=[(EX * cells, cells), (EZ * cells, 3 * cells)]),
     )
     oney = call(
         "oney",
         [(k_y1, ("f", "eps", "xl", "xr", "msgy", "p1", "ey1") + liney + ("rt", "ep"))],
         dict(f=f, eps=one["eps"], xl=xl, xr=xr),
-        dict(
-            zip(
-                ("msgy", "p1", "ey1") + liney,
-                (YB, cells + PY, cells + PY, nyl, nyl, nyl, nyl, 4 * YR),
-            )
-        ),
+        dict(msgy=YB, p1=cells + PY, ey1=cells + PY, ly=lines_y),
         dict(rt=YR * PY, ep=YR * PY),
         near=("msgy",),
+        views=of(liney),
         only=dict(f=[(EX * cells, 2 * cells), (HX * cells, 3 * cells)]),
     )
     one.update(oney)
@@ -768,7 +778,9 @@
     ci, co, cyi, cyo = [tuple(k + a for k in chains) for a in ("i", "o", "yi", "yo")]
     cx, cy = ci + co, cyi + cyo
     size = lambda n, rows: (n * rows,) * 4 + ((n + 1) * rows,) * 2
-    keep = {k: one[k] for k in ("q1", "p1", "ey1") + linex + liney}
+    keep = {k: one[k] for k in ("q1", "p1", "ey1", "lx", "ly")}
+    rows_y, rows_x = size(nc, YR) + size(nz, YR), size(nb, XR) + size(na, XR)
+    views = {**stacked("cy", cy, rows_y), **stacked("cx", cx, rows_x)}
     two = call(
         "two",
         [
@@ -786,16 +798,11 @@
             ),
             (k_y3_sweep, ("rt", "my", "hby", "msgy2", "vy2", "vny2")),
         ],
-        dict(argy, **{k: keep[k] for k in ("hby", "vy", "by", "hy", "p1")}, gi=group["inner"], go=goto, f=f, xr=xr, **{k: keep[k] for k in linex + ("ey1", "q1", "my")}),
+        dict(argy, **{k: keep[k] for k in ("ly", "p1")}, gi=group["inner"], go=goto, f=f, xr=xr, **{k: keep[k] for k in ("lx", "ey1", "q1")}),
         dict(
             zip(
-                ("p2",) + cy + ("msgx2", "vx2", "vnx2") + cx + ("msgy2", "vy2", "vny2", "ex2", "hy1", "q2"),
-                (cells + PY,)
-                + size(nc, YR)
-                + size(nz, YR)
-                + (na * nb * 2 * PY, cells, PY)
-                + size(nb, XR)
-                + size(na, XR)
+                ("p2", "cy", "msgx2", "vx2", "vnx2", "cx", "msgy2", "vy2", "vny2", "ex2", "hy1", "q2"),
+                (cells + PY, sum(rows_y), na * nb * 2 * PY, cells, PY, sum(rows_x))
                 + (2 * YR, nyl, YR, cells, cells, cells),
             )
         ),
@@ -805,7 +812,8 @@
         ),
         into=into,
         near=("go", "msgy2", "party2") + NEAR + tuple(k for k in argy if k not in pair),
-        flush={0: [("p2", 0, cells + PY)] + [(k, 0, c) for k, c in zip(cy, size(nc, YR) + size(nz, YR))]},
+        flush={0: [("p2", 0, cells + PY), ("cy", 0, sum(rows_y))]},
+        views={**views, **lines},
         only=dict(f=[(EX * cells, cells), (EZ * cells, 3 * cells)]),
     )
     gotx = swap(two["msgx2"], along_x)
@@ -813,16 +821,18 @@
     group = call(
         "ends",
         [(k_join_ends, ("gyi",) + cyi[:4] + ("msg", "aly", "gay"))],
-        dict(pair, **{k: two[k] for k in cyi[:4]}),
+        dict(pair, cy=two["cy"]),
         dict(msg=2 * YR),
         dict(gyi=nc * 2 * YR, aly=ey, gay=ey),
         into=into,
         near=tuple(pair) + ("msg",),
+        views={k: views[k] for k in cyi[:4]},
+        only=dict(cy=[(0, sum(rows_y[:4]))]),
     )
     argy, into_o = from_all(group["msg"], "gz", "gyo")
     argy.update(pair)
     into.update(into_o)
-    order = cy + ("hby", "vny2", "vy2", "by", "hy", "ex2", "q2", "hy1") + cx + ("hbx", "vnx2", "vx2", "bx", "hx", "p2")
+    order = ("cy", "ly", "vny2", "vy2", "ex2", "q2", "hy1", "cx", "lx", "vnx2", "vx2", "p2")
     need = {k: two.get(k, one.get(k)) for k in order}
     three = call(
         "three",
@@ -842,6 +852,8 @@
         ),
         into=into,
         near=("gx",) + tuple(argy),
+        views={**views, **of(("hx", "bx", "hbx", "hy", "by", "hby"))},
+        only=dict(lx=[(2 * nxl, lines_x - 2 * nxl)], ly=[(2 * nyl, lines_y - 2 * nyl)]),
         flush={
             0: [("out", EX * cells, cells), ("out", EZ * cells, 3 * cells)],
             1: [("out", EY * cells, cells), ("out", HZ * cells, cells)],

time: 67.3 us -> 66.8 us (level)
  transfers between devices with their start and end apart: 15 -> 15, of which waited for: 11 -> 11; matrix products, arithmetic and copies ran while one was open for 0% -> 0% of each run, Pallas kernels for 6% -> 7%
where the time goes in v5:
time: 66.8 us; the launch traced here: 66.3 us
  starting transfers between devices  29 us (43%)
  Pallas kernels  19.9 us (30%)
  waiting for transfers between devices  17.3 us (26%)
    pallas_call x6, Pallas kernels, call(): pl.pallas_call(body, out_shape=[(pltpu.VMEM if k in near else pltpu.HBM)(...  18.3 us
    ppermute x12, starting transfers between devices, ring(): return lax.ppermute(block, axis, [(i, (i + step) % n) for i in range(n)])  16.6 us
    ppermute x12, waiting for transfers between devices, ring(): return lax.ppermute(block, axis, [(i, (i + step) % n) for i in range(n)])  12.6 us
    all_to_all x3, starting transfers between devices, swap(): got = lax.all_to_all(msg.reshape(n, -1, PZ), axis, 0, 0, tiled=True)  12.4 us
    all_to_all x3, waiting for transfers between devices, swap(): got = lax.all_to_all(msg.reshape(n, -1, PZ), axis, 0, 0, tiled=True)  4.72 us
    pallas_call x1, Pallas kernels, edges(): pl.pallas_call(k_edges, out_shape=[pltpu.VMEM((c, PZ), F32) for c in (5 *...  1.58 us
  transfers between devices with their start and end apart: 15, of which 11 were waited for; matrix products, arithmetic and copies ran while one was open for 0% of the time, Pallas kernels for 7%

profile of v5, /device:TPU:0, one launch (start us, length us, event | category | flops | bytes accessed | tf_op | source)
XLA Modules:
  0.0 66.3 jit_solution(5952613964345709752)
XLA Ops:
  0.0 0.0 copy-start.4
  0.0 1.6 %edges.1 = (f32[160,128]{1,0:T(8,128)S(1)}, f32[160,128]{1,0:T(8,128)S(1)}, f32[96,128]{1,0:T(8,128)S(1)}, f32[96,128]{1,0:T(8,128)S(1)}) custom-call(f32[6,16,32,128]{3,2,1,0:T(8,128)} %f.1, s32[16,32,128]{2,1,0:T(8,128)} %reg.1, f32[16]{0:T(128)} %refs_6_.1), custom_call_target="tpu_custom_call" | custom-call | flops 1000 | bytes 1000 | tf_op jit(solution)/shard_map/edges/pallas_call | solution.py:133
  1.6 1.7 %collective-permute-start = (f32[160,128]{1,0:T(8,128)S(1)}, f32[160,128]{1,0:T(8,128)S(1)}, u32[]{:S(2)}, u32[]{:S(2)}) collective-permute-start(f32[160,128]{1,0:T(8,128)S(1)} %get-tuple-element.32), channel_id=1, source_target_pairs={{0,8},{8,16},{16,24},{24,32},{32,40},{40,48},{48,56},{56,64},{64,7... | collective-permute-start | bytes 245768 | tf_op jit(solution)/shard_map/ppermute | solution.py:687
  3.3 3.7 %collective-permute-start.1 = (f32[160,128]{1,0:T(8,128)S(1)}, f32[160,128]{1,0:T(8,128)S(1)}, u32[]{:S(2)}, u32[]{:S(2)}) collective-permute-start(f32[160,128]{1,0:T(8,128)S(1)} %get-tuple-element.33), channel_id=1, source_target_pairs={{0,120},{8,0},{16,8},{24,16},{32,24},{40,32},{48,40},{56,48},{64,5... | collective-permute-start | bytes 245768 | tf_op jit(solution)/shard_map/ppermute | solution.py:687
  7.0 0.0 collective-permute-start.2
  7.0 3.2 %collective-permute-start.3 = (f32[96,128]{1,0:T(8,128)S(1)}, f32[96,128]{1,0:T(8,128)S(1)}, u32[]{:S(2)}, u32[]{:S(2)}) collective-permute-start(f32[96,128]{1,0:T(8,128)S(1)} %get-tuple-element.35), channel_id=1, source_target_pairs={{0,7},{1,0},{2,1},{3,2},{4,3},{5,4},{6,5},{7,6},{8,15},{9,8},{10,9... | collective-permute-start | bytes 147464 | tf_op jit(solution)/shard_map/ppermute | solution.py:687
  10.2 1.8 %collective-permute-done.2.refs_2_ = f32[96,128]{1,0:T(8,128)S(1)} collective-permute-done((f32[96,128]{1,0:T(8,128)S(1)}, f32[96,128]{1,0:T(8,128)S(1)}, u32[]{:S(2)}, u32[]{:S(2)}) %collective-permute-start.2) | collective-permute-done | bytes 49184 | tf_op jit(solution)/shard_map/ppermute | solution.py:687
  12.0 0.0 collective-permute-done.3.refs_3_
  12.0 0.0 collective-permute-done.refs_0_.refs_2_
  12.0 0.0 copy-start.1
  12.0 0.0 collective-permute-done.1.refs_1_.refs_3_.refs_11_
  12.0 0.0 copy-start
  12.0 0.0 copy-done.4
  12.0 3.4 %onex.1 = (f32[512,128]{1,0:T(8,128)}, f32[512,128]{1,0:T(8,128)}, f32[2720,128]{1,0:T(8,128)}, f32[704,128]{1,0:T(8,128)}) custom-call(f32[160,128]{1,0:T(8,128)S(1)} %collective-permute-done.refs_0_.refs_2_, f32[160,128]{1,0:T(8,128)S(1)} %collective-permute-done.1.refs_1_.refs_3_.refs_11_, f32[96,128]{1,0:T(8,128)S(1)} %collective-permute-done.2.refs_2_, ...), custom_call_target="tpu_custom_call" | custom-call | flops 1000 | bytes 1000 | tf_op jit(solution)/shard_map/onex/pallas_call | solution.py:662
  15.5 3.5 %all-to-all-start = ((f32[4,176,128]{2,1,0:T(8,128)}), f32[4,176,128]{2,1,0:T(8,128)S(1)}, u32[]{:S(2)}, u32[]{:S(2)}) async-start(f32[4,176,128]{2,1,0:T(8,128)} %bitcast.18), calls=%async_computation | async-start | bytes 720896 | tf_op jit(solution)/shard_map/all_to_all | solution.py:692
  19.0 0.0 copy-done.1
  19.0 0.0 copy-done
  19.0 3.6 %oney.1 = (f32[128,128]{1,0:T(8,128)S(1)}, f32[544,128]{1,0:T(8,128)}, f32[544,128]{1,0:T(8,128)}, f32[3168,128]{1,0:T(8,128)}) custom-call(f32[3072,128]{1,0:T(8,128)} %bitcast.13, f32[512,128]{1,0:T(8,128)} %get-tuple-element.36.refs_1_, f32[160,128]{1,0:T(8,128)} %copy-done.1, f32[160,128]{1,0:T(8,128)} %copy-done), custom_call_target="tpu_custom_call" | custom-call | flops 1000 | bytes 1000 | tf_op jit(solution)/shard_map/oney/pallas_call | solution.py:662
  22.6 0.0 copy-start.2
  22.6 0.7 %collective-permute-start.4 = (f32[128,128]{1,0:T(8,128)S(1)}, f32[128,128]{1,0:T(8,128)S(1)}, u32[]{:S(2)}, u32[]{:S(2)}) collective-permute-start(f32[128,128]{1,0:T(8,128)S(1)} %get-tuple-element.37.refs_0_.refs_4_), channel_id=1, source_target_pairs={{0,1},{1,0},{2,3},{3,2},{4,5},{5,4},{6,7},{7,6},{8,9},{9,8},{10,11... | collective-permute-start | bytes 196616 | tf_op jit(solution)/shard_map/ppermute | solution.py:687
  23.3 0.9 %collective-permute-done.4.refs_1_.refs_5_ = f32[128,128]{1,0:T(8,128)S(1)} collective-permute-done((f32[128,128]{1,0:T(8,128)S(1)}, f32[128,128]{1,0:T(8,128)S(1)}, u32[]{:S(2)}, u32[]{:S(2)}) %collective-permute-start.4) | collective-permute-done | bytes 65568 | tf_op jit(solution)/shard_map/ppermute | solution.py:687
  24.2 0.0 copy-start.3
  24.2 3.5 %all-to-all-done = f32[4,176,128]{2,1,0:T(8,128)S(1)} async-done(((f32[4,176,128]{2,1,0:T(8,128)}), f32[4,176,128]{2,1,0:T(8,128)S(1)}, u32[]{:S(2)}, u32[]{:S(2)}) %all-to-all-start) | async-done | bytes 360480 | tf_op jit(solution)/shard_map/all_to_all | solution.py:692
  27.7 1.1 %group.1 = (f32[128,128]{1,0:T(8,128)S(1)}, f32[704,128]{1,0:T(8,128)}, f32[704,128]{1,0:T(8,128)}) custom-call(f32[128,128]{1,0:T(8,128)S(1)} %get-tuple-element.37.refs_0_.refs_4_, f32[128,128]{1,0:T(8,128)S(1)} %collective-permute-done.4.refs_1_.refs_5_, f32[704,128]{1,0:T(8,128)S(1)} %bitcast.10), custom_call_target="tpu_custom_call" | custom-call | flops 1000 | bytes 1000 | tf_op jit(solution)/shard_map/group/pallas_call | solution.py:662
  28.9 3.5 %all-to-all-start.1 = ((f32[4,176,128]{2,1,0:T(8,128)}), f32[4,176,128]{2,1,0:T(8,128)S(1)}, u32[]{:S(2)}, u32[]{:S(2)}) async-start(f32[4,176,128]{2,1,0:T(8,128)} %bitcast.17), calls=%async_computation.1 | async-start | bytes 720896 | tf_op jit(solution)/shard_map/all_to_all | solution.py:692
  32.3 2.8 %collective-permute-start.7 = (f32[128,128]{1,0:T(8,128)S(1)}, f32[128,128]{1,0:T(8,128)S(1)}, u32[]{:S(2)}, u32[]{:S(2)}) collective-permute-start(f32[128,128]{1,0:T(8,128)S(1)} %get-tuple-element.39.refs_0_), channel_id=1, source_target_pairs={{0,6},{2,0},{4,2},{6,4},{1,7},{3,1},{5,3},{7,5},{8,14},{10,8},{12,... | collective-permute-start | bytes 196616 | tf_op jit(solution)/shard_map/ppermute | solution.py:687
  35.1 0.6 collective-permute-start.6
  35.7 1.0 %collective-permute-start.5 = (f32[128,128]{1,0:T(8,128)S(1)}, f32[128,128]{1,0:T(8,128)S(1)}, u32[]{:S(2)}, u32[]{:S(2)}) collective-permute-start(f32[128,128]{1,0:T(8,128)S(1)} %get-tuple-element.39.refs_0_), channel_id=1, source_target_pairs={{0,2},{2,4},{4,6},{6,0},{1,3},{3,5},{5,7},{7,1},{8,10},{10,12},{12... | collective-permute-start | bytes 196616 | tf_op jit(solution)/shard_map/ppermute | solution.py:687
  36.7 0.5 collective-permute-done.7.refs_3_
  37.2 3.7 %collective-permute-done.6.refs_2_ = f32[128,128]{1,0:T(8,128)S(1)} collective-permute-done((f32[128,128]{1,0:T(8,128)S(1)}, f32[128,128]{1,0:T(8,128)S(1)}, u32[]{:S(2)}, u32[]{:S(2)}) %collective-permute-start.6) | collective-permute-done | bytes 65568 | tf_op jit(solution)/shard_map/ppermute | solution.py:687
  40.9 0.7 collective-permute-done.5.refs_1_
  41.6 0.0 all-to-all-done.1
  41.6 0.0 copy-done.2
  41.6 0.0 copy-done.3
  41.6 5.4 %two.1 = (f32[544,128]{1,0:T(8,128)}, f32[960,128]{1,0:T(8,128)}, f32[1024,128]{1,0:T(8,128)}, f32[512,128]{1,0:T(8,128)}, f32[32,128]{1,0:T(8,128)}, /*index=5*...) custom-call(f32[128,128]{1,0:T(8,128)S(1)} %get-tuple-element.39.ref, ...), custom_call_target="tpu_custom_call" | custom-call | flops 1000 | bytes 1000 | tf_op jit(solution)/shard_map/two/pallas_call | solution.py:662
  47.0 5.4 %all-to-all-start.2 = ((f32[16,64,128]{2,1,0:T(8,128)}), f32[16,64,128]{2,1,0:T(8,128)S(1)}, u32[]{:S(2)}, u32[]{:S(2)}) async-start(f32[16,64,128]{2,1,0:T(8,128)} %bitcast.16), calls=%async_computation.2 | async-start | bytes 1048576 | tf_op jit(solution)/shard_map/all_to_all | solution.py:692
  52.5 0.1 collective-permute-start.8
  52.6 1.2 %collective-permute-done.8.refs_1_.refs_5_ = f32[48,128]{1,0:T(8,128)S(1)} collective-permute-done((f32[48,128]{1,0:T(8,128)S(1)}, f32[48,128]{1,0:T(8,128)S(1)}, u32[]{:S(2)}, u32[]{:S(2)}) %collective-permute-start.8) | collective-permute-done | bytes 24608 | tf_op jit(solution)/shard_map/ppermute | solution.py:687
  53.7 1.0 %ends.1.refs_0_ = f32[48,128]{1,0:T(8,128)S(1)} custom-call(f32[48,128]{1,0:T(8,128)S(1)} %get-tuple-element.47.refs_0_.refs_4_, f32[48,128]{1,0:T(8,128)S(1)} %collective-permute-done.8.refs_1_.refs_5_, f32[960,128]{1,0:T(8,128)} %get-tuple-element.48.refs_2_.refs_7_), custom_call_target="tpu_custom_call" | custom-call | flops 1000 | bytes 1000 | tf_op jit(solution)/shard_map/ends/pallas_call | solution.py:662
  54.7 0.6 collective-permute-start.11
  55.4 1.0 %collective-permute-start.10 = (f32[48,128]{1,0:T(8,128)S(1)}, f32[48,128]{1,0:T(8,128)S(1)}, u32[]{:S(2)}, u32[]{:S(2)}) collective-permute-start(f32[48,128]{1,0:T(8,128)S(1)} %ends.1.refs_0_), channel_id=1, source_target_pairs={{0,4},{2,6},{4,0},{6,2},{1,5},{3,7},{5,1},{7,3},{8,12},{10,14},{12... | collective-permute-start | bytes 73736 | tf_op jit(solution)/shard_map/ppermute | solution.py:687
  56.3 1.2 %collective-permute-start.9 = (f32[48,128]{1,0:T(8,128)S(1)}, f32[48,128]{1,0:T(8,128)S(1)}, u32[]{:S(2)}, u32[]{:S(2)}) collective-permute-start(f32[48,128]{1,0:T(8,128)S(1)} %ends.1.refs_0_), channel_id=1, source_target_pairs={{0,2},{2,4},{4,6},{6,0},{1,3},{3,5},{5,7},{7,1},{8,10},{10,12},{12... | collective-permute-start | bytes 73736 | tf_op jit(solution)/shard_map/ppermute | solution.py:687
  57.5 1.1 %collective-permute-done.11.refs_3_ = f32[48,128]{1,0:T(8,128)S(1)} collective-permute-done((f32[48,128]{1,0:T(8,128)S(1)}, f32[48,128]{1,0:T(8,128)S(1)}, u32[]{:S(2)}, u32[]{:S(2)}) %collective-permute-start.11) | collective-permute-done | bytes 24608 | tf_op jit(solution)/shard_map/ppermute | solution.py:687
  58.6 2.1 %collective-permute-done.10.refs_2_ = f32[48,128]{1,0:T(8,128)S(1)} collective-permute-done((f32[48,128]{1,0:T(8,128)S(1)}, f32[48,128]{1,0:T(8,128)S(1)}, u32[]{:S(2)}, u32[]{:S(2)}) %collective-permute-start.10) | collective-permute-done | bytes 24608 | tf_op jit(solution)/shard_map/ppermute | solution.py:687
  60.7 0.7 %collective-permute-done.9.refs_1_ = f32[48,128]{1,0:T(8,128)S(1)} collective-permute-done((f32[48,128]{1,0:T(8,128)S(1)}, f32[48,128]{1,0:T(8,128)S(1)}, u32[]{:S(2)}, u32[]{:S(2)}) %collective-permute-start.9) | collective-permute-done | bytes 24608 | tf_op jit(solution)/shard_map/ppermute | solution.py:687
  61.4 1.2 %all-to-all-done.2 = f32[16,64,128]{2,1,0:T(8,128)S(1)} async-done(((f32[16,64,128]{2,1,0:T(8,128)}), f32[16,64,128]{2,1,0:T(8,128)S(1)}, u32[]{:S(2)}, u32[]{:S(2)}) %all-to-all-start.2) | async-done | bytes 524320 | tf_op jit(solution)/shard_map/all_to_all | solution.py:692
  62.6 3.7 %three.1 = f32[3072,128]{1,0:T(8,128)} custom-call(f32[48,128]{1,0:T(8,128)S(1)} %ends.1.refs_0_, f32[48,128]{1,0:T(8,128)S(1)} %collective-permute-done.9.refs_1_, f32[48,128]{1,0:T(8,128)S(1)} %collective-permute-done.10.refs_2_, f32[48,128]{1,0:T(8,128)S(1)} %collective-permute-done.11.refs_3_, f32[48,128]{1,0:T(8,128)S(1)} %get-tuple-element.47.refs_0_.refs_4_, ...), custom_call_target="tpu_custom_call" | custom-call | flops 1000 | bytes 1000 | tf_op jit(solution)/shard_map/three/pallas_call | solution.py:662
Async XLA Ops:
  0.0 12.0 %copy-start.4 = (f32[16]{0:T(128)S(1)}, f32[16]{0:T(128)}, u32[]{:S(2)}) copy-start(f32[16]{0:T(128)} %refs_6_.1) | copy-start | bytes 196
  1.6 10.4 %collective-permute-start = (f32[160,128]{1,0:T(8,128)S(1)}, f32[160,128]{1,0:T(8,128)S(1)}, u32[]{:S(2)}, u32[]{:S(2)}) collective-permute-start(f32[160,128]{1,0:T(8,128)S(1)} %get-tuple-element.32), channel_id=1, source_target_pairs={{0,8},{8,16},{16,24},{24,32},{32,40},{40,48},{48,56},{56,64},{64,7... | collective-permute-start | bytes 245768 | tf_op jit(solution)/shard_map/ppermute | solution.py:687
  3.3 8.7 %collective-permute-start.1 = (f32[160,128]{1,0:T(8,128)S(1)}, f32[160,128]{1,0:T(8,128)S(1)}, u32[]{:S(2)}, u32[]{:S(2)}) collective-permute-start(f32[160,128]{1,0:T(8,128)S(1)} %get-tuple-element.33), channel_id=1, source_target_pairs={{0,120},{8,0},{16,8},{24,16},{32,24},{40,32},{48,40},{56,48},{64,5... | collective-permute-start | bytes 245768 | tf_op jit(solution)/shard_map/ppermute | solution.py:687
  7.0 5.0 %collective-permute-start.2 = (f32[96,128]{1,0:T(8,128)S(1)}, f32[96,128]{1,0:T(8,128)S(1)}, u32[]{:S(2)}, u32[]{:S(2)}) collective-permute-start(f32[96,128]{1,0:T(8,128)S(1)} %get-tuple-element.34), channel_id=1, source_target_pairs={{0,1},{1,2},{2,3},{3,4},{4,5},{5,6},{6,7},{7,0},{8,9},{9,10},{10,1... | collective-permute-start | bytes 147464 | tf_op jit(solution)/shard_map/ppermute | solution.py:687
  7.0 5.0 %collective-permute-start.3 = (f32[96,128]{1,0:T(8,128)S(1)}, f32[96,128]{1,0:T(8,128)S(1)}, u32[]{:S(2)}, u32[]{:S(2)}) collective-permute-start(f32[96,128]{1,0:T(8,128)S(1)} %get-tuple-element.35), channel_id=1, source_target_pairs={{0,7},{1,0},{2,1},{3,2},{4,3},{5,4},{6,5},{7,6},{8,15},{9,8},{10,9... | collective-permute-start | bytes 147464 | tf_op jit(solution)/shard_map/ppermute | solution.py:687
  12.0 7.0 %copy-start.1 = (f32[160,128]{1,0:T(8,128)}, f32[160,128]{1,0:T(8,128)S(1)}, u32[]{:S(2)}) copy-start(f32[160,128]{1,0:T(8,128)S(1)} %collective-permute-done.refs_0_.refs_2_) | copy-start | bytes 245764
  12.0 7.0 %copy-start = (f32[160,128]{1,0:T(8,128)}, f32[160,128]{1,0:T(8,128)S(1)}, u32[]{:S(2)}) copy-start(f32[160,128]{1,0:T(8,128)S(1)} %collective-permute-done.1.refs_1_.refs_3_.refs_11_) | copy-start | bytes 245764
  15.5 12.2 %all-to-all-start = ((f32[4,176,128]{2,1,0:T(8,128)}), f32[4,176,128]{2,1,0:T(8,128)S(1)}, u32[]{:S(2)}, u32[]{:S(2)}) async-start(f32[4,176,128]{2,1,0:T(8,128)} %bitcast.18), calls=%async_computation | async-start | bytes 720896 | tf_op jit(solution)/shard_map/all_to_all | solution.py:692
  22.6 19.0 %copy-start.2 = (f32[128,128]{1,0:T(8,128)}, f32[128,128]{1,0:T(8,128)S(1)}, u32[]{:S(2)}) copy-start(f32[128,128]{1,0:T(8,128)S(1)} %get-tuple-element.37.refs_0_.refs_4_) | copy-start | bytes 196612
  22.6 1.6 %collective-permute-start.4 = (f32[128,128]{1,0:T(8,128)S(1)}, f32[128,128]{1,0:T(8,128)S(1)}, u32[]{:S(2)}, u32[]{:S(2)}) collective-permute-start(f32[128,128]{1,0:T(8,128)S(1)} %get-tuple-element.37.refs_0_.refs_4_), channel_id=1, source_target_pairs={{0,1},{1,0},{2,3},{3,2},{4,5},{5,4},{6,7},{7,6},{8,9},{9,8},{10,11... | collective-permute-start | bytes 196616 | tf_op jit(solution)/shard_map/ppermute | solution.py:687
  24.2 17.4 %copy-start.3 = (f32[128,128]{1,0:T(8,128)}, f32[128,128]{1,0:T(8,128)S(1)}, u32[]{:S(2)}) copy-start(f32[128,128]{1,0:T(8,128)S(1)} %collective-permute-done.4.refs_1_.refs_5_) | copy-start | bytes 196612
  28.9 12.7 %all-to-all-start.1 = ((f32[4,176,128]{2,1,0:T(8,128)}), f32[4,176,128]{2,1,0:T(8,128)S(1)}, u32[]{:S(2)}, u32[]{:S(2)}) async-start(f32[4,176,128]{2,1,0:T(8,128)} %bitcast.17), calls=%async_computation.1 | async-start | bytes 720896 | tf_op jit(solution)/shard_map/all_to_all | solution.py:692
  32.3 4.9 %collective-permute-start.7 = (f32[128,128]{1,0:T(8,128)S(1)}, f32[128,128]{1,0:T(8,128)S(1)}, u32[]{:S(2)}, u32[]{:S(2)}) collective-permute-start(f32[128,128]{1,0:T(8,128)S(1)} %get-tuple-element.39.refs_0_), channel_id=1, source_target_pairs={{0,6},{2,0},{4,2},{6,4},{1,7},{3,1},{5,3},{7,5},{8,14},{10,8},{12,... | collective-permute-start | bytes 196616 | tf_op jit(solution)/shard_map/ppermute | solution.py:687
  35.1 5.8 %collective-permute-start.6 = (f32[128,128]{1,0:T(8,128)S(1)}, f32[128,128]{1,0:T(8,128)S(1)}, u32[]{:S(2)}, u32[]{:S(2)}) collective-permute-start(f32[128,128]{1,0:T(8,128)S(1)} %get-tuple-element.39.refs_0_), channel_id=1, source_target_pairs={{0,4},{2,6},{4,0},{6,2},{1,5},{3,7},{5,1},{7,3},{8,12},{10,14},{12... | collective-permute-start | bytes 196616 | tf_op jit(solution)/shard_map/ppermute | solution.py:687
  35.7 5.9 %collective-permute-start.5 = (f32[128,128]{1,0:T(8,128)S(1)}, f32[128,128]{1,0:T(8,128)S(1)}, u32[]{:S(2)}, u32[]{:S(2)}) collective-permute-start(f32[128,128]{1,0:T(8,128)S(1)} %get-tuple-element.39.refs_0_), channel_id=1, source_target_pairs={{0,2},{2,4},{4,6},{6,0},{1,3},{3,5},{5,7},{7,1},{8,10},{10,12},{12... | collective-permute-start | bytes 196616 | tf_op jit(solution)/shard_map/ppermute | solution.py:687
  47.0 15.5 %all-to-all-start.2 = ((f32[16,64,128]{2,1,0:T(8,128)}), f32[16,64,128]{2,1,0:T(8,128)S(1)}, u32[]{:S(2)}, u32[]{:S(2)}) async-start(f32[16,64,128]{2,1,0:T(8,128)} %bitcast.16), calls=%async_computation.2 | async-start | bytes 1048576 | tf_op jit(solution)/shard_map/all_to_all | solution.py:692
  52.5 1.3 %collective-permute-start.8 = (f32[48,128]{1,0:T(8,128)S(1)}, f32[48,128]{1,0:T(8,128)S(1)}, u32[]{:S(2)}, u32[]{:S(2)}) collective-permute-start(f32[48,128]{1,0:T(8,128)S(1)} %get-tuple-element.47.refs_0_.refs_4_), channel_id=1, source_target_pairs={{0,1},{1,0},{2,3},{3,2},{4,5},{5,4},{6,7},{7,6},{8,9},{9,8},{10,11... | collective-permute-start | bytes 73736 | tf_op jit(solution)/shard_map/ppermute | solution.py:687
  54.7 3.9 %collective-permute-start.11 = (f32[48,128]{1,0:T(8,128)S(1)}, f32[48,128]{1,0:T(8,128)S(1)}, u32[]{:S(2)}, u32[]{:S(2)}) collective-permute-start(f32[48,128]{1,0:T(8,128)S(1)} %ends.1.refs_0_), channel_id=1, source_target_pairs={{0,6},{2,0},{4,2},{6,4},{1,7},{3,1},{5,3},{7,5},{8,14},{10,8},{12,... | collective-permute-start | bytes 73736 | tf_op jit(solution)/shard_map/ppermute | solution.py:687
  55.4 5.3 %collective-permute-start.10 = (f32[48,128]{1,0:T(8,128)S(1)}, f32[48,128]{1,0:T(8,128)S(1)}, u32[]{:S(2)}, u32[]{:S(2)}) collective-permute-start(f32[48,128]{1,0:T(8,128)S(1)} %ends.1.refs_0_), channel_id=1, source_target_pairs={{0,4},{2,6},{4,0},{6,2},{1,5},{3,7},{5,1},{7,3},{8,12},{10,14},{12... | collective-permute-start | bytes 73736 | tf_op jit(solution)/shard_map/ppermute | solution.py:687
  56.3 5.0 %collective-permute-start.9 = (f32[48,128]{1,0:T(8,128)S(1)}, f32[48,128]{1,0:T(8,128)S(1)}, u32[]{:S(2)}, u32[]{:S(2)}) collective-permute-start(f32[48,128]{1,0:T(8,128)S(1)} %ends.1.refs_0_), channel_id=1, source_target_pairs={{0,2},{2,4},{4,6},{6,0},{1,3},{3,5},{5,7},{7,1},{8,10},{10,12},{12... | collective-permute-start | bytes 73736 | tf_op jit(solution)/shard_map/ppermute | solution.py:687

commit v6 on v5

--- a/solution.py
+++ b/solution.py
@@ -731,25 +731,29 @@
         **stacked("ly", ("my", "vy", "hy", "by", "hby"), (nyl,) * 4 + (4 * YR,)),
     }
     of = lambda names: {k: lines[k] for k in names}
+    pre = call(
+        "eps",
+        [(k_eps, ("reg", "table", "eps"))],
+        dict(reg=reg, table=eps_table),
+        dict(eps=cells),
+        smem=("table",),
+    )
     one = call(
         "onex",
         [
-            (k_eps, ("reg", "table", "eps")),
             (k_x1, ("f", "eps", "xl", "xr", "yl", "yr", "msgx", "q1") + linex + ("r",)),
         ],
-        dict(xl=xl, xr=xr, yl=yl, yr=yr, reg=reg, f=f, table=eps_table),
-        dict(eps=cells, q1=cells, lx=lines_x, msgx=nb * XB),
+        dict(xl=xl, xr=xr, yl=yl, yr=yr, eps=pre["eps"], f=f),
+        dict(q1=cells, lx=lines_x, msgx=nb * XB),
         dict(r=nxl),
-        smem=("table",),
         near=("xl", "xr", "yl", "yr") + NEAR,
-        flush={0: [("eps", 0, cells)]},
         views=of(linex),
         only=dict(f=[(EX * cells, cells), (EZ * cells, 3 * cells)]),
     )
     oney = call(
         "oney",
         [(k_y1, ("f", "eps", "xl", "xr", "msgy", "p1", "ey1") + liney + ("rt", "ep"))],
-        dict(f=f, eps=one["eps"], xl=xl, xr=xr),
+        dict(f=f, eps=pre["eps"], xl=xl, xr=xr),
         dict(msgy=YB, p1=cells + PY, ey1=cells + PY, ly=lines_y),
         dict(rt=YR * PY, ep=YR * PY),
         near=("msgy",),

time: 66.8 us -> 66.3 us (level)
  waiting for transfers between devices: 17.3 us -> 15 us
  Pallas kernels: 19.9 us -> 21.8 us
    pallas_call x6 -> x7, Pallas kernels: 18.3 us -> 20.2 us  [call(): pl.pallas_call(body, out_shape=[(pltpu.VMEM if k in near else pltpu.HBM)(...]
    ppermute x12, waiting for transfers between devices: 12.6 us -> 11.1 us  [ring(): return lax.ppermute(block, axis, [(i, (i + step) % n) for i in range(n)])]
    all_to_all x3, waiting for transfers between devices: 4.72 us -> 3.88 us  [swap(): got = lax.all_to_all(msg.reshape(n, -1, PZ), axis, 0, 0, tiled=True)]
  transfers between devices with their start and end apart: 15 -> 15, of which waited for: 11 -> 10; matrix products, arithmetic and copies ran while one was open for 0% -> 0% of each run, Pallas kernels for 7% -> 11%
where the time goes in v6:
time: 66.3 us; the launch traced here: 65.8 us
  starting transfers between devices  28.8 us (43%)
  Pallas kernels  21.8 us (33%)
  waiting for transfers between devices  15 us (23%)
    pallas_call x7, Pallas kernels, call(): pl.pallas_call(body, out_shape=[(pltpu.VMEM if k in near else pltpu.HBM)(...  20.2 us
    ppermute x12, starting transfers between devices, ring(): return lax.ppermute(block, axis, [(i, (i + step) % n) for i in range(n)])  16.5 us
    all_to_all x3, starting transfers between devices, swap(): got = lax.all_to_all(msg.reshape(n, -1, PZ), axis, 0, 0, tiled=True)  12.3 us
    ppermute x12, waiting for transfers between devices, ring(): return lax.ppermute(block, axis, [(i, (i + step) % n) for i in range(n)])  11.1 us
    all_to_all x3, waiting for transfers between devices, swap(): got = lax.all_to_all(msg.reshape(n, -1, PZ), axis, 0, 0, tiled=True)  3.88 us
    pallas_call x1, Pallas kernels, edges(): pl.pallas_call(k_edges, out_shape=[pltpu.VMEM((c, PZ), F32) for c in (5 *...  1.58 us
  transfers between devices with their start and end apart: 15, of which 10 were waited for; matrix products, arithmetic and copies ran while one was open for 0% of the time, Pallas kernels for 11%

profile of v6, /device:TPU:0, one launch (start us, length us, event | category | flops | bytes accessed | tf_op | source)
XLA Modules:
  0.0 65.8 jit_solution(15932652710633941349)
XLA Ops:
  0.0 0.0 copy-start.4
  0.0 1.6 %edges.1 = (f32[160,128]{1,0:T(8,128)S(1)}, f32[160,128]{1,0:T(8,128)S(1)}, f32[96,128]{1,0:T(8,128)S(1)}, f32[96,128]{1,0:T(8,128)S(1)}) custom-call(f32[6,16,32,128]{3,2,1,0:T(8,128)} %f.1, s32[16,32,128]{2,1,0:T(8,128)} %reg.1, f32[16]{0:T(128)} %table.1), custom_call_target="tpu_custom_call" | custom-call | flops 1000 | bytes 1000 | tf_op jit(solution)/shard_map/edges/pallas_call | solution.py:133
  1.6 1.7 %collective-permute-start = (f32[160,128]{1,0:T(8,128)S(1)}, f32[160,128]{1,0:T(8,128)S(1)}, u32[]{:S(2)}, u32[]{:S(2)}) collective-permute-start(f32[160,128]{1,0:T(8,128)S(1)} %get-tuple-element.31), channel_id=1, source_target_pairs={{0,8},{8,16},{16,24},{24,32},{32,40},{40,48},{48,56},{56,64},{64,7... | collective-permute-start | bytes 245768 | tf_op jit(solution)/shard_map/ppermute | solution.py:687
  3.3 3.7 %collective-permute-start.1 = (f32[160,128]{1,0:T(8,128)S(1)}, f32[160,128]{1,0:T(8,128)S(1)}, u32[]{:S(2)}, u32[]{:S(2)}) collective-permute-start(f32[160,128]{1,0:T(8,128)S(1)} %get-tuple-element.32), channel_id=1, source_target_pairs={{0,120},{8,0},{16,8},{24,16},{32,24},{40,32},{48,40},{56,48},{64,5... | collective-permute-start | bytes 245768 | tf_op jit(solution)/shard_map/ppermute | solution.py:687
  7.0 0.0 collective-permute-start.3
  7.0 3.2 %collective-permute-start.4 = (f32[96,128]{1,0:T(8,128)S(1)}, f32[96,128]{1,0:T(8,128)S(1)}, u32[]{:S(2)}, u32[]{:S(2)}) collective-permute-start(f32[96,128]{1,0:T(8,128)S(1)} %get-tuple-element.35), channel_id=1, source_target_pairs={{0,7},{1,0},{2,1},{3,2},{4,3},{5,4},{6,5},{7,6},{8,15},{9,8},{10,9... | collective-permute-start | bytes 147464 | tf_op jit(solution)/shard_map/ppermute | solution.py:687
  10.2 0.0 copy-done.4
  10.2 2.4 %eps.1.refs_1_.refs_4_ = f32[512,128]{1,0:T(8,128)} custom-call(s32[512,128]{1,0:T(8,128)} %bitcast.15, f32[16]{0:T(128)S(1)} %copy-done.4), custom_call_target="tpu_custom_call" | custom-call | flops 1000 | bytes 1000 | tf_op jit(solution)/shard_map/eps/pallas_call | solution.py:662
  12.7 0.0 collective-permute-done.3.refs_2_
  12.7 0.0 collective-permute-done.4.refs_3_
  12.7 0.0 collective-permute-done.refs_2_.refs_0_
  12.7 0.0 copy-start.1
  12.7 0.0 collective-permute-done.1.refs_3_.refs_1_.refs_11_
  12.7 0.0 copy-start
  12.7 2.9 %onex.1 = (f32[512,128]{1,0:T(8,128)}, f32[2720,128]{1,0:T(8,128)}, f32[704,128]{1,0:T(8,128)}) custom-call(f32[160,128]{1,0:T(8,128)S(1)} %collective-permute-done.refs_2_.refs_0_, f32[160,128]{1,0:T(8,128)S(1)} %collective-permute-done.1.refs_3_.refs_1_.refs_11_, f32[96,128]{1,0:T(8,128)S(1)} %collective-permute-done.3.refs_2_, ...), custom_call_target="tpu_custom_call" | custom-call | flops 1000 | bytes 1000 | tf_op jit(solution)/shard_map/onex/pallas_call | solution.py:662
  15.7 3.5 %all-to-all-start = ((f32[4,176,128]{2,1,0:T(8,128)}), f32[4,176,128]{2,1,0:T(8,128)S(1)}, u32[]{:S(2)}, u32[]{:S(2)}) async-start(f32[4,176,128]{2,1,0:T(8,128)} %bitcast.18), calls=%async_computation | async-start | bytes 720896 | tf_op jit(solution)/shard_map/all_to_all | solution.py:692
  19.1 0.0 copy-done.1
  19.2 0.0 copy-done
  19.2 3.6 %oney.1 = (f32[128,128]{1,0:T(8,128)S(1)}, f32[544,128]{1,0:T(8,128)}, f32[544,128]{1,0:T(8,128)}, f32[3168,128]{1,0:T(8,128)}) custom-call(f32[3072,128]{1,0:T(8,128)} %bitcast.13, f32[512,128]{1,0:T(8,128)} %eps.1.refs_1_.refs_4_, f32[160,128]{1,0:T(8,128)} %copy-done.1, f32[160,128]{1,0:T(8,128)} %copy-done), custom_call_target="tpu_custom_call" | custom-call | flops 1000 | bytes 1000 | tf_op jit(solution)/shard_map/oney/pallas_call | solution.py:662
  22.8 0.0 copy-start.2
  22.8 0.1 collective-permute-start.2
  22.9 1.2 %collective-permute-done.2.refs_1_.refs_5_ = f32[128,128]{1,0:T(8,128)S(1)} collective-permute-done((f32[128,128]{1,0:T(8,128)S(1)}, f32[128,128]{1,0:T(8,128)S(1)}, u32[]{:S(2)}, u32[]{:S(2)}) %collective-permute-start.2) | collective-permute-done | bytes 65568 | tf_op jit(solution)/shard_map/ppermute | solution.py:687
  24.1 0.0 copy-start.3
  24.1 3.1 %all-to-all-done = f32[4,176,128]{2,1,0:T(8,128)S(1)} async-done(((f32[4,176,128]{2,1,0:T(8,128)}), f32[4,176,128]{2,1,0:T(8,128)S(1)}, u32[]{:S(2)}, u32[]{:S(2)}) %all-to-all-start) | async-done | bytes 360480 | tf_op jit(solution)/shard_map/all_to_all | solution.py:692
  27.2 1.1 %group.1 = (f32[128,128]{1,0:T(8,128)S(1)}, f32[704,128]{1,0:T(8,128)}, f32[704,128]{1,0:T(8,128)}) custom-call(f32[128,128]{1,0:T(8,128)S(1)} %get-tuple-element.33.refs_0_.refs_4_, f32[128,128]{1,0:T(8,128)S(1)} %collective-permute-done.2.refs_1_.refs_5_, f32[704,128]{1,0:T(8,128)S(1)} %bitcast.10), custom_call_target="tpu_custom_call" | custom-call | flops 1000 | bytes 1000 | tf_op jit(solution)/shard_map/group/pallas_call | solution.py:662
  28.4 3.5 %all-to-all-start.1 = ((f32[4,176,128]{2,1,0:T(8,128)}), f32[4,176,128]{2,1,0:T(8,128)S(1)}, u32[]{:S(2)}, u32[]{:S(2)}) async-start(f32[4,176,128]{2,1,0:T(8,128)} %bitcast.17), calls=%async_computation.1 | async-start | bytes 720896 | tf_op jit(solution)/shard_map/all_to_all | solution.py:692
  31.8 2.8 %collective-permute-start.7 = (f32[128,128]{1,0:T(8,128)S(1)}, f32[128,128]{1,0:T(8,128)S(1)}, u32[]{:S(2)}, u32[]{:S(2)}) collective-permute-start(f32[128,128]{1,0:T(8,128)S(1)} %get-tuple-element.37.refs_0_), channel_id=1, source_target_pairs={{0,6},{2,0},{4,2},{6,4},{1,7},{3,1},{5,3},{7,5},{8,14},{10,8},{12,... | collective-permute-start | bytes 196616 | tf_op jit(solution)/shard_map/ppermute | solution.py:687
  34.6 0.8 %collective-permute-start.6 = (f32[128,128]{1,0:T(8,128)S(1)}, f32[128,128]{1,0:T(8,128)S(1)}, u32[]{:S(2)}, u32[]{:S(2)}) collective-permute-start(f32[128,128]{1,0:T(8,128)S(1)} %get-tuple-element.37.refs_0_), channel_id=1, source_target_pairs={{0,4},{2,6},{4,0},{6,2},{1,5},{3,7},{5,1},{7,3},{8,12},{10,14},{12... | collective-permute-start | bytes 196616 | tf_op jit(solution)/shard_map/ppermute | solution.py:687
  35.4 1.3 %collective-permute-start.5 = (f32[128,128]{1,0:T(8,128)S(1)}, f32[128,128]{1,0:T(8,128)S(1)}, u32[]{:S(2)}, u32[]{:S(2)}) collective-permute-start(f32[128,128]{1,0:T(8,128)S(1)} %get-tuple-element.37.refs_0_), channel_id=1, source_target_pairs={{0,2},{2,4},{4,6},{6,0},{1,3},{3,5},{5,7},{7,1},{8,10},{10,12},{12... | collective-permute-start | bytes 196616 | tf_op jit(solution)/shard_map/ppermute | solution.py:687
  36.7 0.4 collective-permute-done.7.refs_3_
  37.1 3.3 %collective-permute-done.6.refs_2_ = f32[128,128]{1,0:T(8,128)S(1)} collective-permute-done((f32[128,128]{1,0:T(8,128)S(1)}, f32[128,128]{1,0:T(8,128)S(1)}, u32[]{:S(2)}, u32[]{:S(2)}) %collective-permute-start.6) | collective-permute-done | bytes 65568 | tf_op jit(solution)/shard_map/ppermute | solution.py:687
  40.5 0.7 %collective-permute-done.5.refs_1_ = f32[128,128]{1,0:T(8,128)S(1)} collective-permute-done((f32[128,128]{1,0:T(8,128)S(1)}, f32[128,128]{1,0:T(8,128)S(1)}, u32[]{:S(2)}, u32[]{:S(2)}) %collective-permute-start.5) | collective-permute-done | bytes 65568 | tf_op jit(solution)/shard_map/ppermute | solution.py:687
  41.1 0.0 all-to-all-done.1
  41.2 0.0 copy-done.2
  41.2 0.0 copy-done.3
  41.2 5.4 %two.1 = (f32[544,128]{1,0:T(8,128)}, f32[960,128]{1,0:T(8,128)}, f32[1024,128]{1,0:T(8,128)}, f32[512,128]{1,0:T(8,128)}, f32[32,128]{1,0:T(8,128)}, /*index=5*...) custom-call(f32[128,128]{1,0:T(8,128)S(1)} %get-tuple-element.37.ref, ...), custom_call_target="tpu_custom_call" | custom-call | flops 1000 | bytes 1000 | tf_op jit(solution)/shard_map/two/pallas_call | solution.py:662
  46.6 5.4 %all-to-all-start.2 = ((f32[16,64,128]{2,1,0:T(8,128)}), f32[16,64,128]{2,1,0:T(8,128)S(1)}, u32[]{:S(2)}, u32[]{:S(2)}) async-start(f32[16,64,128]{2,1,0:T(8,128)} %bitcast.16), calls=%async_computation.2 | async-start | bytes 1048576 | tf_op jit(solution)/shard_map/all_to_all | solution.py:692
  52.0 0.1 collective-permute-start.8
  52.1 1.2 %collective-permute-done.8.refs_1_.refs_5_ = f32[48,128]{1,0:T(8,128)S(1)} collective-permute-done((f32[48,128]{1,0:T(8,128)S(1)}, f32[48,128]{1,0:T(8,128)S(1)}, u32[]{:S(2)}, u32[]{:S(2)}) %collective-permute-start.8) | collective-permute-done | bytes 24608 | tf_op jit(solution)/shard_map/ppermute | solution.py:687
  53.2 1.0 %ends.1.refs_0_ = f32[48,128]{1,0:T(8,128)S(1)} custom-call(f32[48,128]{1,0:T(8,128)S(1)} %get-tuple-element.45.refs_0_.refs_4_, f32[48,128]{1,0:T(8,128)S(1)} %collective-permute-done.8.refs_1_.refs_5_, f32[960,128]{1,0:T(8,128)} %get-tuple-element.46.refs_2_.refs_7_), custom_call_target="tpu_custom_call" | custom-call | flops 1000 | bytes 1000 | tf_op jit(solution)/shard_map/ends/pallas_call | solution.py:662
  54.2 0.6 collective-permute-start.11
  54.9 1.4 %collective-permute-start.10 = (f32[48,128]{1,0:T(8,128)S(1)}, f32[48,128]{1,0:T(8,128)S(1)}, u32[]{:S(2)}, u32[]{:S(2)}) collective-permute-start(f32[48,128]{1,0:T(8,128)S(1)} %ends.1.refs_0_), channel_id=1, source_target_pairs={{0,4},{2,6},{4,0},{6,2},{1,5},{3,7},{5,1},{7,3},{8,12},{10,14},{12... | collective-permute-start | bytes 73736 | tf_op jit(solution)/shard_map/ppermute | solution.py:687
  56.3 0.8 %collective-permute-start.9 = (f32[48,128]{1,0:T(8,128)S(1)}, f32[48,128]{1,0:T(8,128)S(1)}, u32[]{:S(2)}, u32[]{:S(2)}) collective-permute-start(f32[48,128]{1,0:T(8,128)S(1)} %ends.1.refs_0_), channel_id=1, source_target_pairs={{0,2},{2,4},{4,6},{6,0},{1,3},{3,5},{5,7},{7,1},{8,10},{10,12},{12... | collective-permute-start | bytes 73736 | tf_op jit(solution)/shard_map/ppermute | solution.py:687
  57.0 1.1 %collective-permute-done.11.refs_3_ = f32[48,128]{1,0:T(8,128)S(1)} collective-permute-done((f32[48,128]{1,0:T(8,128)S(1)}, f32[48,128]{1,0:T(8,128)S(1)}, u32[]{:S(2)}, u32[]{:S(2)}) %collective-permute-start.11) | collective-permute-done | bytes 24608 | tf_op jit(solution)/shard_map/ppermute | solution.py:687
  58.1 2.1 %collective-permute-done.10.refs_2_ = f32[48,128]{1,0:T(8,128)S(1)} collective-permute-done((f32[48,128]{1,0:T(8,128)S(1)}, f32[48,128]{1,0:T(8,128)S(1)}, u32[]{:S(2)}, u32[]{:S(2)}) %collective-permute-start.10) | collective-permute-done | bytes 24608 | tf_op jit(solution)/shard_map/ppermute | solution.py:687
  60.2 1.1 %collective-permute-done.9.refs_1_ = f32[48,128]{1,0:T(8,128)S(1)} collective-permute-done((f32[48,128]{1,0:T(8,128)S(1)}, f32[48,128]{1,0:T(8,128)S(1)}, u32[]{:S(2)}, u32[]{:S(2)}) %collective-permute-start.9) | collective-permute-done | bytes 24608 | tf_op jit(solution)/shard_map/ppermute | solution.py:687
  61.3 0.8 %all-to-all-done.2 = f32[16,64,128]{2,1,0:T(8,128)S(1)} async-done(((f32[16,64,128]{2,1,0:T(8,128)}), f32[16,64,128]{2,1,0:T(8,128)S(1)}, u32[]{:S(2)}, u32[]{:S(2)}) %all-to-all-start.2) | async-done | bytes 524320 | tf_op jit(solution)/shard_map/all_to_all | solution.py:692
  62.1 3.7 %three.1 = f32[3072,128]{1,0:T(8,128)} custom-call(f32[48,128]{1,0:T(8,128)S(1)} %ends.1.refs_0_, f32[48,128]{1,0:T(8,128)S(1)} %collective-permute-done.9.refs_1_, f32[48,128]{1,0:T(8,128)S(1)} %collective-permute-done.10.refs_2_, f32[48,128]{1,0:T(8,128)S(1)} %collective-permute-done.11.refs_3_, f32[48,128]{1,0:T(8,128)S(1)} %get-tuple-element.45.refs_0_.refs_4_, ...), custom_call_target="tpu_custom_call" | custom-call | flops 1000 | bytes 1000 | tf_op jit(solution)/shard_map/three/pallas_call | solution.py:662
Async XLA Ops:
  0.0 10.2 %copy-start.4 = (f32[16]{0:T(128)S(1)}, f32[16]{0:T(128)}, u32[]{:S(2)}) copy-start(f32[16]{0:T(128)} %table.1) | copy-start | bytes 196
  1.6 11.1 %collective-permute-start = (f32[160,128]{1,0:T(8,128)S(1)}, f32[160,128]{1,0:T(8,128)S(1)}, u32[]{:S(2)}, u32[]{:S(2)}) collective-permute-start(f32[160,128]{1,0:T(8,128)S(1)} %get-tuple-element.31), channel_id=1, source_target_pairs={{0,8},{8,16},{16,24},{24,32},{32,40},{40,48},{48,56},{56,64},{64,7... | collective-permute-start | bytes 245768 | tf_op jit(solution)/shard_map/ppermute | solution.py:687
  3.3 9.4 %collective-permute-start.1 = (f32[160,128]{1,0:T(8,128)S(1)}, f32[160,128]{1,0:T(8,128)S(1)}, u32[]{:S(2)}, u32[]{:S(2)}) collective-permute-start(f32[160,128]{1,0:T(8,128)S(1)} %get-tuple-element.32), channel_id=1, source_target_pairs={{0,120},{8,0},{16,8},{24,16},{32,24},{40,32},{48,40},{56,48},{64,5... | collective-permute-start | bytes 245768 | tf_op jit(solution)/shard_map/ppermute | solution.py:687
  7.0 5.6 %collective-permute-start.3 = (f32[96,128]{1,0:T(8,128)S(1)}, f32[96,128]{1,0:T(8,128)S(1)}, u32[]{:S(2)}, u32[]{:S(2)}) collective-permute-start(f32[96,128]{1,0:T(8,128)S(1)} %get-tuple-element.34), channel_id=1, source_target_pairs={{0,1},{1,2},{2,3},{3,4},{4,5},{5,6},{6,7},{7,0},{8,9},{9,10},{10,1... | collective-permute-start | bytes 147464 | tf_op jit(solution)/shard_map/ppermute | solution.py:687
  7.0 5.6 %collective-permute-start.4 = (f32[96,128]{1,0:T(8,128)S(1)}, f32[96,128]{1,0:T(8,128)S(1)}, u32[]{:S(2)}, u32[]{:S(2)}) collective-permute-start(f32[96,128]{1,0:T(8,128)S(1)} %get-tuple-element.35), channel_id=1, source_target_pairs={{0,7},{1,0},{2,1},{3,2},{4,3},{5,4},{6,5},{7,6},{8,15},{9,8},{10,9... | collective-permute-start | bytes 147464 | tf_op jit(solution)/shard_map/ppermute | solution.py:687
  12.7 6.5 %copy-start.1 = (f32[160,128]{1,0:T(8,128)}, f32[160,128]{1,0:T(8,128)S(1)}, u32[]{:S(2)}) copy-start(f32[160,128]{1,0:T(8,128)S(1)} %collective-permute-done.refs_2_.refs_0_) | copy-start | bytes 245764
  12.7 6.4 %copy-start = (f32[160,128]{1,0:T(8,128)}, f32[160,128]{1,0:T(8,128)S(1)}, u32[]{:S(2)}) copy-start(f32[160,128]{1,0:T(8,128)S(1)} %collective-permute-done.1.refs_3_.refs_1_.refs_11_) | copy-start | bytes 245764
  15.7 11.6 %all-to-all-start = ((f32[4,176,128]{2,1,0:T(8,128)}), f32[4,176,128]{2,1,0:T(8,128)S(1)}, u32[]{:S(2)}, u32[]{:S(2)}) async-start(f32[4,176,128]{2,1,0:T(8,128)} %bitcast.18), calls=%async_computation | async-start | bytes 720896 | tf_op jit(solution)/shard_map/all_to_all | solution.py:692
  22.8 18.4 %copy-start.2 = (f32[128,128]{1,0:T(8,128)}, f32[128,128]{1,0:T(8,128)S(1)}, u32[]{:S(2)}) copy-start(f32[128,128]{1,0:T(8,128)S(1)} %get-tuple-element.33.refs_0_.refs_4_) | copy-start | bytes 196612
  22.8 1.3 %collective-permute-start.2 = (f32[128,128]{1,0:T(8,128)S(1)}, f32[128,128]{1,0:T(8,128)S(1)}, u32[]{:S(2)}, u32[]{:S(2)}) collective-permute-start(f32[128,128]{1,0:T(8,128)S(1)} %get-tuple-element.33.refs_0_.refs_4_), channel_id=1, source_target_pairs={{0,1},{1,0},{2,3},{3,2},{4,5},{5,4},{6,7},{7,6},{8,9},{9,8},{10,11... | collective-permute-start | bytes 196616 | tf_op jit(solution)/shard_map/ppermute | solution.py:687
  24.1 17.1 %copy-start.3 = (f32[128,128]{1,0:T(8,128)}, f32[128,128]{1,0:T(8,128)S(1)}, u32[]{:S(2)}) copy-start(f32[128,128]{1,0:T(8,128)S(1)} %collective-permute-done.2.refs_1_.refs_5_) | copy-start | bytes 196612
  28.4 12.8 %all-to-all-start.1 = ((f32[4,176,128]{2,1,0:T(8,128)}), f32[4,176,128]{2,1,0:T(8,128)S(1)}, u32[]{:S(2)}, u32[]{:S(2)}) async-start(f32[4,176,128]{2,1,0:T(8,128)} %bitcast.17), calls=%async_computation.1 | async-start | bytes 720896 | tf_op jit(solution)/shard_map/all_to_all | solution.py:692
  31.8 5.3 %collective-permute-start.7 = (f32[128,128]{1,0:T(8,128)S(1)}, f32[128,128]{1,0:T(8,128)S(1)}, u32[]{:S(2)}, u32[]{:S(2)}) collective-permute-start(f32[128,128]{1,0:T(8,128)S(1)} %get-tuple-element.37.refs_0_), channel_id=1, source_target_pairs={{0,6},{2,0},{4,2},{6,4},{1,7},{3,1},{5,3},{7,5},{8,14},{10,8},{12,... | collective-permute-start | bytes 196616 | tf_op jit(solution)/shard_map/ppermute | solution.py:687
  34.6 5.9 %collective-permute-start.6 = (f32[128,128]{1,0:T(8,128)S(1)}, f32[128,128]{1,0:T(8,128)S(1)}, u32[]{:S(2)}, u32[]{:S(2)}) collective-permute-start(f32[128,128]{1,0:T(8,128)S(1)} %get-tuple-element.37.refs_0_), channel_id=1, source_target_pairs={{0,4},{2,6},{4,0},{6,2},{1,5},{3,7},{5,1},{7,3},{8,12},{10,14},{12... | collective-permute-start | bytes 196616 | tf_op jit(solution)/shard_map/ppermute | solution.py:687
  35.4 5.7 %collective-permute-start.5 = (f32[128,128]{1,0:T(8,128)S(1)}, f32[128,128]{1,0:T(8,128)S(1)}, u32[]{:S(2)}, u32[]{:S(2)}) collective-permute-start(f32[128,128]{1,0:T(8,128)S(1)} %get-tuple-element.37.refs_0_), channel_id=1, source_target_pairs={{0,2},{2,4},{4,6},{6,0},{1,3},{3,5},{5,7},{7,1},{8,10},{10,12},{12... | collective-permute-start | bytes 196616 | tf_op jit(solution)/shard_map/ppermute | solution.py:687
  46.6 15.5 %all-to-all-start.2 = ((f32[16,64,128]{2,1,0:T(8,128)}), f32[16,64,128]{2,1,0:T(8,128)S(1)}, u32[]{:S(2)}, u32[]{:S(2)}) async-start(f32[16,64,128]{2,1,0:T(8,128)} %bitcast.16), calls=%async_computation.2 | async-start | bytes 1048576 | tf_op jit(solution)/shard_map/all_to_all | solution.py:692
  52.0 1.3 %collective-permute-start.8 = (f32[48,128]{1,0:T(8,128)S(1)}, f32[48,128]{1,0:T(8,128)S(1)}, u32[]{:S(2)}, u32[]{:S(2)}) collective-permute-start(f32[48,128]{1,0:T(8,128)S(1)} %get-tuple-element.45.refs_0_.refs_4_), channel_id=1, source_target_pairs={{0,1},{1,0},{2,3},{3,2},{4,5},{5,4},{6,7},{7,6},{8,9},{9,8},{10,11... | collective-permute-start | bytes 73736 | tf_op jit(solution)/shard_map/ppermute | solution.py:687
  54.2 3.9 %collective-permute-start.11 = (f32[48,128]{1,0:T(8,128)S(1)}, f32[48,128]{1,0:T(8,128)S(1)}, u32[]{:S(2)}, u32[]{:S(2)}) collective-permute-start(f32[48,128]{1,0:T(8,128)S(1)} %ends.1.refs_0_), channel_id=1, source_target_pairs={{0,6},{2,0},{4,2},{6,4},{1,7},{3,1},{5,3},{7,5},{8,14},{10,8},{12,... | collective-permute-start | bytes 73736 | tf_op jit(solution)/shard_map/ppermute | solution.py:687
  54.9 5.3 %collective-permute-start.10 = (f32[48,128]{1,0:T(8,128)S(1)}, f32[48,128]{1,0:T(8,128)S(1)}, u32[]{:S(2)}, u32[]{:S(2)}) collective-permute-start(f32[48,128]{1,0:T(8,128)S(1)} %ends.1.refs_0_), channel_id=1, source_target_pairs={{0,4},{2,6},{4,0},{6,2},{1,5},{3,7},{5,1},{7,3},{8,12},{10,14},{12... | collective-permute-start | bytes 73736 | tf_op jit(solution)/shard_map/ppermute | solution.py:687
  56.3 5.0 %collective-permute-start.9 = (f32[48,128]{1,0:T(8,128)S(1)}, f32[48,128]{1,0:T(8,128)S(1)}, u32[]{:S(2)}, u32[]{:S(2)}) collective-permute-start(f32[48,128]{1,0:T(8,128)S(1)} %ends.1.refs_0_), channel_id=1, source_target_pairs={{0,2},{2,4},{4,6},{6,0},{1,3},{3,5},{5,7},{7,1},{8,10},{10,12},{12... | collective-permute-start | bytes 73736 | tf_op jit(solution)/shard_map/ppermute | solution.py:687

commit v7 on v6

--- a/solution.py
+++ b/solution.py
@@ -97,6 +97,11 @@
     tab = [table[i] for i in range(16)]
     for x in range(PX):
         put(eps, x, lookup(plane(reg, x), tab))
+
+
+def k_q1(f, q1):
+    for x in range(PX):
+        put(q1, x, fplane(f, HY, x) - 0.5 * fz(fplane(f, EX, x)))
 
 
 def k_edges(f, reg, table, xup, xdn, yup, ydn, tab, ends, low, high, rlow, rhigh, sems):
@@ -192,7 +197,7 @@
             at += v.shape[0]
 
 
-def k_x1(f, eps, xl, xr, yl, yr, msg, q1, m, h, b, v, hb, r):
+def k_x1(f, eps, q1, xl, xr, yl, yr, msg, m, h, b, v, hb, r):
     gx = x_index()
     gy = y_index()
     xlo = gx > 0
@@ -214,8 +219,7 @@
     one = jnp.ones((XR - PY - 2, PZ), F32)
     before = jnp.where(xlo, plane(xl, 2) - 0.5 * fz(plane(xl, 0)), 0.0)
     for x in range(PX):
-        q = fplane(f, HY, x) - 0.5 * fz(fplane(f, EX, x))
-        put(q1, x, q)
+        q = plane(q1, x)
         e = plane(eps, x)
         hx = fplane(f, HX, x)
         ce = 32.0 / e
@@ -733,22 +737,23 @@
     of = lambda names: {k: lines[k] for k in names}
     pre = call(
         "eps",
-        [(k_eps, ("reg", "table", "eps"))],
-        dict(reg=reg, table=eps_table),
-        dict(eps=cells),
+        [(k_eps, ("reg", "table", "eps")), (k_q1, ("f", "q1"))],
+        dict(reg=reg, table=eps_table, f=f),
+        dict(eps=cells, q1=cells),
         smem=("table",),
+        only=dict(f=[(EX * cells, cells), (HY * cells, cells)]),
     )
     one = call(
         "onex",
         [
-            (k_x1, ("f", "eps", "xl", "xr", "yl", "yr", "msgx", "q1") + linex + ("r",)),
+            (k_x1, ("f", "eps", "q1", "xl", "xr", "yl", "yr", "msgx") + linex + ("r",)),
         ],
-        dict(xl=xl, xr=xr, yl=yl, yr=yr, eps=pre["eps"], f=f),
-        dict(q1=cells, lx=lines_x, msgx=nb * XB),
+        dict(xl=xl, xr=xr, yl=yl, yr=yr, eps=pre["eps"], q1=pre["q1"], f=f),
+        dict( lx=lines_x, msgx=nb * XB),
         dict(r=nxl),
         near=("xl", "xr", "yl", "yr") + NEAR,
         views=of(linex),
-        only=dict(f=[(EX * cells, cells), (EZ * cells, 3 * cells)]),
+        only=dict(f=[(EZ * cells, 2 * cells)]),
     )
     oney = call(
         "oney",
@@ -782,7 +787,8 @@
     ci, co, cyi, cyo = [tuple(k + a for k in chains) for a in ("i", "o", "yi", "yo")]
     cx, cy = ci + co, cyi + cyo
     size = lambda n, rows: (n * rows,) * 4 + ((n + 1) * rows,) * 2
-    keep = {k: one[k] for k in ("q1", "p1", "ey1", "lx", "ly")}
+    keep = {k: one[k] for k in ("p1", "ey1", "lx", "ly")}
+    keep["q1"] = pre["q1"]
     rows_y, rows_x = size(nc, YR) + size(nz, YR), size(nb, XR) + size(na, XR)
     views = {**stacked("cy", cy, rows_y), **stacked("cx", cx, rows_x)}
     two = call(

time: 66.3 us -> 66.1 us (level)
  transfers between devices with their start and end apart: 15 -> 15, of which waited for: 10 -> 9; matrix products, arithmetic and copies ran while one was open for 0% -> 0% of each run, Pallas kernels for 11% -> 11%
where the time goes in v7:
time: 66.1 us; the launch traced here: 65.6 us
  starting transfers between devices  28.9 us (44%)
  Pallas kernels  21.8 us (33%)
  waiting for transfers between devices  14.7 us (22%)
    pallas_call x7, Pallas kernels, call(): pl.pallas_call(body, out_shape=[(pltpu.VMEM if k in near else pltpu.HBM)(...  20.2 us
    ppermute x12, starting transfers between devices, ring(): return lax.ppermute(block, axis, [(i, (i + step) % n) for i in range(n)])  16.7 us
    all_to_all x3, starting transfers between devices, swap(): got = lax.all_to_all(msg.reshape(n, -1, PZ), axis, 0, 0, tiled=True)  12.2 us
    ppermute x12, waiting for transfers between devices, ring(): return lax.ppermute(block, axis, [(i, (i + step) % n) for i in range(n)])  11.2 us
    all_to_all x3, waiting for transfers between devices, swap(): got = lax.all_to_all(msg.reshape(n, -1, PZ), axis, 0, 0, tiled=True)  3.53 us
    pallas_call x1, Pallas kernels, edges(): pl.pallas_call(k_edges, out_shape=[pltpu.VMEM((c, PZ), F32) for c in (5 *...  1.58 us
  transfers between devices with their start and end apart: 15, of which 9 were waited for; matrix products, arithmetic and copies ran while one was open for 0% of the time, Pallas kernels for 11%

profile of v7, /device:TPU:0, one launch (start us, length us, event | category | flops | bytes accessed | tf_op | source)
XLA Modules:
  0.0 65.6 jit_solution(793818028535841382)
XLA Ops:
  0.0 0.0 copy-start.4
  0.0 1.6 %edges.1 = (f32[160,128]{1,0:T(8,128)S(1)}, f32[160,128]{1,0:T(8,128)S(1)}, f32[96,128]{1,0:T(8,128)S(1)}, f32[96,128]{1,0:T(8,128)S(1)}) custom-call(f32[6,16,32,128]{3,2,1,0:T(8,128)} %f.1, s32[16,32,128]{2,1,0:T(8,128)} %reg.1, f32[16]{0:T(128)} %table.1), custom_call_target="tpu_custom_call" | custom-call | flops 1000 | bytes 1000 | tf_op jit(solution)/shard_map/edges/pallas_call | solution.py:138
  1.6 1.7 %collective-permute-start = (f32[160,128]{1,0:T(8,128)S(1)}, f32[160,128]{1,0:T(8,128)S(1)}, u32[]{:S(2)}, u32[]{:S(2)}) collective-permute-start(f32[160,128]{1,0:T(8,128)S(1)} %get-tuple-element.33), channel_id=1, source_target_pairs={{0,8},{8,16},{16,24},{24,32},{32,40},{40,48},{48,56},{56,64},{64,7... | collective-permute-start | bytes 245768 | tf_op jit(solution)/shard_map/ppermute | solution.py:691
  3.3 3.7 %collective-permute-start.1 = (f32[160,128]{1,0:T(8,128)S(1)}, f32[160,128]{1,0:T(8,128)S(1)}, u32[]{:S(2)}, u32[]{:S(2)}) collective-permute-start(f32[160,128]{1,0:T(8,128)S(1)} %get-tuple-element.34), channel_id=1, source_target_pairs={{0,120},{8,0},{16,8},{24,16},{32,24},{40,32},{48,40},{56,48},{64,5... | collective-permute-start | bytes 245768 | tf_op jit(solution)/shard_map/ppermute | solution.py:691
  7.0 0.0 collective-permute-start.3
  7.0 3.2 %collective-permute-start.4 = (f32[96,128]{1,0:T(8,128)S(1)}, f32[96,128]{1,0:T(8,128)S(1)}, u32[]{:S(2)}, u32[]{:S(2)}) collective-permute-start(f32[96,128]{1,0:T(8,128)S(1)} %get-tuple-element.37), channel_id=1, source_target_pairs={{0,7},{1,0},{2,1},{3,2},{4,3},{5,4},{6,5},{7,6},{8,15},{9,8},{10,9... | collective-permute-start | bytes 147464 | tf_op jit(solution)/shard_map/ppermute | solution.py:691
  10.2 0.0 copy-done.4
  10.2 2.6 %eps.1 = (f32[512,128]{1,0:T(8,128)}, f32[512,128]{1,0:T(8,128)}) custom-call(s32[512,128]{1,0:T(8,128)} %bitcast.16, f32[16]{0:T(128)S(1)} %copy-done.4, f32[3072,128]{1,0:T(8,128)} %bitcast.12), custom_call_target="tpu_custom_call" | custom-call | flops 1000 | bytes 1000 | tf_op jit(solution)/shard_map/eps/pallas_call | solution.py:666
  12.8 0.0 collective-permute-done.3.refs_2_
  12.8 0.0 collective-permute-done.4.refs_3_
  12.9 0.0 collective-permute-done.refs_2_.refs_0_
  12.9 0.0 copy-start.1
  12.9 0.0 collective-permute-done.1.refs_3_.refs_1_.refs_11_
  12.9 0.0 copy-start
  12.9 2.8 %onex.1 = (f32[2720,128]{1,0:T(8,128)}, f32[704,128]{1,0:T(8,128)}) custom-call(f32[160,128]{1,0:T(8,128)S(1)} %collective-permute-done.refs_2_.refs_0_, f32[160,128]{1,0:T(8,128)S(1)} %collective-permute-done.1.refs_3_.refs_1_.refs_11_, f32[96,128]{1,0:T(8,128)S(1)} %collective-permute-done.3.refs_2_, f32[96,128]{1,0:T(8,128)S(1)} %collective-permute-done.4.refs_3_, ...), custom_call_target="tpu_custom_call" | custom-call | flops 1000 | bytes 1000 | tf_op jit(solution)/shard_map/onex/pallas_call | solution.py:666
  15.7 3.5 %all-to-all-start = ((f32[4,176,128]{2,1,0:T(8,128)}), f32[4,176,128]{2,1,0:T(8,128)S(1)}, u32[]{:S(2)}, u32[]{:S(2)}) async-start(f32[4,176,128]{2,1,0:T(8,128)} %bitcast.19), calls=%async_computation | async-start | bytes 720896 | tf_op jit(solution)/shard_map/all_to_all | solution.py:696
  19.1 0.0 copy-done.1
  19.2 0.0 copy-done
  19.2 3.6 %oney.1 = (f32[128,128]{1,0:T(8,128)S(1)}, f32[544,128]{1,0:T(8,128)}, f32[544,128]{1,0:T(8,128)}, f32[3168,128]{1,0:T(8,128)}) custom-call(f32[3072,128]{1,0:T(8,128)} %bitcast.14, f32[512,128]{1,0:T(8,128)} %get-tuple-element.32.refs_1_.refs_4_, f32[160,128]{1,0:T(8,128)} %copy-done.1, f32[160,128]{1,0:T(8,128)} %copy-done), custom_call_target="tpu_custom_call" | custom-call | flops 1000 | bytes 1000 | tf_op jit(solution)/shard_map/oney/pallas_call | solution.py:666
  22.8 0.0 copy-start.2
  22.8 0.1 collective-permute-start.2
  22.9 1.2 %collective-permute-done.2.refs_1_.refs_5_ = f32[128,128]{1,0:T(8,128)S(1)} collective-permute-done((f32[128,128]{1,0:T(8,128)S(1)}, f32[128,128]{1,0:T(8,128)S(1)}, u32[]{:S(2)}, u32[]{:S(2)}) %collective-permute-start.2) | collective-permute-done | bytes 65568 | tf_op jit(solution)/shard_map/ppermute | solution.py:691
  24.1 0.0 copy-start.3
  24.1 2.9 %all-to-all-done = f32[4,176,128]{2,1,0:T(8,128)S(1)} async-done(((f32[4,176,128]{2,1,0:T(8,128)}), f32[4,176,128]{2,1,0:T(8,128)S(1)}, u32[]{:S(2)}, u32[]{:S(2)}) %all-to-all-start) | async-done | bytes 360480 | tf_op jit(solution)/shard_map/all_to_all | solution.py:696
  27.0 1.1 %group.1 = (f32[128,128]{1,0:T(8,128)S(1)}, f32[704,128]{1,0:T(8,128)}, f32[704,128]{1,0:T(8,128)}) custom-call(f32[128,128]{1,0:T(8,128)S(1)} %get-tuple-element.35.refs_0_.refs_4_, f32[128,128]{1,0:T(8,128)S(1)} %collective-permute-done.2.refs_1_.refs_5_, f32[704,128]{1,0:T(8,128)S(1)} %bitcast.10), custom_call_target="tpu_custom_call" | custom-call | flops 1000 | bytes 1000 | tf_op jit(solution)/shard_map/group/pallas_call | solution.py:666
  28.2 3.5 %all-to-all-start.1 = ((f32[4,176,128]{2,1,0:T(8,128)}), f32[4,176,128]{2,1,0:T(8,128)S(1)}, u32[]{:S(2)}, u32[]{:S(2)}) async-start(f32[4,176,128]{2,1,0:T(8,128)} %bitcast.18), calls=%async_computation.1 | async-start | bytes 720896 | tf_op jit(solution)/shard_map/all_to_all | solution.py:696
  31.7 2.8 %collective-permute-start.7 = (f32[128,128]{1,0:T(8,128)S(1)}, f32[128,128]{1,0:T(8,128)S(1)}, u32[]{:S(2)}, u32[]{:S(2)}) collective-permute-start(f32[128,128]{1,0:T(8,128)S(1)} %get-tuple-element.40.refs_0_), channel_id=1, source_target_pairs={{0,6},{2,0},{4,2},{6,4},{1,7},{3,1},{5,3},{7,5},{8,14},{10,8},{12,... | collective-permute-start | bytes 196616 | tf_op jit(solution)/shard_map/ppermute | solution.py:691
  34.4 1.0 %collective-permute-start.6 = (f32[128,128]{1,0:T(8,128)S(1)}, f32[128,128]{1,0:T(8,128)S(1)}, u32[]{:S(2)}, u32[]{:S(2)}) collective-permute-start(f32[128,128]{1,0:T(8,128)S(1)} %get-tuple-element.40.refs_0_), channel_id=1, source_target_pairs={{0,4},{2,6},{4,0},{6,2},{1,5},{3,7},{5,1},{7,3},{8,12},{10,14},{12... | collective-permute-start | bytes 196616 | tf_op jit(solution)/shard_map/ppermute | solution.py:691
  35.4 1.3 %collective-permute-start.5 = (f32[128,128]{1,0:T(8,128)S(1)}, f32[128,128]{1,0:T(8,128)S(1)}, u32[]{:S(2)}, u32[]{:S(2)}) collective-permute-start(f32[128,128]{1,0:T(8,128)S(1)} %get-tuple-element.40.refs_0_), channel_id=1, source_target_pairs={{0,2},{2,4},{4,6},{6,0},{1,3},{3,5},{5,7},{7,1},{8,10},{10,12},{12... | collective-permute-start | bytes 196616 | tf_op jit(solution)/shard_map/ppermute | solution.py:691
  36.7 0.0 collective-permute-done.7.refs_3_
  36.7 3.6 %collective-permute-done.6.refs_2_ = f32[128,128]{1,0:T(8,128)S(1)} collective-permute-done((f32[128,128]{1,0:T(8,128)S(1)}, f32[128,128]{1,0:T(8,128)S(1)}, u32[]{:S(2)}, u32[]{:S(2)}) %collective-permute-start.6) | collective-permute-done | bytes 65568 | tf_op jit(solution)/shard_map/ppermute | solution.py:691
  40.3 0.7 %collective-permute-done.5.refs_1_ = f32[128,128]{1,0:T(8,128)S(1)} collective-permute-done((f32[128,128]{1,0:T(8,128)S(1)}, f32[128,128]{1,0:T(8,128)S(1)}, u32[]{:S(2)}, u32[]{:S(2)}) %collective-permute-start.5) | collective-permute-done | bytes 65568 | tf_op jit(solution)/shard_map/ppermute | solution.py:691
  41.1 0.0 all-to-all-done.1
  41.1 0.0 copy-done.2
  41.1 0.0 copy-done.3
  41.1 5.4 %two.1 = (f32[544,128]{1,0:T(8,128)}, f32[960,128]{1,0:T(8,128)}, f32[1024,128]{1,0:T(8,128)}, f32[512,128]{1,0:T(8,128)}, f32[32,128]{1,0:T(8,128)}, /*index=5*...) custom-call(f32[128,128]{1,0:T(8,128)S(1)} %get-tuple-element.40.ref, ...), custom_call_target="tpu_custom_call" | custom-call | flops 1000 | bytes 1000 | tf_op jit(solution)/shard_map/two/pallas_call | solution.py:666
  46.5 5.3 %all-to-all-start.2 = ((f32[16,64,128]{2,1,0:T(8,128)}), f32[16,64,128]{2,1,0:T(8,128)S(1)}, u32[]{:S(2)}, u32[]{:S(2)}) async-start(f32[16,64,128]{2,1,0:T(8,128)} %bitcast.17), calls=%async_computation.2 | async-start | bytes 1048576 | tf_op jit(solution)/shard_map/all_to_all | solution.py:696
  51.8 0.1 collective-permute-start.8
  51.9 1.2 %collective-permute-done.8.refs_1_.refs_5_ = f32[48,128]{1,0:T(8,128)S(1)} collective-permute-done((f32[48,128]{1,0:T(8,128)S(1)}, f32[48,128]{1,0:T(8,128)S(1)}, u32[]{:S(2)}, u32[]{:S(2)}) %collective-permute-start.8) | collective-permute-done | bytes 24608 | tf_op jit(solution)/shard_map/ppermute | solution.py:691
  53.1 1.0 %ends.1.refs_0_ = f32[48,128]{1,0:T(8,128)S(1)} custom-call(f32[48,128]{1,0:T(8,128)S(1)} %get-tuple-element.47.refs_0_.refs_4_, f32[48,128]{1,0:T(8,128)S(1)} %collective-permute-done.8.refs_1_.refs_5_, f32[960,128]{1,0:T(8,128)} %get-tuple-element.48.refs_2_.refs_7_), custom_call_target="tpu_custom_call" | custom-call | flops 1000 | bytes 1000 | tf_op jit(solution)/shard_map/ends/pallas_call | solution.py:666
  54.0 0.8 %collective-permute-start.11 = (f32[48,128]{1,0:T(8,128)S(1)}, f32[48,128]{1,0:T(8,128)S(1)}, u32[]{:S(2)}, u32[]{:S(2)}) collective-permute-start(f32[48,128]{1,0:T(8,128)S(1)} %ends.1.refs_0_), channel_id=1, source_target_pairs={{0,6},{2,0},{4,2},{6,4},{1,7},{3,1},{5,3},{7,5},{8,14},{10,8},{12,... | collective-permute-start | bytes 73736 | tf_op jit(solution)/shard_map/ppermute | solution.py:691
  54.8 1.4 %collective-permute-start.10 = (f32[48,128]{1,0:T(8,128)S(1)}, f32[48,128]{1,0:T(8,128)S(1)}, u32[]{:S(2)}, u32[]{:S(2)}) collective-permute-start(f32[48,128]{1,0:T(8,128)S(1)} %ends.1.refs_0_), channel_id=1, source_target_pairs={{0,4},{2,6},{4,0},{6,2},{1,5},{3,7},{5,1},{7,3},{8,12},{10,14},{12... | collective-permute-start | bytes 73736 | tf_op jit(solution)/shard_map/ppermute | solution.py:691
  56.3 0.6 collective-permute-start.9
  56.9 1.1 %collective-permute-done.11.refs_3_ = f32[48,128]{1,0:T(8,128)S(1)} collective-permute-done((f32[48,128]{1,0:T(8,128)S(1)}, f32[48,128]{1,0:T(8,128)S(1)}, u32[]{:S(2)}, u32[]{:S(2)}) %collective-permute-start.11) | collective-permute-done | bytes 24608 | tf_op jit(solution)/shard_map/ppermute | solution.py:691
  57.9 2.3 %collective-permute-done.10.refs_2_ = f32[48,128]{1,0:T(8,128)S(1)} collective-permute-done((f32[48,128]{1,0:T(8,128)S(1)}, f32[48,128]{1,0:T(8,128)S(1)}, u32[]{:S(2)}, u32[]{:S(2)}) %collective-permute-start.10) | collective-permute-done | bytes 24608 | tf_op jit(solution)/shard_map/ppermute | solution.py:691
  60.2 1.1 %collective-permute-done.9.refs_1_ = f32[48,128]{1,0:T(8,128)S(1)} collective-permute-done((f32[48,128]{1,0:T(8,128)S(1)}, f32[48,128]{1,0:T(8,128)S(1)}, u32[]{:S(2)}, u32[]{:S(2)}) %collective-permute-start.9) | collective-permute-done | bytes 24608 | tf_op jit(solution)/shard_map/ppermute | solution.py:691
  61.3 0.6 all-to-all-done.2
  61.9 3.7 %three.1 = f32[3072,128]{1,0:T(8,128)} custom-call(f32[48,128]{1,0:T(8,128)S(1)} %ends.1.refs_0_, f32[48,128]{1,0:T(8,128)S(1)} %collective-permute-done.9.refs_1_, f32[48,128]{1,0:T(8,128)S(1)} %collective-permute-done.10.refs_2_, f32[48,128]{1,0:T(8,128)S(1)} %collective-permute-done.11.refs_3_, f32[48,128]{1,0:T(8,128)S(1)} %get-tuple-element.47.refs_0_.refs_4_, ...), custom_call_target="tpu_custom_call" | custom-call | flops 1000 | bytes 1000 | tf_op jit(solution)/shard_map/three/pallas_call | solution.py:666
Async XLA Ops:
  0.0 10.2 %copy-start.4 = (f32[16]{0:T(128)S(1)}, f32[16]{0:T(128)}, u32[]{:S(2)}) copy-start(f32[16]{0:T(128)} %table.1) | copy-start | bytes 196
  1.6 11.3 %collective-permute-start = (f32[160,128]{1,0:T(8,128)S(1)}, f32[160,128]{1,0:T(8,128)S(1)}, u32[]{:S(2)}, u32[]{:S(2)}) collective-permute-start(f32[160,128]{1,0:T(8,128)S(1)} %get-tuple-element.33), channel_id=1, source_target_pairs={{0,8},{8,16},{16,24},{24,32},{32,40},{40,48},{48,56},{56,64},{64,7... | collective-permute-start | bytes 245768 | tf_op jit(solution)/shard_map/ppermute | solution.py:691
  3.3 9.6 %collective-permute-start.1 = (f32[160,128]{1,0:T(8,128)S(1)}, f32[160,128]{1,0:T(8,128)S(1)}, u32[]{:S(2)}, u32[]{:S(2)}) collective-permute-start(f32[160,128]{1,0:T(8,128)S(1)} %get-tuple-element.34), channel_id=1, source_target_pairs={{0,120},{8,0},{16,8},{24,16},{32,24},{40,32},{48,40},{56,48},{64,5... | collective-permute-start | bytes 245768 | tf_op jit(solution)/shard_map/ppermute | solution.py:691
  7.0 5.8 %collective-permute-start.3 = (f32[96,128]{1,0:T(8,128)S(1)}, f32[96,128]{1,0:T(8,128)S(1)}, u32[]{:S(2)}, u32[]{:S(2)}) collective-permute-start(f32[96,128]{1,0:T(8,128)S(1)} %get-tuple-element.36), channel_id=1, source_target_pairs={{0,1},{1,2},{2,3},{3,4},{4,5},{5,6},{6,7},{7,0},{8,9},{9,10},{10,1... | collective-permute-start | bytes 147464 | tf_op jit(solution)/shard_map/ppermute | solution.py:691
  7.0 5.8 %collective-permute-start.4 = (f32[96,128]{1,0:T(8,128)S(1)}, f32[96,128]{1,0:T(8,128)S(1)}, u32[]{:S(2)}, u32[]{:S(2)}) collective-permute-start(f32[96,128]{1,0:T(8,128)S(1)} %get-tuple-element.37), channel_id=1, source_target_pairs={{0,7},{1,0},{2,1},{3,2},{4,3},{5,4},{6,5},{7,6},{8,15},{9,8},{10,9... | collective-permute-start | bytes 147464 | tf_op jit(solution)/shard_map/ppermute | solution.py:691
  12.9 6.3 %copy-start.1 = (f32[160,128]{1,0:T(8,128)}, f32[160,128]{1,0:T(8,128)S(1)}, u32[]{:S(2)}) copy-start(f32[160,128]{1,0:T(8,128)S(1)} %collective-permute-done.refs_2_.refs_0_) | copy-start | bytes 245764
  12.9 6.3 %copy-start = (f32[160,128]{1,0:T(8,128)}, f32[160,128]{1,0:T(8,128)S(1)}, u32[]{:S(2)}) copy-start(f32[160,128]{1,0:T(8,128)S(1)} %collective-permute-done.1.refs_3_.refs_1_.refs_11_) | copy-start | bytes 245764
  15.7 11.4 %all-to-all-start = ((f32[4,176,128]{2,1,0:T(8,128)}), f32[4,176,128]{2,1,0:T(8,128)S(1)}, u32[]{:S(2)}, u32[]{:S(2)}) async-start(f32[4,176,128]{2,1,0:T(8,128)} %bitcast.19), calls=%async_computation | async-start | bytes 720896 | tf_op jit(solution)/shard_map/all_to_all | solution.py:696
  22.8 18.3 %copy-start.2 = (f32[128,128]{1,0:T(8,128)}, f32[128,128]{1,0:T(8,128)S(1)}, u32[]{:S(2)}) copy-start(f32[128,128]{1,0:T(8,128)S(1)} %get-tuple-element.35.refs_0_.refs_4_) | copy-start | bytes 196612
  22.8 1.3 %collective-permute-start.2 = (f32[128,128]{1,0:T(8,128)S(1)}, f32[128,128]{1,0:T(8,128)S(1)}, u32[]{:S(2)}, u32[]{:S(2)}) collective-permute-start(f32[128,128]{1,0:T(8,128)S(1)} %get-tuple-element.35.refs_0_.refs_4_), channel_id=1, source_target_pairs={{0,1},{1,0},{2,3},{3,2},{4,5},{5,4},{6,7},{7,6},{8,9},{9,8},{10,11... | collective-permute-start | bytes 196616 | tf_op jit(solution)/shard_map/ppermute | solution.py:691
  24.1 17.0 %copy-start.3 = (f32[128,128]{1,0:T(8,128)}, f32[128,128]{1,0:T(8,128)S(1)}, u32[]{:S(2)}) copy-start(f32[128,128]{1,0:T(8,128)S(1)} %collective-permute-done.2.refs_1_.refs_5_) | copy-start | bytes 196612
  28.2 12.9 %all-to-all-start.1 = ((f32[4,176,128]{2,1,0:T(8,128)}), f32[4,176,128]{2,1,0:T(8,128)S(1)}, u32[]{:S(2)}, u32[]{:S(2)}) async-start(f32[4,176,128]{2,1,0:T(8,128)} %bitcast.18), calls=%async_computation.1 | async-start | bytes 720896 | tf_op jit(solution)/shard_map/all_to_all | solution.py:696
  31.7 5.1 %collective-permute-start.7 = (f32[128,128]{1,0:T(8,128)S(1)}, f32[128,128]{1,0:T(8,128)S(1)}, u32[]{:S(2)}, u32[]{:S(2)}) collective-permute-start(f32[128,128]{1,0:T(8,128)S(1)} %get-tuple-element.40.refs_0_), channel_id=1, source_target_pairs={{0,6},{2,0},{4,2},{6,4},{1,7},{3,1},{5,3},{7,5},{8,14},{10,8},{12,... | collective-permute-start | bytes 196616 | tf_op jit(solution)/shard_map/ppermute | solution.py:691
  34.4 5.9 %collective-permute-start.6 = (f32[128,128]{1,0:T(8,128)S(1)}, f32[128,128]{1,0:T(8,128)S(1)}, u32[]{:S(2)}, u32[]{:S(2)}) collective-permute-start(f32[128,128]{1,0:T(8,128)S(1)} %get-tuple-element.40.refs_0_), channel_id=1, source_target_pairs={{0,4},{2,6},{4,0},{6,2},{1,5},{3,7},{5,1},{7,3},{8,12},{10,14},{12... | collective-permute-start | bytes 196616 | tf_op jit(solution)/shard_map/ppermute | solution.py:691
  35.4 5.7 %collective-permute-start.5 = (f32[128,128]{1,0:T(8,128)S(1)}, f32[128,128]{1,0:T(8,128)S(1)}, u32[]{:S(2)}, u32[]{:S(2)}) collective-permute-start(f32[128,128]{1,0:T(8,128)S(1)} %get-tuple-element.40.refs_0_), channel_id=1, source_target_pairs={{0,2},{2,4},{4,6},{6,0},{1,3},{3,5},{5,7},{7,1},{8,10},{10,12},{12... | collective-permute-start | bytes 196616 | tf_op jit(solution)/shard_map/ppermute | solution.py:691
  46.5 15.4 %all-to-all-start.2 = ((f32[16,64,128]{2,1,0:T(8,128)}), f32[16,64,128]{2,1,0:T(8,128)S(1)}, u32[]{:S(2)}, u32[]{:S(2)}) async-start(f32[16,64,128]{2,1,0:T(8,128)} %bitcast.17), calls=%async_computation.2 | async-start | bytes 1048576 | tf_op jit(solution)/shard_map/all_to_all | solution.py:696
  51.8 1.3 %collective-permute-start.8 = (f32[48,128]{1,0:T(8,128)S(1)}, f32[48,128]{1,0:T(8,128)S(1)}, u32[]{:S(2)}, u32[]{:S(2)}) collective-permute-start(f32[48,128]{1,0:T(8,128)S(1)} %get-tuple-element.47.refs_0_.refs_4_), channel_id=1, source_target_pairs={{0,1},{1,0},{2,3},{3,2},{4,5},{5,4},{6,7},{7,6},{8,9},{9,8},{10,11... | collective-permute-start | bytes 73736 | tf_op jit(solution)/shard_map/ppermute | solution.py:691
  54.0 3.9 %collective-permute-start.11 = (f32[48,128]{1,0:T(8,128)S(1)}, f32[48,128]{1,0:T(8,128)S(1)}, u32[]{:S(2)}, u32[]{:S(2)}) collective-permute-start(f32[48,128]{1,0:T(8,128)S(1)} %ends.1.refs_0_), channel_id=1, source_target_pairs={{0,6},{2,0},{4,2},{6,4},{1,7},{3,1},{5,3},{7,5},{8,14},{10,8},{12,... | collective-permute-start | bytes 73736 | tf_op jit(solution)/shard_map/ppermute | solution.py:691
  54.8 5.3 %collective-permute-start.10 = (f32[48,128]{1,0:T(8,128)S(1)}, f32[48,128]{1,0:T(8,128)S(1)}, u32[]{:S(2)}, u32[]{:S(2)}) collective-permute-start(f32[48,128]{1,0:T(8,128)S(1)} %ends.1.refs_0_), channel_id=1, source_target_pairs={{0,4},{2,6},{4,0},{6,2},{1,5},{3,7},{5,1},{7,3},{8,12},{10,14},{12... | collective-permute-start | bytes 73736 | tf_op jit(solution)/shard_map/ppermute | solution.py:691
  56.3 5.0 %collective-permute-start.9 = (f32[48,128]{1,0:T(8,128)S(1)}, f32[48,128]{1,0:T(8,128)S(1)}, u32[]{:S(2)}, u32[]{:S(2)}) collective-permute-start(f32[48,128]{1,0:T(8,128)S(1)} %ends.1.refs_0_), channel_id=1, source_target_pairs={{0,2},{2,4},{4,6},{6,0},{1,3},{3,5},{5,7},{7,1},{8,10},{10,12},{12... | collective-permute-start | bytes 73736 | tf_op jit(solution)/shard_map/ppermute | solution.py:691
